TPU v7x, 512 devices: a whole 4x4x16 slice. The times are simulated.
512 devices in a mesh: sec: 2 (over core), ep: 64 (over x, z), tp: 4 (over y).
Axes of the slice: x: 4, y: 4, z: 16, core: 2. Of those that a mesh axis runs over, the one named last changes fastest.
Arguments:
- tokens: bfloat16 [8192, 4096], P('ep', ('sec', 'tp')), may hold values from -6 to 6
- router_weight: bfloat16 [4096, 64], P(('sec', 'tp')), may hold values from -0.09375 to 0.09375
- expert_ids: int32 [8192, 8], P('ep'), may hold values from 0 to 63, all different within a row; in each aligned block of 128 rows (0 to 127, 128 to 255, ...) at most 20 rows name the same one
- gate_weight: bfloat16 [64, 4096, 1536], P('ep', 'sec', 'tp'), may hold values from -0.09375 to 0.09375
- up_weight: bfloat16 [64, 4096, 1536], P('ep', 'sec', 'tp'), may hold values from -0.09375 to 0.09375
- down_weight: bfloat16 [64, 1536, 4096], P('ep', None, ('sec', 'tp')), may hold values from -0.15625 to 0.15625
Outputs:
- mixture: bfloat16 [8192, 4096], P('ep', ('sec', 'tp'))
Inputs may be any that keep to these rules, and one draw needn't show every extreme that they name: `expert_ids`: each row names 8 different experts. The 128 rows of one index of ep name no expert more than 20 times, a bound that some block reaches.
All inputs are finite; a program needn't handle non-finite values.
Results may differ from a plain program's by a relative error of at most 0.0057.
Values may be sent and summed in bfloat16 or wider, within the bound.
No kernel may reach another device: no remote copies, remote signals or barrier semaphores. Data moves between devices by JAX's collectives and lax.ppermute only.
A program may use at most 64 MiB of HBM per device.

v0:
```python
import jax
import jax.numpy as jnp
from jax import lax
from jax.sharding import PartitionSpec as P

EXPERTS = 64
TOP = 8
CAP = 20


def per_device(tokens, router_weight, expert_ids, gate_weight, up_weight, down_weight):
    tok_rows = tokens.shape[0]
    partial_logits = jnp.dot(tokens, router_weight, preferred_element_type=jnp.float32)
    logits = lax.psum(partial_logits, ("sec", "tp"))
    expert_grid = lax.broadcasted_iota(jnp.int32, (1, 1, EXPERTS), 2)
    chosen = expert_ids[:, :, None] == expert_grid
    picked = jnp.sum(jnp.where(chosen, logits[:, None, :], jnp.float32(0.0)), axis=2)
    raised = jnp.exp(picked)
    route_probs = raised / jnp.sum(raised, axis=1, keepdims=True)
    flat_ids = expert_ids.reshape(-1)
    onehot = (flat_ids[:, None] == expert_grid[0]).astype(jnp.int32)
    running = jnp.cumsum(onehot, axis=0) - 1
    slot_rank = jnp.sum(running * onehot, axis=1)
    target = flat_ids * CAP + slot_rank
    source_tok = lax.broadcasted_iota(jnp.int32, (tok_rows * TOP,), 0) // TOP
    half_rows = lax.all_gather(tokens, "tp", axis=1, tiled=True)
    outgoing = jnp.zeros((EXPERTS * CAP, half_rows.shape[1]), jnp.bfloat16)
    outgoing = (
        outgoing.at[target].set(half_rows[source_tok]).reshape(EXPERTS, CAP, half_rows.shape[1])
    )
    arrived = lax.all_to_all(outgoing, "ep", split_axis=0, concat_axis=1, tiled=True)
    gate_half = jnp.einsum("esd,edf->esf", arrived, gate_weight, preferred_element_type=jnp.float32)
    up_half = jnp.einsum("esd,edf->esf", arrived, up_weight, preferred_element_type=jnp.float32)
    gate_acts, up_acts = lax.psum((gate_half, up_half), "sec")
    hidden = (jax.nn.silu(gate_acts) * up_acts).astype(jnp.bfloat16)
    produced = jnp.einsum(
        "esk,ekd->esd",
        lax.all_gather(hidden, "tp", axis=2, tiled=True),
        down_weight,
        preferred_element_type=jnp.float32,
    ).astype(jnp.bfloat16)
    returned = lax.all_to_all(produced, "ep", split_axis=1, concat_axis=0, tiled=True)
    returned = returned.reshape(EXPERTS * CAP, returned.shape[2])
    own_rows = returned[target].reshape(tok_rows, TOP, returned.shape[1]).astype(jnp.float32)
    mixture = jnp.sum(route_probs[:, :, None] * own_rows, axis=1)
    return mixture.astype(jnp.bfloat16)


def solution(mesh):
    placed = (
        P("ep", ("sec", "tp")),
        P(("sec", "tp"), None),
        P("ep", None),
        P("ep", "sec", "tp"),
        P("ep", "sec", "tp"),
        P("ep", None, ("sec", "tp")),
    )
    return jax.shard_map(
        per_device, mesh=mesh, in_specs=placed, out_specs=P("ep", ("sec", "tp")), check_vma=False
    )
```

profile of v0, /device:TPU:6, one launch (start us, length us, event | category | flops | bytes accessed | tf_op | source)
XLA Modules:
  0.0 613.8 jit_solution(15710930430318812767)
XLA Ops:
  6.5 0.0 copy-start
  6.5 0.0 copy-start.2
  6.5 0.0 all-reduce.3.cloned.1.call-start
  6.5 0.9 copy.34
  7.5 0.1 eq.45
  7.6 0.1 eq.41
  7.6 0.7 broadcast_multiply_fusion
  8.4 18.0 %reduce-window.6 = s32[64,8,128]{2,1,0:T(8,128)S(1)} reduce-window(s32[64,8,128]{2,1,0:T(8,128)S(1)} %fusion.17, s32[]{:T(128)} %constant.31.clone.1), window={size=1x1x128 pad=0_0x0_0x127_0}, to_apply=%region_3.4 | reduce-window | flops 8323072 | bytes 524292 | tf_op jit(solution)/shard_map/reduce-window
  26.4 0.1 slice.12
  26.5 0.1 copy.36
  26.7 0.1 copy.37
  26.8 0.1 add_add_fusion
  26.9 0.1 copy.33
  27.0 0.1 mul.37
  27.1 0.0 copy-done.2
  27.1 13.3 %all_gather.6 = bf16[128,2048]{1,0:T(8,128)(2,1)S(1)} all-gather(bf16[128,512]{1,0:T(8,128)(2,1)S(1)} %copy-done.2), channel_id=1, replica_groups=mesh['sec'=2,'ep'=64,'tp'=4] {'tp'}, dimensions={1}, use_global_device_ids=true | all-gather | bytes 655360 | tf_op jit(solution)/shard_map/all_gather | solution.py:26
  40.5 0.1 fusion.16
  40.5 23.2 %scatter_custom_fusion = bf16[1280,2048]{1,0:T(8,128)(2,1)} fusion(s32[1024]{0:T(1024)S(1)} %bitcast.59, bf16[128,2048]{1,0:T(8,128)(2,1)S(1)} %all_gather.6, s32[1024]{0:T(1024)S(1)} %broadcast_clamp_fusion.1, bf16[]{:T(256)} %constant.29.clone.1), kind=kCustom, calls=%fused_computation.3 | custom fusion | bytes 5242882 | tf_op jit(solution)/shard_map/scatter | solution.py:29
  63.7 8.9 %reshape.151 = bf16[64,20,2048]{2,1,0:T(8,128)(2,1)} reshape(bf16[1280,2048]{1,0:T(8,128)(2,1)} %scatter_custom_fusion) | data formatting | bytes 10485760 | tf_op jit(solution)/shard_map/reshape | solution.py:29
  72.7 295.4 %all_to_all.8 = bf16[64,20,2048]{2,1,0:T(8,128)(2,1)} all-to-all(bf16[64,20,2048]{2,1,0:T(8,128)(2,1)} %reshape.151), channel_id=1, replica_groups=mesh['sec'=2,'ep'=64,'tp'=4] {'ep'}, dimensions={0} | all-to-all | bytes 10485760 | tf_op jit(solution)/shard_map/all_to_all | solution.py:31
  368.0 9.0 %reshape.152 = bf16[1280,2048]{1,0:T(8,128)(2,1)} reshape(bf16[64,20,2048]{2,1,0:T(8,128)(2,1)} %all_to_all.8) | data formatting | bytes 10485760 | tf_op jit(solution)/shard_map/reshape.9
  377.0 0.0 copy-start.1
  377.0 0.0 copy-start.5
  377.0 7.3 %convolution_bitcast_fusion = f32[1,1280,384]{2,1,0:T(8,128)} fusion(bf16[1280,2048]{1,0:T(8,128)(2,1)} %reshape.152, bf16[1,2048,384]{2,1,0:T(8,128)(2,1)} %param.10), kind=kOutput, calls=%fused_computation.8 | convolution fusion | flops 2013265920 | bytes 8781824 | tf_op jit(solution)/shard_map/esd,edf->esf/dot_general | solution.py:33
  384.3 0.0 copy-done.1
  384.3 0.0 copy-done.5
  384.4 4.3 convolution_bitcast_fusion.1
  388.6 0.0 all-reduce.3.cloned.1.call-update
  388.7 0.3 all-gather.2.cloned.1.call-start
  388.9 37.0 %all-reduce.3.cloned.1.call-done = (f32[1,1280,384]{2,1,0:T(8,128)}, f32[1,1280,384]{2,1,0:T(8,128)}) async-done(((f32[1,1280,384]{2,1,0:T(8,128)}, f32[1,1280,384]{2,1,0:T(8,128)}), (f32[1,1280,384]{2,1,0:T(8,128)}, f32[1,1280,384]{2,1,0:T(8,128)})) %all-reduce.3.cloned.1.call-update) | async-done | bytes 3932176 | tf_op jit(solution)/shard_map/psum | solution.py:34
  425.9 3.6 multiply_convert_fusion
  429.5 0.0 all-gather.2.cloned.1.call-update
  429.6 55.3 %all-gather.2.cloned.1.call-done = bf16[1,1280,1536]{2,1,0:T(8,128)(2,1)} async-done(((bf16[1,1280,384]{2,1,0:T(8,128)(2,1)}), bf16[1,1280,1536]{2,1,0:T(8,128)(2,1)}) %all-gather.2.cloned.1.call-update) | async-done | bytes 3932176 | tf_op jit(solution)/shard_map/all_gather | solution.py:38
  484.8 0.0 copy-done
  484.8 4.3 fusion.7
  489.2 11.9 %copy.45 = bf16[1,1280,512]{2,0,1:T(2,128)(2,1)} copy(bf16[1,1280,512]{2,1,0:T(8,128)(2,1)S(1)} %fusion.7) | data formatting | bytes 2621440 | tf_op jit(solution)/shard_map/convert_element_type | solution.py:41
  501.0 0.5 broadcast.147
  501.5 9.4 %reduce = bf16[1280,512]{1,0:T(8,128)(2,1)S(1)} reduce(bf16[1280,1,512]{2,1,0:T(2,128)(2,1)} %bitcast.54, bf16[]{:T(256)} %broadcast.147), dimensions={1}, to_apply=%bitcast.52.reduce_sub_computation | reduce | bytes 2621442
  511.0 1.4 reshape.189
  512.4 0.0 copy-start.3
  512.4 0.0 copy-start.4
  512.4 16.0 %all-to-all-start.1 = ((bf16[64,2,5120]{2,1,0:T(2,128)(2,1)}), bf16[64,2,5120]{2,1,0:T(2,128)(2,1)S(1)}, u32[]{:S(2)}, u32[]{:S(2)}) async-start(bf16[64,2,5120]{2,1,0:T(2,128)(2,1)} %reshape.189), calls=%async_computation.1 | async-start | bytes 2621440 | tf_op jit(solution)/shard_map/all_to_all | solution.py:42
  528.5 0.0 copy-done.3
  528.5 0.2 fusion.18
  528.7 25.1 %psum.21 = f32[128,64]{0,1:T(8,128)S(1)} all-reduce(f32[128,64]{0,1:T(8,128)S(1)} %fusion.18), channel_id=1, replica_groups=mesh['sec'=2,'ep'=64,'tp'=4] {'sec','tp'}, use_global_device_ids=true, to_apply=%region_0.0 | all-reduce | flops 8192 | bytes 65536 | tf_op jit(solution)/shard_map/psum | solution.py:14
  553.8 0.0 copy-done.4
  553.9 0.1 copy.32
  554.0 39.7 %all-to-all-done.1 = bf16[64,2,5120]{2,1,0:T(2,128)(2,1)S(1)} async-done(((bf16[64,2,5120]{2,1,0:T(2,128)(2,1)}), bf16[64,2,5120]{2,1,0:T(2,128)(2,1)S(1)}, u32[]{:S(2)}, u32[]{:S(2)}) %all-to-all-start.1) | async-done | bytes 1310752 | tf_op jit(solution)/shard_map/all_to_all | solution.py:42
  593.6 3.5 reshape.190
  597.2 2.1 copy.44
  599.3 5.1 gather_fusion
  604.3 2.6 fusion.11
  (10 shorter events, 0.1 us)
Async XLA Ops:
  6.5 478.3 %copy-start = (bf16[1,1536,512]{2,1,0:T(8,128)(2,1)S(1)}, bf16[1,1536,512]{2,1,0:T(8,128)(2,1)}, u32[]{:S(2)}) copy-start(bf16[1,1536,512]{2,1,0:T(8,128)(2,1)} %param.11) | copy-start | bytes 4718596
  6.5 20.6 %copy-start.2 = (bf16[128,512]{1,0:T(8,128)(2,1)S(1)}, bf16[128,512]{1,0:T(8,128)(2,1)}, u32[]{:S(2)}) copy-start(bf16[128,512]{1,0:T(8,128)(2,1)} %param.6) | copy-start | bytes 393220
  6.5 419.4 %all-reduce.3.cloned.1.call-start = ((), (), s32[]{:S(2)}) async-start(), calls=%async_computation.3 | async-start | bytes 7864320 | tf_op jit(solution)/shard_map/psum | solution.py:34
  377.0 7.3 %copy-start.1 = (bf16[1280,2048]{1,0:T(8,128)(2,1)S(1)}, bf16[1280,2048]{1,0:T(8,128)(2,1)}, u32[]{:S(2)}) copy-start(bf16[1280,2048]{1,0:T(8,128)(2,1)} %reshape.152) | copy-start | bytes 15728644
  377.0 7.3 %copy-start.5 = (bf16[1,2048,384]{2,1,0:T(8,128)(2,1)S(1)}, bf16[1,2048,384]{2,1,0:T(8,128)(2,1)}, u32[]{:S(2)}) copy-start(bf16[1,2048,384]{2,1,0:T(8,128)(2,1)} %param.9) | copy-start | bytes 4718596
  388.7 96.2 %all-gather.2.cloned.1.call-start = ((), (), s32[]{:S(2)}) async-start(), calls=%async_computation.2 | async-start | bytes 4915200 | tf_op jit(solution)/shard_map/all_gather | solution.py:38
  512.4 16.1 %copy-start.3 = (bf16[512,64]{0,1:T(8,128)(2,1)S(1)}, bf16[512,64]{0,1:T(8,128)(2,1)}, u32[]{:S(2)}) copy-start(bf16[512,64]{0,1:T(8,128)(2,1)} %param.7) | copy-start | bytes 196612
  512.4 41.4 %copy-start.4 = (s32[128,8]{0,1:T(8,128)S(1)}, s32[128,8]{0,1:T(8,128)}, u32[]{:S(2)}) copy-start(s32[128,8]{0,1:T(8,128)} %param.8) | copy-start | bytes 12292
  512.4 81.2 %all-to-all-start.1 = ((bf16[64,2,5120]{2,1,0:T(2,128)(2,1)}), bf16[64,2,5120]{2,1,0:T(2,128)(2,1)S(1)}, u32[]{:S(2)}, u32[]{:S(2)}) async-start(bf16[64,2,5120]{2,1,0:T(2,128)(2,1)} %reshape.189), calls=%async_computation.1 | async-start | bytes 2621440 | tf_op jit(solution)/shard_map/all_to_all | solution.py:42
Sparse Core Ops, SparseCore 0:
  388.8 37.0 all-reduce.2
  429.7 55.1 all-gather.1
where the time goes:
time: 615 us; the launch traced here: 614 us
  blocking collectives  334 us (54%)
  waiting for transfers between devices  132 us (21%)
  local copies, waits for them, and re-layouts  67.4 us (11%)
  other arithmetic  34.7 us (6%)
  starting transfers between devices  16.3 us (3%)
  matrix products  16 us (3%)
  between operations  13.5 us (2%)
    all_to_all x1, blocking collectives, per_device(): lax.all_to_all(outgoing, 'ep', split_axis=0, concat_axis=1, tiled=True)  295 us
    all_gather x1, waiting for transfers between devices, per_device(): lax.all_gather(hidden, 'tp', axis=2, tiled=True)  55.3 us
    all_to_all x1, waiting for transfers between devices, per_device(): lax.all_to_all(produced, 'ep', split_axis=1, concat_axis=0, tiled=True)  39.7 us
    psum x1, waiting for transfers between devices, per_device(): gate_acts, up_acts = lax.psum((gate_half, up_half), 'sec')  37 us
    psum x1, blocking collectives, per_device(): logits = lax.psum(partial_logits, ('sec', 'tp'))  25.1 us
    scatter x1, local copies, waits for them, and re-layouts, per_device(): outgoing.at[target].set(half_rows[source_tok])  23.2 us
    another operation x2, other arithmetic  18 us
    all_to_all x1, starting transfers between devices, per_device(): lax.all_to_all(produced, 'ep', split_axis=1, concat_axis=0, tiled=True)  16 us
  transfers between devices with their start and end apart: 3, of which 3 were waited for; matrix products, arithmetic and copies ran while one was open for 0% of the time, Pallas kernels for 0%

commit v1 on v0

v1 whole, which is shorter than its diff:
```python
import jax
import jax.numpy as jnp
from jax import lax
from jax.sharding import PartitionSpec as P

EXPERTS = 64
CAP = 20
CHUNKS = 2
BF = jnp.bfloat16
F32 = jnp.float32


def shift(x, axis, size, by):
    return lax.ppermute(x, axis, [(i, (i + by) % size) for i in range(size)])


def ring_gather(x):
    half = x.shape[0] // 2
    behind = shift(x, "tp", 4, 1)
    ahead = shift(x, "tp", 4, -1)
    far_low = shift(behind[:half], "tp", 4, 1)
    far_high = shift(ahead[half:], "tp", 4, -1)
    return x, behind, far_low, far_high, ahead


def rolled(weight, me):
    rows = weight.shape[0] // 4
    parts = [lax.dynamic_slice_in_dim(weight, ((me - i) % 4) * rows, rows, 0) for i in range(4)]
    return jnp.concatenate(parts, axis=0)


def dot(a, b):
    return jnp.dot(a, b, preferred_element_type=F32)


def route(tokens, router_weight, expert_ids):
    rows = tokens.shape[0]
    chosen = jnp.any(expert_ids[:, :, None] == lax.broadcasted_iota(jnp.int32, (1, 1, EXPERTS), 2), axis=1)
    before = lax.broadcasted_iota(jnp.int32, (rows, rows), 0) > lax.broadcasted_iota(jnp.int32, (rows, rows), 1)
    rank = dot(before.astype(BF), chosen.astype(BF))
    slot = jnp.where(chosen, rank, F32(-1.0))
    return chosen, slot


def route_weights(tokens, router_weight, chosen):
    logits = dot(tokens, router_weight)
    logits = logits + shift(logits, "sec", 2, 1)
    logits = logits + shift(logits, "tp", 4, 1)
    logits = logits + shift(logits, "tp", 4, 2)
    raised = jnp.where(chosen, jnp.exp(logits), F32(0.0))
    return raised / jnp.sum(raised, axis=1, keepdims=True)


def per_device(tokens, router_weight, expert_ids, gate_weight, up_weight, down_weight):
    me = lax.axis_index("tp")
    sec = lax.axis_index("sec")
    width = tokens.shape[1]
    slots = CAP // CHUNKS
    rows = EXPERTS * slots
    pieces = width // 128
    gate_w, up_w, down_w = (rolled(w[0], me) for w in (gate_weight, up_weight, down_weight))

    chosen, slot = route(tokens, router_weight, expert_ids)
    column = lax.broadcasted_iota(jnp.int32, (1, rows), 1)
    spread = (lax.broadcasted_iota(jnp.int32, (EXPERTS, rows), 0) == column // slots).astype(BF)
    slot_wide = dot(slot.astype(BF), spread)
    picks = [slot_wide == (column % slots + c * slots).astype(F32) for c in range(CHUNKS)]

    arrived = []
    for pick in picks:
        outgoing = lax.dot_general(pick.astype(BF), tokens, (((0,), (0,)), ((), ())), preferred_element_type=F32).astype(BF)
        outgoing = outgoing.reshape(EXPERTS, slots * pieces, 128)
        arrived.append(lax.all_to_all(outgoing, "ep", split_axis=0, concat_axis=0, tiled=True))

    probs = route_weights(tokens, router_weight, chosen)
    probs_high = probs.astype(BF)
    probs_low = (probs - probs_high.astype(F32)).astype(BF)
    wide_high = dot(probs_high, spread).astype(BF)
    wide_low = dot(probs_low, spread).astype(BF)

    returned = []
    for block in arrived:
        own, behind, far_low, far_high, ahead = ring_gather(block)
        far = jnp.concatenate([far_low, far_high], axis=0)
        features = jnp.concatenate([b.reshape(rows, width) for b in (own, behind, far, ahead)], axis=1)
        acts = jnp.concatenate([dot(features, gate_w), dot(features, up_w)], axis=1)
        half = rows // 2
        kept = lax.dynamic_slice_in_dim(acts, sec * half, half, 0)
        sent = lax.dynamic_slice_in_dim(acts, (1 - sec) * half, half, 0).astype(BF)
        acts = kept + shift(sent, "sec", 2, 1).astype(F32)
        units = acts.shape[1] // 2
        hidden = (jax.nn.silu(acts[:, :units]) * acts[:, units:]).astype(BF)
        parts = ring_gather(hidden)
        others = [shift(p, "sec", 2, 1) for p in parts]
        outs = []
        for own, behind, far_low, far_high, ahead in (parts, others):
            far = jnp.concatenate([far_low, far_high], axis=0)
            outs.append(dot(jnp.concatenate([own, behind, far, ahead], axis=1), down_w).astype(BF))
        first = jnp.where(sec == 0, outs[0], outs[1])
        second = jnp.where(sec == 0, outs[1], outs[0])
        produced = jnp.concatenate([first, second], axis=0).reshape(EXPERTS, slots * pieces, 128)
        returned.append(lax.all_to_all(produced, "ep", split_axis=0, concat_axis=0, tiled=True))

    mixture = jnp.zeros(tokens.shape, F32)
    for pick, block in zip(picks, returned):
        block = block.reshape(rows, width)
        for wide in (wide_high, wide_low):
            mixture = mixture + dot(jnp.where(pick, wide, BF(0.0)), block)
    return mixture.astype(BF)


def solution(mesh):
    placed = (
        P("ep", ("sec", "tp")),
        P(("sec", "tp"), None),
        P("ep", None),
        P("ep", "sec", "tp"),
        P("ep", "sec", "tp"),
        P("ep", None, ("sec", "tp")),
    )
    return jax.shard_map(
        per_device, mesh=mesh, in_specs=placed, out_specs=P("ep", ("sec", "tp")), check_vma=False
    )
```

time: 615 us -> 299 us (0.49)
  blocking collectives: 334 us -> 0 us
  starting transfers between devices: 16.3 us -> 137 us
  local copies, waits for them, and re-layouts: 67.4 us -> 31.5 us
  other arithmetic: 34.7 us -> 6.57 us
  waiting for transfers between devices: 132 us -> 105 us
  between operations: 13.5 us -> 1.26 us
    all_to_all x1 -> x0, blocking collectives: 295 us -> none  [per_device(): lax.all_to_all(outgoing, 'ep', split_axis=0, concat_axis=1, tiled=True)]
    ppermute x0 -> x31, starting transfers between devices: none -> 89.3 us  [shift(): return lax.ppermute(x, axis, [(i, (i + by) % size) for i in range(size)])]
    all_gather x1 -> x0, waiting for transfers between devices: 55.3 us -> none  [per_device(): lax.all_gather(hidden, 'tp', axis=2, tiled=True)]
    all_to_all x1 -> x4, waiting for transfers between devices: 39.7 us -> 84.3 us  [the longest x2 65.7 us: per_device(): lax.all_to_all(outgoing, 'ep', split_axis=0, concat_axis=0, tiled=True)]
    psum x1 -> x0, waiting for transfers between devices: 37 us -> none  [per_device(): gate_acts, up_acts = lax.psum((gate_half, up_half), 'sec')]
    all_to_all x1 -> x4, starting transfers between devices: 16 us -> 47.3 us  [the longest x2 25.5 us: per_device(): lax.all_to_all(outgoing, 'ep', split_axis=0, concat_axis=0, tiled=True)]
    psum x1 -> x0, blocking collectives: 25.1 us -> none  [per_device(): logits = lax.psum(partial_logits, ('sec', 'tp'))]
    scatter x1 -> x0, local copies, waits for them, and re-layouts: 23.2 us -> none  [per_device(): outgoing.at[target].set(half_rows[source_tok])]
  transfers between devices with their start and end apart: 3 -> 35, of which waited for: 3 -> 11; matrix products, arithmetic and copies ran while one was open for 0% -> 16% of each run, Pallas kernels for 0% -> 0%
where the time goes in v1:
time: 299 us; the launch traced here: 297 us
  starting transfers between devices  137 us (46%)
  waiting for transfers between devices  105 us (35%)
  local copies, waits for them, and re-layouts  31.5 us (11%)
  matrix products  16 us (5%)
  other arithmetic  6.57 us (2%)
    ppermute x31, starting transfers between devices, shift(): return lax.ppermute(x, axis, [(i, (i + by) % size) for i in range(size)])  89.3 us
    all_to_all x2, waiting for transfers between devices, per_device(): lax.all_to_all(outgoing, 'ep', split_axis=0, concat_axis=0, tiled=True)  65.7 us
    all_to_all x2, starting transfers between devices, per_device(): lax.all_to_all(outgoing, 'ep', split_axis=0, concat_axis=0, tiled=True)  25.5 us
    all_to_all x2, starting transfers between devices, per_device(): lax.all_to_all(produced, 'ep', split_axis=0, concat_axis=0, tiled=True)  21.9 us
    ppermute x31, waiting for transfers between devices, shift(): return lax.ppermute(x, axis, [(i, (i + by) % size) for i in range(size)])  20.6 us
    all_to_all x2, waiting for transfers between devices, per_device(): lax.all_to_all(produced, 'ep', split_axis=0, concat_axis=0, tiled=True)  18.6 us
    dot_general x16, matrix products, dot(): return jnp.dot(a, b, preferred_element_type=F32)  15.2 us
    reshape x8, local copies, waits for them, and re-layouts, per_device(): b.reshape(rows, width)  8.63 us
  transfers between devices with their start and end apart: 35, of which 11 were waited for; matrix products, arithmetic and copies ran while one was open for 16% of the time, Pallas kernels for 0%

profile of v1, /device:TPU:6, one launch (start us, length us, event | category | flops | bytes accessed | tf_op | source)
XLA Modules:
  0.0 296.8 jit_solution(18119507711058981898)
XLA Ops:
  1.6 1.2 reshape.98
  2.9 18.8 %all-to-all-start = ((bf16[64,40,128]{2,1,0:T(8,128)(2,1)}), bf16[64,40,128]{2,1,0:T(8,128)(2,1)S(1)}, u32[]{:S(2)}, u32[]{:S(2)}) async-start(bf16[64,40,128]{2,1,0:T(8,128)(2,1)} %reshape.98), calls=%async_computation | async-start | bytes 1310720 | tf_op jit(solution)/shard_map/all_to_all | solution.py:73
  22.1 1.3 reshape.105
  23.3 35.5 %all-to-all-done = bf16[64,40,128]{2,1,0:T(8,128)(2,1)S(1)} async-done(((bf16[64,40,128]{2,1,0:T(8,128)(2,1)}), bf16[64,40,128]{2,1,0:T(8,128)(2,1)S(1)}, u32[]{:S(2)}, u32[]{:S(2)}) %all-to-all-start) | async-done | bytes 655392 | tf_op jit(solution)/shard_map/all_to_all | solution.py:73
  58.9 6.7 %all-to-all-start.2 = ((bf16[64,40,128]{2,1,0:T(8,128)(2,1)}), bf16[64,40,128]{2,1,0:T(8,128)(2,1)S(1)}, u32[]{:S(2)}, u32[]{:S(2)}) async-start(bf16[64,40,128]{2,1,0:T(8,128)(2,1)} %reshape.105), calls=%async_computation.2 | async-start | bytes 1310720 | tf_op jit(solution)/shard_map/all_to_all | solution.py:73
  65.6 4.9 %collective-permute-start.5 = (bf16[64,40,128]{2,1,0:T(8,128)(2,1)S(1)}, bf16[64,40,128]{2,1,0:T(8,128)(2,1)}, u32[]{:S(2)}, u32[]{:S(2)}) collective-permute-start(bf16[64,40,128]{2,1,0:T(8,128)(2,1)S(1)} %all-to-all-done), channel_id=1, source_target_pairs={{0,3},{1,0},{2,1},{3,2},{4,7},{5,4},{6,5},{7,6},{8,11},{9,8},{10,9... | collective-permute-start | bytes 1966088 | tf_op jit(solution)/shard_map/ppermute | solution.py:14
  70.5 1.9 collective-permute-start.3
  72.4 30.1 %all-to-all-done.2 = bf16[64,40,128]{2,1,0:T(8,128)(2,1)S(1)} async-done(((bf16[64,40,128]{2,1,0:T(8,128)(2,1)}), bf16[64,40,128]{2,1,0:T(8,128)(2,1)S(1)}, u32[]{:S(2)}, u32[]{:S(2)}) %all-to-all-start.2) | async-done | bytes 655392 | tf_op jit(solution)/shard_map/all_to_all | solution.py:73
  102.6 4.9 %collective-permute-start.19 = (bf16[64,40,128]{2,1,0:T(8,128)(2,1)S(1)}, bf16[64,40,128]{2,1,0:T(8,128)(2,1)}, u32[]{:S(2)}, u32[]{:S(2)}) collective-permute-start(bf16[64,40,128]{2,1,0:T(8,128)(2,1)S(1)} %all-to-all-done.2), channel_id=1, source_target_pairs={{0,3},{1,0},{2,1},{3,2},{4,7},{5,4},{6,5},{7,6},{8,11},{9,8},{10,9... | collective-permute-start | bytes 1966088 | tf_op jit(solution)/shard_map/ppermute | solution.py:14
  107.5 1.9 collective-permute-start.17
  109.5 1.7 slice.49
  111.2 5.1 %collective-permute-start.6 = (bf16[32,40,128]{2,1,0:T(8,128)(2,1)}, bf16[32,40,128]{2,1,0:T(8,128)(2,1)}, u32[]{:S(2)}, u32[]{:S(2)}) collective-permute-start(bf16[32,40,128]{2,1,0:T(8,128)(2,1)} %slice.49), channel_id=1, source_target_pairs={{0,3},{1,0},{2,1},{3,2},{4,7},{5,4},{6,5},{7,6},{8,11},{9,8},{10,9... | collective-permute-start | bytes 983048 | tf_op jit(solution)/shard_map/ppermute | solution.py:14
  116.4 1.7 slice.48
  118.1 1.9 collective-permute-start.4
  120.0 3.0 %dynamic-slice_bitcast_fusion.7 = (bf16[512,384]{1,0:T(8,128)(2,1)}, bf16[512,384]{1,0:T(8,128)(2,1)}, bf16[512,384]{1,0:T(8,128)(2,1)}, bf16[512,384]{1,0:T(8,1...) fusion(bf16[1,2048,384]{2,1,0:T(8,128)(2,1)S(1)} %copy-done.1, ...), kind=kLoop, calls=%fused_computation.85 | loop fusion | bytes 6291472 | tf_op jit(solution)/shard_map/dynamic_slice | solution.py:28
  124.4 1.7 slice.55
  126.1 5.1 %collective-permute-start.20 = (bf16[32,40,128]{2,1,0:T(8,128)(2,1)}, bf16[32,40,128]{2,1,0:T(8,128)(2,1)}, u32[]{:S(2)}, u32[]{:S(2)}) collective-permute-start(bf16[32,40,128]{2,1,0:T(8,128)(2,1)} %slice.55), channel_id=1, source_target_pairs={{0,3},{1,0},{2,1},{3,2},{4,7},{5,4},{6,5},{7,6},{8,11},{9,8},{10,9... | collective-permute-start | bytes 983048 | tf_op jit(solution)/shard_map/ppermute | solution.py:14
  131.2 1.7 slice.54
  132.9 1.9 collective-permute-start.18
  134.9 1.5 reshape.102
  136.4 1.5 reshape.100
  142.3 3.4 %fusion.52 = f32[640,384]{1,0:T(8,128)S(1)} fusion(bf16[640,2048]{1,0:T(8,128)(2,1)} %constant_dynamic-update-slice_fusion, bf16[512,384]{1,0:T(8,128)(2,1)S(1)} %copy-done.7, bf16[512,384]{1,0:T(8,128)(2,1)S(1)} %get-tuple-element.27, bf16[512,384]{1,0:T(8,128)(2,1)S(1)} %copy-done.9, bf16[512,384]{1,0:T(8,128)(2,1)S(1)} %copy-done.11), kind=kOutput, calls=%fused_computation.97 | convolution fusion | flops 1012924416 | bytes 5177344 | tf_op jit(solution)/shard_map/dot_general | solution.py:33
  145.8 1.5 fusion.50
  148.1 1.9 collective-permute-start.7
  150.1 1.2 dynamic-slice_bitcast_fusion.3
  152.6 1.5 reshape.109
  154.1 1.5 reshape.107
  156.6 2.0 pad_maximum_fusion.5
  158.5 1.5 reshape.108
  160.1 1.3 fusion.10
  161.5 5.3 %collective-permute-start.10 = (bf16[320,384]{1,0:T(8,128)(2,1)S(1)}, bf16[320,384]{1,0:T(8,128)(2,1)S(1)}, u32[]{:S(2)}, u32[]{:S(2)}) collective-permute-start(bf16[320,384]{1,0:T(8,128)(2,1)S(1)} %fusion.48), channel_id=1, source_target_pairs={{0,3},{1,0},{2,1},{3,2},{4,7},{5,4},{6,5},{7,6},{8,11},{9,8},{10,9... | collective-permute-start | bytes 737288 | tf_op jit(solution)/shard_map/ppermute | solution.py:14
  166.8 2.1 collective-permute-start.8
  169.1 3.5 %collective-permute-done.10 = bf16[320,384]{1,0:T(8,128)(2,1)S(1)} collective-permute-done((bf16[320,384]{1,0:T(8,128)(2,1)S(1)}, bf16[320,384]{1,0:T(8,128)(2,1)S(1)}, u32[]{:S(2)}, u32[]{:S(2)}) %collective-permute-start.10) | collective-permute-done | bytes 245792 | tf_op jit(solution)/shard_map/ppermute | solution.py:14
  172.7 5.6 %collective-permute-start.11 = (bf16[160,384]{1,0:T(8,128)(2,1)S(1)}, bf16[160,384]{1,0:T(8,128)(2,1)S(1)}, u32[]{:S(2)}, u32[]{:S(2)}) collective-permute-start(bf16[160,384]{1,0:T(8,128)(2,1)S(1)} %slice.53), channel_id=1, source_target_pairs={{0,3},{1,0},{2,1},{3,2},{4,7},{5,4},{6,5},{7,6},{8,11},{9,8},{10,9... | collective-permute-start | bytes 368648 | tf_op jit(solution)/shard_map/ppermute | solution.py:14
  178.4 2.1 collective-permute-start.9
  180.5 1.5 fusion.49
  182.0 1.9 collective-permute-start.12
  183.9 2.4 collective-permute-start.16
  186.3 1.9 collective-permute-start.13
  188.3 2.4 collective-permute-start.15
  190.7 1.9 collective-permute-start.14
  194.7 1.2 reshape.103
  195.9 6.6 %all-to-all-start.1 = ((bf16[64,40,128]{2,1,0:T(8,128)(2,1)}), bf16[64,40,128]{2,1,0:T(8,128)(2,1)S(1)}, u32[]{:S(2)}, u32[]{:S(2)}) async-start(bf16[64,40,128]{2,1,0:T(8,128)(2,1)} %reshape.103), calls=%async_computation.1 | async-start | bytes 1310720 | tf_op jit(solution)/shard_map/all_to_all | solution.py:102
  202.6 3.3 %fusion.51 = f32[640,384]{1,0:T(8,128)S(1)} fusion(bf16[640,2048]{1,0:T(8,128)(2,1)} %copy-done.31, bf16[512,384]{1,0:T(8,128)(2,1)S(1)} %copy-done.8, bf16[512,384]{1,0:T(8,128)(2,1)S(1)} %copy-done.6, bf16[512,384]{1,0:T(8,128)(2,1)S(1)} %copy-done.10, bf16[512,384]{1,0:T(8,128)(2,1)S(1)} %copy-done.12), kind=kOutput, calls=%fused_computation.96 | convolution fusion | flops 1012924416 | bytes 5177344 | tf_op jit(solution)/shard_map/dot_general | solution.py:33
  206.0 2.1 collective-permute-start.21
  208.0 1.8 collective-permute-done.21
  210.1 5.1 %collective-permute-start.24 = (bf16[320,384]{1,0:T(8,128)(2,1)S(1)}, bf16[320,384]{1,0:T(8,128)(2,1)S(1)}, u32[]{:S(2)}, u32[]{:S(2)}) collective-permute-start(bf16[320,384]{1,0:T(8,128)(2,1)S(1)} %fusion.47), channel_id=1, source_target_pairs={{0,3},{1,0},{2,1},{3,2},{4,7},{5,4},{6,5},{7,6},{8,11},{9,8},{10,9... | collective-permute-start | bytes 737288 | tf_op jit(solution)/shard_map/ppermute | solution.py:14
  215.2 1.9 collective-permute-start.22
  217.2 3.6 %collective-permute-done.24 = bf16[320,384]{1,0:T(8,128)(2,1)S(1)} collective-permute-done((bf16[320,384]{1,0:T(8,128)(2,1)S(1)}, bf16[320,384]{1,0:T(8,128)(2,1)S(1)}, u32[]{:S(2)}, u32[]{:S(2)}) %collective-permute-start.24) | collective-permute-done | bytes 245792 | tf_op jit(solution)/shard_map/ppermute | solution.py:14
  220.7 5.6 %collective-permute-start.25 = (bf16[160,384]{1,0:T(8,128)(2,1)S(1)}, bf16[160,384]{1,0:T(8,128)(2,1)S(1)}, u32[]{:S(2)}, u32[]{:S(2)}) collective-permute-start(bf16[160,384]{1,0:T(8,128)(2,1)S(1)} %slice.59), channel_id=1, source_target_pairs={{0,3},{1,0},{2,1},{3,2},{4,7},{5,4},{6,5},{7,6},{8,11},{9,8},{10,9... | collective-permute-start | bytes 368648 | tf_op jit(solution)/shard_map/ppermute | solution.py:14
  226.4 1.9 collective-permute-start.23
  228.3 1.9 collective-permute-start.26
  230.2 2.4 collective-permute-start.30
  232.7 1.9 collective-permute-start.27
  234.6 2.4 collective-permute-start.29
  237.0 1.9 collective-permute-start.28
  241.0 1.3 reshape.110
  242.3 15.3 %all-to-all-start.3 = ((bf16[64,40,128]{2,1,0:T(8,128)(2,1)}), bf16[64,40,128]{2,1,0:T(8,128)(2,1)S(1)}, u32[]{:S(2)}, u32[]{:S(2)}) async-start(bf16[64,40,128]{2,1,0:T(8,128)(2,1)} %reshape.110), calls=%async_computation.3 | async-start | bytes 1310720 | tf_op jit(solution)/shard_map/all_to_all | solution.py:102
  257.7 1.9 collective-permute-start
  260.8 1.9 collective-permute-start.1
  262.7 5.1 %collective-permute-done.1 = f32[128,64]{0,1:T(8,128)S(1)} collective-permute-done((f32[128,64]{0,1:T(8,128)S(1)}, f32[128,64]{0,1:T(8,128)S(1)}, u32[]{:S(2)}, u32[]{:S(2)}) %collective-permute-start.1) | collective-permute-done | bytes 32800 | tf_op jit(solution)/shard_map/ppermute | solution.py:14
  267.8 3.1 %collective-permute-start.2 = (f32[128,64]{0,1:T(8,128)S(1)}, f32[128,64]{0,1:T(8,128)S(1)}, u32[]{:S(2)}, u32[]{:S(2)}) collective-permute-start(f32[128,64]{0,1:T(8,128)S(1)} %add.126), channel_id=1, source_target_pairs={{0,2},{1,3},{2,0},{3,1},{4,6},{5,7},{6,4},{7,5},{8,10},{9,11},{10,... | collective-permute-start | bytes 98312 | tf_op jit(solution)/shard_map/ppermute | solution.py:14
  270.9 4.2 %collective-permute-done.2 = f32[128,64]{0,1:T(8,128)S(1)} collective-permute-done((f32[128,64]{0,1:T(8,128)S(1)}, f32[128,64]{0,1:T(8,128)S(1)}, u32[]{:S(2)}, u32[]{:S(2)}) %collective-permute-start.2) | collective-permute-done | bytes 32800 | tf_op jit(solution)/shard_map/ppermute | solution.py:14
  276.6 18.6 %all-to-all-done.3 = bf16[64,40,128]{2,1,0:T(8,128)(2,1)S(1)} async-done(((bf16[64,40,128]{2,1,0:T(8,128)(2,1)}), bf16[64,40,128]{2,1,0:T(8,128)(2,1)S(1)}, u32[]{:S(2)}, u32[]{:S(2)}) %all-to-all-start.3) | async-done | bytes 655392 | tf_op jit(solution)/shard_map/all_to_all | solution.py:102
  (138 shorter events, 19.9 us)
Async XLA Ops:
  2.9 56.0 %all-to-all-start = ((bf16[64,40,128]{2,1,0:T(8,128)(2,1)}), bf16[64,40,128]{2,1,0:T(8,128)(2,1)S(1)}, u32[]{:S(2)}, u32[]{:S(2)}) async-start(bf16[64,40,128]{2,1,0:T(8,128)(2,1)} %reshape.98), calls=%async_computation | async-start | bytes 1310720 | tf_op jit(solution)/shard_map/all_to_all | solution.py:73
  22.1 98.0 %copy-start.1 = (bf16[1,2048,384]{2,1,0:T(8,128)(2,1)S(1)}, bf16[1,2048,384]{2,1,0:T(8,128)(2,1)}, u32[]{:S(2)}) copy-start(bf16[1,2048,384]{2,1,0:T(8,128)(2,1)} %param.10) | copy-start | bytes 4718596
  58.9 43.7 %all-to-all-start.2 = ((bf16[64,40,128]{2,1,0:T(8,128)(2,1)}), bf16[64,40,128]{2,1,0:T(8,128)(2,1)S(1)}, u32[]{:S(2)}, u32[]{:S(2)}) async-start(bf16[64,40,128]{2,1,0:T(8,128)(2,1)} %reshape.105), calls=%async_computation.2 | async-start | bytes 1310720 | tf_op jit(solution)/shard_map/all_to_all | solution.py:73
  65.6 43.9 %collective-permute-start.5 = (bf16[64,40,128]{2,1,0:T(8,128)(2,1)S(1)}, bf16[64,40,128]{2,1,0:T(8,128)(2,1)}, u32[]{:S(2)}, u32[]{:S(2)}) collective-permute-start(bf16[64,40,128]{2,1,0:T(8,128)(2,1)S(1)} %all-to-all-done), channel_id=1, source_target_pairs={{0,3},{1,0},{2,1},{3,2},{4,7},{5,4},{6,5},{7,6},{8,11},{9,8},{10,9... | collective-permute-start | bytes 1966088 | tf_op jit(solution)/shard_map/ppermute | solution.py:14
  70.5 45.9 %collective-permute-start.3 = (bf16[64,40,128]{2,1,0:T(8,128)(2,1)S(1)}, bf16[64,40,128]{2,1,0:T(8,128)(2,1)}, u32[]{:S(2)}, u32[]{:S(2)}) collective-permute-start(bf16[64,40,128]{2,1,0:T(8,128)(2,1)S(1)} %all-to-all-done), channel_id=1, source_target_pairs={{0,1},{1,2},{2,3},{3,0},{4,5},{5,6},{6,7},{7,4},{8,9},{9,10},{10,1... | collective-permute-start | bytes 1966088 | tf_op jit(solution)/shard_map/ppermute | solution.py:14
  102.6 21.8 %collective-permute-start.19 = (bf16[64,40,128]{2,1,0:T(8,128)(2,1)S(1)}, bf16[64,40,128]{2,1,0:T(8,128)(2,1)}, u32[]{:S(2)}, u32[]{:S(2)}) collective-permute-start(bf16[64,40,128]{2,1,0:T(8,128)(2,1)S(1)} %all-to-all-done.2), channel_id=1, source_target_pairs={{0,3},{1,0},{2,1},{3,2},{4,7},{5,4},{6,5},{7,6},{8,11},{9,8},{10,9... | collective-permute-start | bytes 1966088 | tf_op jit(solution)/shard_map/ppermute | solution.py:14
  107.5 23.7 %collective-permute-start.17 = (bf16[64,40,128]{2,1,0:T(8,128)(2,1)S(1)}, bf16[64,40,128]{2,1,0:T(8,128)(2,1)}, u32[]{:S(2)}, u32[]{:S(2)}) collective-permute-start(bf16[64,40,128]{2,1,0:T(8,128)(2,1)S(1)} %all-to-all-done.2), channel_id=1, source_target_pairs={{0,1},{1,2},{2,3},{3,0},{4,5},{5,6},{6,7},{7,4},{8,9},{9,10},{10,1... | collective-permute-start | bytes 1966088 | tf_op jit(solution)/shard_map/ppermute | solution.py:14
  111.2 27.5 %collective-permute-start.6 = (bf16[32,40,128]{2,1,0:T(8,128)(2,1)}, bf16[32,40,128]{2,1,0:T(8,128)(2,1)}, u32[]{:S(2)}, u32[]{:S(2)}) collective-permute-start(bf16[32,40,128]{2,1,0:T(8,128)(2,1)} %slice.49), channel_id=1, source_target_pairs={{0,3},{1,0},{2,1},{3,2},{4,7},{5,4},{6,5},{7,6},{8,11},{9,8},{10,9... | collective-permute-start | bytes 983048 | tf_op jit(solution)/shard_map/ppermute | solution.py:14
  118.1 20.7 %collective-permute-start.4 = (bf16[32,40,128]{2,1,0:T(8,128)(2,1)}, bf16[32,40,128]{2,1,0:T(8,128)(2,1)}, u32[]{:S(2)}, u32[]{:S(2)}) collective-permute-start(bf16[32,40,128]{2,1,0:T(8,128)(2,1)} %slice.48), channel_id=1, source_target_pairs={{0,1},{1,2},{2,3},{3,0},{4,5},{5,6},{6,7},{7,4},{8,9},{9,10},{10,1... | collective-permute-start | bytes 983048 | tf_op jit(solution)/shard_map/ppermute | solution.py:14
  123.0 19.2 %copy-start.5 = (bf16[512,384]{1,0:T(8,128)(2,1)}, bf16[512,384]{1,0:T(8,128)(2,1)S(1)}, u32[]{:S(2)}) copy-start(bf16[512,384]{1,0:T(8,128)(2,1)S(1)} %get-tuple-element.27) | copy-start | bytes 1179652
  126.1 30.5 %collective-permute-start.20 = (bf16[32,40,128]{2,1,0:T(8,128)(2,1)}, bf16[32,40,128]{2,1,0:T(8,128)(2,1)}, u32[]{:S(2)}, u32[]{:S(2)}) collective-permute-start(bf16[32,40,128]{2,1,0:T(8,128)(2,1)} %slice.55), channel_id=1, source_target_pairs={{0,3},{1,0},{2,1},{3,2},{4,7},{5,4},{6,5},{7,6},{8,11},{9,8},{10,9... | collective-permute-start | bytes 983048 | tf_op jit(solution)/shard_map/ppermute | solution.py:14
  132.9 23.6 %collective-permute-start.18 = (bf16[32,40,128]{2,1,0:T(8,128)(2,1)}, bf16[32,40,128]{2,1,0:T(8,128)(2,1)}, u32[]{:S(2)}, u32[]{:S(2)}) collective-permute-start(bf16[32,40,128]{2,1,0:T(8,128)(2,1)} %slice.54), channel_id=1, source_target_pairs={{0,1},{1,2},{2,3},{3,0},{4,5},{5,6},{6,7},{7,4},{8,9},{9,10},{10,1... | collective-permute-start | bytes 983048 | tf_op jit(solution)/shard_map/ppermute | solution.py:14
  140.3 1.9 copy-start.7
  142.3 3.5 %copy-start.13 = (bf16[512,384]{1,0:T(8,128)(2,1)S(1)}, bf16[512,384]{1,0:T(8,128)(2,1)}, u32[]{:S(2)}) copy-start(bf16[512,384]{1,0:T(8,128)(2,1)} %get-tuple-element.11) | copy-start | bytes 1179652
  142.3 3.5 %copy-start.15 = (bf16[512,384]{1,0:T(8,128)(2,1)S(1)}, bf16[512,384]{1,0:T(8,128)(2,1)}, u32[]{:S(2)}) copy-start(bf16[512,384]{1,0:T(8,128)(2,1)} %get-tuple-element.12) | copy-start | bytes 1179652
  142.3 3.5 %copy-start.17 = (bf16[512,384]{1,0:T(8,128)(2,1)S(1)}, bf16[512,384]{1,0:T(8,128)(2,1)}, u32[]{:S(2)}) copy-start(bf16[512,384]{1,0:T(8,128)(2,1)} %get-tuple-element.13) | copy-start | bytes 1179652
  142.3 3.5 %copy-start.19 = (bf16[512,384]{1,0:T(8,128)(2,1)S(1)}, bf16[512,384]{1,0:T(8,128)(2,1)}, u32[]{:S(2)}) copy-start(bf16[512,384]{1,0:T(8,128)(2,1)} %get-tuple-element.14) | copy-start | bytes 1179652
  142.3 3.5 %copy-start.29 = (bf16[640,2048]{1,0:T(8,128)(2,1)S(1)}, bf16[640,2048]{1,0:T(8,128)(2,1)}, u32[]{:S(2)}) copy-start(bf16[640,2048]{1,0:T(8,128)(2,1)} %constant_dynamic-update-slice_fusion) | copy-start | bytes 7864324
  147.3 2.8 copy-start.2
  148.1 11.9 %collective-permute-start.7 = (bf16[320,768]{1,0:T(8,128)(2,1)}, bf16[320,768]{1,0:T(8,128)(2,1)}, u32[]{:S(2)}, u32[]{:S(2)}) collective-permute-start(bf16[320,768]{1,0:T(8,128)(2,1)} %fusion.8), channel_id=1, source_target_pairs={{0,256},{256,0},{1,257},{257,1},{2,258},{258,2},{3,259},{259,3},{4... | collective-permute-start | bytes 1474568 | tf_op jit(solution)/shard_map/ppermute | solution.py:14
  160.0 8.9 %copy-start.30 = (bf16[640,2048]{1,0:T(8,128)(2,1)S(1)}, bf16[640,2048]{1,0:T(8,128)(2,1)}, u32[]{:S(2)}) copy-start(bf16[640,2048]{1,0:T(8,128)(2,1)} %constant_dynamic-update-slice_fusion.6) | copy-start | bytes 7864324
  161.3 19.1 %copy-start.14 = (bf16[512,384]{1,0:T(8,128)(2,1)S(1)}, bf16[512,384]{1,0:T(8,128)(2,1)}, u32[]{:S(2)}) copy-start(bf16[512,384]{1,0:T(8,128)(2,1)} %get-tuple-element.11) | copy-start | bytes 1179652
  161.3 19.1 %copy-start.16 = (bf16[512,384]{1,0:T(8,128)(2,1)S(1)}, bf16[512,384]{1,0:T(8,128)(2,1)}, u32[]{:S(2)}) copy-start(bf16[512,384]{1,0:T(8,128)(2,1)} %get-tuple-element.12) | copy-start | bytes 1179652
  161.4 19.1 %copy-start.18 = (bf16[512,384]{1,0:T(8,128)(2,1)S(1)}, bf16[512,384]{1,0:T(8,128)(2,1)}, u32[]{:S(2)}) copy-start(bf16[512,384]{1,0:T(8,128)(2,1)} %get-tuple-element.13) | copy-start | bytes 1179652
  161.4 19.1 %copy-start.20 = (bf16[512,384]{1,0:T(8,128)(2,1)S(1)}, bf16[512,384]{1,0:T(8,128)(2,1)}, u32[]{:S(2)}) copy-start(bf16[512,384]{1,0:T(8,128)(2,1)} %get-tuple-element.14) | copy-start | bytes 1179652
  161.5 11.1 %collective-permute-start.10 = (bf16[320,384]{1,0:T(8,128)(2,1)S(1)}, bf16[320,384]{1,0:T(8,128)(2,1)S(1)}, u32[]{:S(2)}, u32[]{:S(2)}) collective-permute-start(bf16[320,384]{1,0:T(8,128)(2,1)S(1)} %fusion.48), channel_id=1, source_target_pairs={{0,3},{1,0},{2,1},{3,2},{4,7},{5,4},{6,5},{7,6},{8,11},{9,8},{10,9... | collective-permute-start | bytes 737288 | tf_op jit(solution)/shard_map/ppermute | solution.py:14
  166.8 11.5 %collective-permute-start.8 = (bf16[320,384]{1,0:T(8,128)(2,1)S(1)}, bf16[320,384]{1,0:T(8,128)(2,1)S(1)}, u32[]{:S(2)}, u32[]{:S(2)}) collective-permute-start(bf16[320,384]{1,0:T(8,128)(2,1)S(1)} %fusion.48), channel_id=1, source_target_pairs={{0,1},{1,2},{2,3},{3,0},{4,5},{5,6},{6,7},{7,4},{8,9},{9,10},{10,1... | collective-permute-start | bytes 737288 | tf_op jit(solution)/shard_map/ppermute | solution.py:14
  169.1 24.2 %copy-start.31 = (bf16[640,2048]{1,0:T(8,128)(2,1)}, bf16[640,2048]{1,0:T(8,128)(2,1)S(1)}, u32[]{:S(2)}) copy-start(bf16[640,2048]{1,0:T(8,128)(2,1)S(1)} %constant_dynamic-update-slice_fusion.4) | copy-start | bytes 7864324
  172.7 15.6 %collective-permute-start.11 = (bf16[160,384]{1,0:T(8,128)(2,1)S(1)}, bf16[160,384]{1,0:T(8,128)(2,1)S(1)}, u32[]{:S(2)}, u32[]{:S(2)}) collective-permute-start(bf16[160,384]{1,0:T(8,128)(2,1)S(1)} %slice.53), channel_id=1, source_target_pairs={{0,3},{1,0},{2,1},{3,2},{4,7},{5,4},{6,5},{7,6},{8,11},{9,8},{10,9... | collective-permute-start | bytes 368648 | tf_op jit(solution)/shard_map/ppermute | solution.py:14
  178.3 14.3 %copy-start.21 = (bf16[384,512]{1,0:T(8,128)(2,1)S(1)}, bf16[384,512]{1,0:T(8,128)(2,1)}, u32[]{:S(2)}) copy-start(bf16[384,512]{1,0:T(8,128)(2,1)} %get-tuple-element.7) | copy-start | bytes 1179652
  178.3 14.3 %copy-start.23 = (bf16[384,512]{1,0:T(8,128)(2,1)S(1)}, bf16[384,512]{1,0:T(8,128)(2,1)}, u32[]{:S(2)}) copy-start(bf16[384,512]{1,0:T(8,128)(2,1)} %get-tuple-element.8) | copy-start | bytes 1179652
  178.3 14.3 %copy-start.25 = (bf16[384,512]{1,0:T(8,128)(2,1)S(1)}, bf16[384,512]{1,0:T(8,128)(2,1)}, u32[]{:S(2)}) copy-start(bf16[384,512]{1,0:T(8,128)(2,1)} %get-tuple-element.9) | copy-start | bytes 1179652
  178.3 14.3 %copy-start.27 = (bf16[384,512]{1,0:T(8,128)(2,1)S(1)}, bf16[384,512]{1,0:T(8,128)(2,1)}, u32[]{:S(2)}) copy-start(bf16[384,512]{1,0:T(8,128)(2,1)} %get-tuple-element.10) | copy-start | bytes 1179652
  178.4 12.3 %collective-permute-start.9 = (bf16[160,384]{1,0:T(8,128)(2,1)S(1)}, bf16[160,384]{1,0:T(8,128)(2,1)S(1)}, u32[]{:S(2)}, u32[]{:S(2)}) collective-permute-start(bf16[160,384]{1,0:T(8,128)(2,1)S(1)} %slice.52), channel_id=1, source_target_pairs={{0,1},{1,2},{2,3},{3,0},{4,5},{5,6},{6,7},{7,4},{8,9},{9,10},{10,1... | collective-permute-start | bytes 368648 | tf_op jit(solution)/shard_map/ppermute | solution.py:14
  182.0 11.4 %collective-permute-start.12 = (bf16[320,384]{1,0:T(8,128)(2,1)S(1)}, bf16[320,384]{1,0:T(8,128)(2,1)S(1)}, u32[]{:S(2)}, u32[]{:S(2)}) collective-permute-start(bf16[320,384]{1,0:T(8,128)(2,1)S(1)} %fusion.48), channel_id=1, source_target_pairs={{0,256},{256,0},{1,257},{257,1},{2,258},{258,2},{3,259},{259,3},{4... | collective-permute-start | bytes 737288 | tf_op jit(solution)/shard_map/ppermute | solution.py:14
  183.9 9.4 %collective-permute-start.16 = (bf16[320,384]{1,0:T(8,128)(2,1)S(1)}, bf16[320,384]{1,0:T(8,128)(2,1)S(1)}, u32[]{:S(2)}, u32[]{:S(2)}) collective-permute-start(bf16[320,384]{1,0:T(8,128)(2,1)S(1)} %collective-permute-done.10), channel_id=1, source_target_pairs={{0,256},{256,0},{1,257},{257,1},{2,258},{258,2},{3,259},{259,3},{4... | collective-permute-start | bytes 737288 | tf_op jit(solution)/shard_map/ppermute | solution.py:14
  186.3 7.0 %collective-permute-start.13 = (bf16[320,384]{1,0:T(8,128)(2,1)S(1)}, bf16[320,384]{1,0:T(8,128)(2,1)S(1)}, u32[]{:S(2)}, u32[]{:S(2)}) collective-permute-start(bf16[320,384]{1,0:T(8,128)(2,1)S(1)} %collective-permute-done.8), channel_id=1, source_target_pairs={{0,256},{256,0},{1,257},{257,1},{2,258},{258,2},{3,259},{259,3},{4... | collective-permute-start | bytes 737288 | tf_op jit(solution)/shard_map/ppermute | solution.py:14
  188.3 5.1 %collective-permute-start.15 = (bf16[160,384]{1,0:T(8,128)(2,1)S(1)}, bf16[160,384]{1,0:T(8,128)(2,1)S(1)}, u32[]{:S(2)}, u32[]{:S(2)}) collective-permute-start(bf16[160,384]{1,0:T(8,128)(2,1)S(1)} %collective-permute-done.11), channel_id=1, source_target_pairs={{0,256},{256,0},{1,257},{257,1},{2,258},{258,2},{3,259},{259,3},{4... | collective-permute-start | bytes 368648 | tf_op jit(solution)/shard_map/ppermute | solution.py:14
  190.7 3.2 %collective-permute-start.14 = (bf16[160,384]{1,0:T(8,128)(2,1)S(1)}, bf16[160,384]{1,0:T(8,128)(2,1)S(1)}, u32[]{:S(2)}, u32[]{:S(2)}) collective-permute-start(bf16[160,384]{1,0:T(8,128)(2,1)S(1)} %collective-permute-done.9), channel_id=1, source_target_pairs={{0,256},{256,0},{1,257},{257,1},{2,258},{258,2},{3,259},{259,3},{4... | collective-permute-start | bytes 368648 | tf_op jit(solution)/shard_map/ppermute | solution.py:14
  194.6 8.0 %copy-start.6 = (bf16[512,384]{1,0:T(8,128)(2,1)S(1)}, bf16[512,384]{1,0:T(8,128)(2,1)}, u32[]{:S(2)}) copy-start(bf16[512,384]{1,0:T(8,128)(2,1)} %copy-done.5) | copy-start | bytes 1179652
  194.6 8.0 %copy-start.8 = (bf16[512,384]{1,0:T(8,128)(2,1)S(1)}, bf16[512,384]{1,0:T(8,128)(2,1)}, u32[]{:S(2)}) copy-start(bf16[512,384]{1,0:T(8,128)(2,1)} %get-tuple-element.28) | copy-start | bytes 1179652
  194.6 8.0 %copy-start.10 = (bf16[512,384]{1,0:T(8,128)(2,1)S(1)}, bf16[512,384]{1,0:T(8,128)(2,1)}, u32[]{:S(2)}) copy-start(bf16[512,384]{1,0:T(8,128)(2,1)} %get-tuple-element.29) | copy-start | bytes 1179652
  194.6 8.0 %copy-start.12 = (bf16[512,384]{1,0:T(8,128)(2,1)S(1)}, bf16[512,384]{1,0:T(8,128)(2,1)}, u32[]{:S(2)}) copy-start(bf16[512,384]{1,0:T(8,128)(2,1)} %get-tuple-element.30) | copy-start | bytes 1179652
  195.9 46.3 %all-to-all-start.1 = ((bf16[64,40,128]{2,1,0:T(8,128)(2,1)}), bf16[64,40,128]{2,1,0:T(8,128)(2,1)S(1)}, u32[]{:S(2)}, u32[]{:S(2)}) async-start(bf16[64,40,128]{2,1,0:T(8,128)(2,1)} %reshape.103), calls=%async_computation.1 | async-start | bytes 1310720 | tf_op jit(solution)/shard_map/all_to_all | solution.py:102
  205.9 33.0 %copy-start.22 = (bf16[384,512]{1,0:T(8,128)(2,1)S(1)}, bf16[384,512]{1,0:T(8,128)(2,1)}, u32[]{:S(2)}) copy-start(bf16[384,512]{1,0:T(8,128)(2,1)} %get-tuple-element.7) | copy-start | bytes 1179652
  205.9 33.0 %copy-start.24 = (bf16[384,512]{1,0:T(8,128)(2,1)S(1)}, bf16[384,512]{1,0:T(8,128)(2,1)}, u32[]{:S(2)}) copy-start(bf16[384,512]{1,0:T(8,128)(2,1)} %get-tuple-element.8) | copy-start | bytes 1179652
  205.9 33.0 %copy-start.26 = (bf16[384,512]{1,0:T(8,128)(2,1)S(1)}, bf16[384,512]{1,0:T(8,128)(2,1)}, u32[]{:S(2)}) copy-start(bf16[384,512]{1,0:T(8,128)(2,1)} %get-tuple-element.9) | copy-start | bytes 1179652
  205.9 33.0 %copy-start.28 = (bf16[384,512]{1,0:T(8,128)(2,1)S(1)}, bf16[384,512]{1,0:T(8,128)(2,1)}, u32[]{:S(2)}) copy-start(bf16[384,512]{1,0:T(8,128)(2,1)} %get-tuple-element.10) | copy-start | bytes 1179652
  206.0 3.9 %collective-permute-start.21 = (bf16[320,768]{1,0:T(8,128)(2,1)S(1)}, bf16[320,768]{1,0:T(8,128)(2,1)S(1)}, u32[]{:S(2)}, u32[]{:S(2)}) collective-permute-start(bf16[320,768]{1,0:T(8,128)(2,1)S(1)} %fusion.4), channel_id=1, source_target_pairs={{0,256},{256,0},{1,257},{257,1},{2,258},{258,2},{3,259},{259,3},{4... | collective-permute-start | bytes 1474568 | tf_op jit(solution)/shard_map/ppermute | solution.py:14
  210.1 10.6 %collective-permute-start.24 = (bf16[320,384]{1,0:T(8,128)(2,1)S(1)}, bf16[320,384]{1,0:T(8,128)(2,1)S(1)}, u32[]{:S(2)}, u32[]{:S(2)}) collective-permute-start(bf16[320,384]{1,0:T(8,128)(2,1)S(1)} %fusion.47), channel_id=1, source_target_pairs={{0,3},{1,0},{2,1},{3,2},{4,7},{5,4},{6,5},{7,6},{8,11},{9,8},{10,9... | collective-permute-start | bytes 737288 | tf_op jit(solution)/shard_map/ppermute | solution.py:14
  215.2 11.1 %collective-permute-start.22 = (bf16[320,384]{1,0:T(8,128)(2,1)S(1)}, bf16[320,384]{1,0:T(8,128)(2,1)S(1)}, u32[]{:S(2)}, u32[]{:S(2)}) collective-permute-start(bf16[320,384]{1,0:T(8,128)(2,1)S(1)} %fusion.47), channel_id=1, source_target_pairs={{0,1},{1,2},{2,3},{3,0},{4,5},{5,6},{6,7},{7,4},{8,9},{9,10},{10,1... | collective-permute-start | bytes 737288 | tf_op jit(solution)/shard_map/ppermute | solution.py:14
  220.7 13.8 %collective-permute-start.25 = (bf16[160,384]{1,0:T(8,128)(2,1)S(1)}, bf16[160,384]{1,0:T(8,128)(2,1)S(1)}, u32[]{:S(2)}, u32[]{:S(2)}) collective-permute-start(bf16[160,384]{1,0:T(8,128)(2,1)S(1)} %slice.59), channel_id=1, source_target_pairs={{0,3},{1,0},{2,1},{3,2},{4,7},{5,4},{6,5},{7,6},{8,11},{9,8},{10,9... | collective-permute-start | bytes 368648 | tf_op jit(solution)/shard_map/ppermute | solution.py:14
  226.4 10.6 %collective-permute-start.23 = (bf16[160,384]{1,0:T(8,128)(2,1)S(1)}, bf16[160,384]{1,0:T(8,128)(2,1)S(1)}, u32[]{:S(2)}, u32[]{:S(2)}) collective-permute-start(bf16[160,384]{1,0:T(8,128)(2,1)S(1)} %slice.58), channel_id=1, source_target_pairs={{0,1},{1,2},{2,3},{3,0},{4,5},{5,6},{6,7},{7,4},{8,9},{9,10},{10,1... | collective-permute-start | bytes 368648 | tf_op jit(solution)/shard_map/ppermute | solution.py:14
  228.3 11.4 %collective-permute-start.26 = (bf16[320,384]{1,0:T(8,128)(2,1)S(1)}, bf16[320,384]{1,0:T(8,128)(2,1)S(1)}, u32[]{:S(2)}, u32[]{:S(2)}) collective-permute-start(bf16[320,384]{1,0:T(8,128)(2,1)S(1)} %fusion.47), channel_id=1, source_target_pairs={{0,256},{256,0},{1,257},{257,1},{2,258},{258,2},{3,259},{259,3},{4... | collective-permute-start | bytes 737288 | tf_op jit(solution)/shard_map/ppermute | solution.py:14
  230.2 9.4 %collective-permute-start.30 = (bf16[320,384]{1,0:T(8,128)(2,1)S(1)}, bf16[320,384]{1,0:T(8,128)(2,1)S(1)}, u32[]{:S(2)}, u32[]{:S(2)}) collective-permute-start(bf16[320,384]{1,0:T(8,128)(2,1)S(1)} %collective-permute-done.24), channel_id=1, source_target_pairs={{0,256},{256,0},{1,257},{257,1},{2,258},{258,2},{3,259},{259,3},{4... | collective-permute-start | bytes 737288 | tf_op jit(solution)/shard_map/ppermute | solution.py:14
  232.7 7.0 %collective-permute-start.27 = (bf16[320,384]{1,0:T(8,128)(2,1)S(1)}, bf16[320,384]{1,0:T(8,128)(2,1)S(1)}, u32[]{:S(2)}, u32[]{:S(2)}) collective-permute-start(bf16[320,384]{1,0:T(8,128)(2,1)S(1)} %collective-permute-done.22), channel_id=1, source_target_pairs={{0,256},{256,0},{1,257},{257,1},{2,258},{258,2},{3,259},{259,3},{4... | collective-permute-start | bytes 737288 | tf_op jit(solution)/shard_map/ppermute | solution.py:14
  234.6 5.1 %collective-permute-start.29 = (bf16[160,384]{1,0:T(8,128)(2,1)S(1)}, bf16[160,384]{1,0:T(8,128)(2,1)S(1)}, u32[]{:S(2)}, u32[]{:S(2)}) collective-permute-start(bf16[160,384]{1,0:T(8,128)(2,1)S(1)} %collective-permute-done.25), channel_id=1, source_target_pairs={{0,256},{256,0},{1,257},{257,1},{2,258},{258,2},{3,259},{259,3},{4... | collective-permute-start | bytes 368648 | tf_op jit(solution)/shard_map/ppermute | solution.py:14
  237.0 3.2 %collective-permute-start.28 = (bf16[160,384]{1,0:T(8,128)(2,1)S(1)}, bf16[160,384]{1,0:T(8,128)(2,1)S(1)}, u32[]{:S(2)}, u32[]{:S(2)}) collective-permute-start(bf16[160,384]{1,0:T(8,128)(2,1)S(1)} %collective-permute-done.23), channel_id=1, source_target_pairs={{0,256},{256,0},{1,257},{257,1},{2,258},{258,2},{3,259},{259,3},{4... | collective-permute-start | bytes 368648 | tf_op jit(solution)/shard_map/ppermute | solution.py:14
  240.9 16.6 %copy-start.32 = (bf16[512,64]{0,1:T(8,128)(2,1)S(1)}, bf16[512,64]{0,1:T(8,128)(2,1)}, u32[]{:S(2)}) copy-start(bf16[512,64]{0,1:T(8,128)(2,1)} %param.7) | copy-start | bytes 196612
  242.3 33.8 %copy-start.4 = (pred[128,640]{1,0:T(32,128)(4,1)S(1)}, pred[128,640]{1,0:T(32,128)(4,1)}, u32[]{:S(2)}) copy-start(pred[128,640]{1,0:T(32,128)(4,1)} %copy-done.3) | copy-start | bytes 245764
  242.3 52.9 %all-to-all-start.3 = ((bf16[64,40,128]{2,1,0:T(8,128)(2,1)}), bf16[64,40,128]{2,1,0:T(8,128)(2,1)S(1)}, u32[]{:S(2)}, u32[]{:S(2)}) async-start(bf16[64,40,128]{2,1,0:T(8,128)(2,1)} %reshape.110), calls=%async_computation.3 | async-start | bytes 1310720 | tf_op jit(solution)/shard_map/all_to_all | solution.py:102
  257.7 3.1 %collective-permute-start = (f32[128,64]{0,1:T(8,128)S(1)}, f32[128,64]{0,1:T(8,128)S(1)}, u32[]{:S(2)}, u32[]{:S(2)}) collective-permute-start(f32[128,64]{0,1:T(8,128)S(1)} %fusion.94), channel_id=1, source_target_pairs={{0,256},{256,0},{1,257},{257,1},{2,258},{258,2},{3,259},{259,3},{4... | collective-permute-start | bytes 98312 | tf_op jit(solution)/shard_map/ppermute | solution.py:14
  260.8 7.0 %collective-permute-start.1 = (f32[128,64]{0,1:T(8,128)S(1)}, f32[128,64]{0,1:T(8,128)S(1)}, u32[]{:S(2)}, u32[]{:S(2)}) collective-permute-start(f32[128,64]{0,1:T(8,128)S(1)} %add.125), channel_id=1, source_target_pairs={{0,1},{1,2},{2,3},{3,0},{4,5},{5,6},{6,7},{7,4},{8,9},{9,10},{10,1... | collective-permute-start | bytes 98312 | tf_op jit(solution)/shard_map/ppermute | solution.py:14
  267.8 7.3 %collective-permute-start.2 = (f32[128,64]{0,1:T(8,128)S(1)}, f32[128,64]{0,1:T(8,128)S(1)}, u32[]{:S(2)}, u32[]{:S(2)}) collective-permute-start(f32[128,64]{0,1:T(8,128)S(1)} %add.126), channel_id=1, source_target_pairs={{0,2},{1,3},{2,0},{3,1},{4,6},{5,7},{6,4},{7,5},{8,10},{9,11},{10,... | collective-permute-start | bytes 98312 | tf_op jit(solution)/shard_map/ppermute | solution.py:14
  (4 other events, 6.7 us)

commit v2 on v0

v2 whole, which is shorter than its diff:
```python
import jax
import jax.numpy as jnp
from jax import lax
from jax.experimental import pallas as pl
from jax.experimental.pallas import tpu as pltpu
from jax.sharding import PartitionSpec as P

EXPERTS = 64
TOP = 8
SLOTS = 10
BF = jnp.bfloat16
F32 = jnp.float32
VMEM = pl.BlockSpec(memory_space=pltpu.VMEM)
SMEM = pl.BlockSpec(memory_space=pltpu.SMEM)


def call(body, outs, args, scalars=False, flops=0):
    specs = [SMEM if scalars and i == 0 else VMEM for i in range(len(args))]
    moved = sum(a.size * a.dtype.itemsize for a in args)
    return pl.pallas_call(
        body,
        out_shape=[jax.ShapeDtypeStruct(*o) for o in outs],
        in_specs=specs,
        out_specs=[VMEM] * len(outs),
        compiler_params=pltpu.CompilerParams(vmem_limit_bytes=44 << 20),
        cost_estimate=pl.CostEstimate(flops=flops, bytes_accessed=moved, transcendentals=0),
    )(*args)


def iota(shape, dim):
    return lax.broadcasted_iota(jnp.int32, shape, dim)


def ones_where(condition):
    return jnp.where(condition, F32(1.0), F32(0.0)).astype(BF)


def dot(a, b):
    return jnp.dot(a, b, preferred_element_type=F32)


def pack(extra):
    n = extra.shape[0]
    shape = (4 * n, n)
    total = jnp.zeros((4 * n, 128), F32)
    for f in range(4):
        total = total + dot(ones_where(iota(shape, 0) == 4 * iota(shape, 1) + f), extra[:, f * 128:(f + 1) * 128])
    return total.astype(BF)


def unpack(pieces):
    n = pieces.shape[0] // 4
    shape = (n, 4 * n)
    parts = [dot(ones_where(iota(shape, 1) == 4 * iota(shape, 0) + f), pieces).astype(BF) for f in range(4)]
    return jnp.concatenate(parts, axis=1)


def rows_of(half):
    return jnp.concatenate([half[:, :512], unpack(half[:, 512:])], axis=0)


def select_body(ids_ref, tokens_ref, a_ref, b_ref):
    ids = ids_ref[...]
    rows = tokens_ref.shape[0]
    shape = (EXPERTS, rows)
    chosen = jnp.zeros(shape, F32)
    for k in range(TOP):
        chosen = chosen + jnp.where(ids[k:k + 1, :] == iota(shape, 0), F32(1.0), F32(0.0))
    square = (rows, rows)
    rank = dot(chosen.astype(BF), ones_where(iota(square, 0) < iota(square, 1)))
    slot = jnp.where(chosen > 0, rank, F32(-1.0)).astype(BF)
    big, small = (EXPERTS * 8, EXPERTS), (EXPERTS * 2, EXPERTS)
    wide = dot(ones_where((iota(big, 0) >> 3) == iota(big, 1)), slot)
    wide2 = dot(ones_where((iota(small, 0) >> 1) == iota(small, 1)), slot)
    number = (iota(wide.shape, 0) & 7).astype(F32)
    number2 = (iota(wide2.shape, 0) & 1).astype(F32)
    tokens = tokens_ref[...]
    for c, ref in enumerate((a_ref, b_ref)):
        ref[:, :512] = dot(ones_where(wide == number + SLOTS * c), tokens).astype(BF)
        extra = dot(ones_where(wide2 == number2 + (SLOTS * c + 8)), tokens).astype(BF)
        ref[:, 512:] = pack(extra)


def near_body(place_ref, own_ref, b_lo, b_hi, a_lo, a_hi, gate_ref, up_ref, acc_ref):
    me = place_ref[0]
    for h in range(2):
        sources = (own_ref[h * 256:(h + 1) * 256, :], (b_lo, b_hi)[h][...], (a_lo, a_hi)[h][...])
        gate = jnp.zeros((320, 384), F32)
        up = jnp.zeros((320, 384), F32)
        for back, half in zip((0, 1, 3), sources):
            at = pl.ds(pl.multiple_of(((me + 4 - back) & 3) * 512, 512), 512)
            features = rows_of(half)
            gate = gate + dot(features, gate_ref[at, :])
            up = up + dot(features, up_ref[at, :])
        acc_ref[h * 320:(h + 1) * 320, :384] = gate
        acc_ref[h * 320:(h + 1) * 320, 384:] = up


def far_body(place_ref, lo, hi, acc_ref, gate_ref, up_ref, kept_ref, sent_ref):
    me = place_ref[0]
    first = place_ref[1] == 0
    at = pl.ds(pl.multiple_of(((me + 2) & 3) * 512, 512), 512)
    features = [rows_of(lo[...]), rows_of(hi[...])]
    for ref, columns in ((gate_ref, slice(0, 384)), (up_ref, slice(384, 768))):
        weight = ref[at, :]
        low = acc_ref[:320, columns] + dot(features[0], weight)
        high = acc_ref[320:, columns] + dot(features[1], weight)
        kept_ref[:, columns] = jnp.where(first, low, high)
        sent_ref[:, columns] = jnp.where(first, high, low).astype(BF)


def act_body(kept_ref, got_ref, hidden_ref):
    gate = kept_ref[:, :384] + got_ref[:, :384].astype(F32)
    up = kept_ref[:, 384:] + got_ref[:, 384:].astype(F32)
    hidden_ref[...] = (gate / (1.0 + jnp.exp(-gate)) * up).astype(BF)


def join_body(own, behind, far_lo, far_hi, ahead, full_ref):
    full_ref[:, :384] = own[...]
    full_ref[:, 384:768] = behind[...]
    full_ref[:160, 768:1152] = far_lo[...]
    full_ref[160:, 768:1152] = far_hi[...]
    full_ref[:, 1152:] = ahead[...]


def down_body(place_ref, full_ref, other_ref, down_ref, out_ref):
    me = place_ref[0]
    first = place_ref[1] == 0
    outs = []
    for ref in (full_ref, other_ref):
        total = jnp.zeros((320, 512), F32)
        for i in range(4):
            at = pl.ds(pl.multiple_of(((me + 4 - i) & 3) * 384, 384), 384)
            total = total + dot(ref[:, i * 384:(i + 1) * 384], down_ref[at, :])
        outs.append(total)
    ordered = (jnp.where(first, outs[0], outs[1]), jnp.where(first, outs[1], outs[0]))
    for h in range(2):
        rows = ordered[h].astype(BF)
        out_ref[h * 256:(h + 1) * 256, :512] = rows[:256]
        out_ref[h * 256:(h + 1) * 256, 512:] = pack(rows[256:])


def slots_of(ids):
    rows = ids.shape[0]
    shape = (rows, EXPERTS)
    chosen = jnp.zeros(shape, F32)
    for k in range(TOP):
        chosen = chosen + jnp.where(ids[:, k:k + 1] == iota(shape, 1), F32(1.0), F32(0.0))
    square = (rows, rows)
    rank = dot(ones_where(iota(square, 0) > iota(square, 1)), chosen.astype(BF))
    return chosen, jnp.where(chosen > 0, rank, F32(-1.0))


def weighted(slot, probs, block, c):
    slot = slot.astype(BF)
    high = probs.astype(BF)
    low = (probs - high.astype(F32)).astype(BF)
    total = jnp.zeros((slot.shape[0], 512), F32)
    for per, start, rows in ((8, 0, block[:, :512]), (2, 8, unpack(block[:, 512:]))):
        shape = (EXPERTS, EXPERTS * per)
        spread = ones_where((iota(shape, 1) >> (3 if per == 8 else 1)) == iota(shape, 0))
        wide = dot(slot, spread)
        number = (iota(wide.shape, 1) & (per - 1)).astype(F32) + (SLOTS * c + start)
        for part in (high, low):
            weight = jnp.where(wide == number, dot(part, spread), F32(0.0)).astype(BF)
            total = total + dot(weight, rows)
    return total


def combine_a_body(ids_ref, logits_ref, block_ref, acc_ref, probs_ref, slot_ref):
    chosen, slot = slots_of(ids_ref[...])
    raised = jnp.where(chosen > 0, jnp.exp(logits_ref[...]), F32(0.0))
    probs = raised / jnp.sum(raised, axis=1, keepdims=True)
    probs_ref[...] = probs
    slot_ref[...] = slot
    acc_ref[...] = weighted(slot, probs, block_ref[...], 0)


def combine_b_body(acc_ref, probs_ref, slot_ref, block_ref, out_ref):
    out_ref[...] = (acc_ref[...] + weighted(slot_ref[...], probs_ref[...], block_ref[...], 1)).astype(BF)


def shift(x, axis, size, by):
    return lax.ppermute(x, axis, [(i, (i + by) % size) for i in range(size)])


def exchange(x):
    return lax.all_to_all(x, "ep", split_axis=0, concat_axis=0, tiled=True)


def gather_features(block):
    lo, hi = block[:256], block[256:]
    b_lo = shift(lo, "tp", 4, 1)
    a_hi = shift(hi, "tp", 4, -1)
    b_hi = shift(hi, "tp", 4, 1)
    a_lo = shift(lo, "tp", 4, -1)
    return b_lo, b_hi, a_lo, a_hi, shift(b_lo, "tp", 4, 1), shift(a_hi, "tp", 4, -1)


def expand(place, block, gate_w, up_w):
    b_lo, b_hi, a_lo, a_hi, far_lo, far_hi = gather_features(block)
    acc, = call(near_body, [((640, 768), F32)], (place, block, b_lo, b_hi, a_lo, a_hi, gate_w, up_w), True, 3 << 29)
    kept, sent = call(
        far_body, [((320, 768), F32), ((320, 768), BF)], (place, far_lo, far_hi, acc, gate_w, up_w), True, 1 << 29
    )
    hidden, = call(act_body, [((320, 384), BF)], (kept, shift(sent, "sec", 2, 1)))
    return hidden


def contract(place, hidden, down_w):
    behind = shift(hidden, "tp", 4, 1)
    ahead = shift(hidden, "tp", 4, -1)
    far_lo = shift(behind[:160], "tp", 4, 1)
    far_hi = shift(ahead[160:], "tp", 4, -1)
    full, = call(join_body, [((320, 1536), BF)], (hidden, behind, far_lo, far_hi, ahead))
    produced, = call(down_body, [((512, 640), BF)], (place, full, shift(full, "sec", 2, 1), down_w), True, 1 << 30)
    return produced


def per_device(tokens, router_weight, expert_ids, gate_weight, up_weight, down_weight):
    place = jnp.stack([lax.axis_index("tp"), lax.axis_index("sec")]).astype(jnp.int32)
    gate_w, up_w, down_w = gate_weight[0], up_weight[0], down_weight[0]
    outgoing = call(select_body, [((512, 640), BF)] * 2, (expert_ids.T, tokens))
    block_a, block_b = exchange(outgoing[0]), exchange(outgoing[1])

    hidden_a = expand(place, block_a, gate_w, up_w)
    block_b, _ = lax.optimization_barrier((block_b, hidden_a))
    produced_a = contract(place, hidden_a, down_w)
    back_a = exchange(produced_a)
    hidden_b = expand(place, block_b, gate_w, up_w)
    produced_b = contract(place, hidden_b, down_w)
    produced_b, back_a = lax.optimization_barrier((produced_b, back_a))
    back_b = exchange(produced_b)

    logits = dot(tokens, router_weight)
    logits, _ = lax.optimization_barrier((logits, produced_b))
    logits = logits + shift(logits, "sec", 2, 1)
    logits = logits + shift(logits, "tp", 4, 1)
    logits = logits + shift(logits, "tp", 4, 2)
    table = ((128, EXPERTS), F32)
    acc, probs, slot = call(combine_a_body, [((128, 512), F32), table, table], (expert_ids, logits, back_a))
    mixture, = call(combine_b_body, [((128, 512), BF)], (acc, probs, slot, back_b))
    return mixture


def solution(mesh):
    placed = (
        P("ep", ("sec", "tp")),
        P(("sec", "tp"), None),
        P("ep", None),
        P("ep", "sec", "tp"),
        P("ep", "sec", "tp"),
        P("ep", None, ("sec", "tp")),
    )
    return jax.shard_map(
        per_device, mesh=mesh, in_specs=placed, out_specs=P("ep", ("sec", "tp")), check_vma=False
    )
```

time: 615 us -> 269 us (0.44)
  blocking collectives: 334 us -> 56 us
  starting transfers between devices: 16.3 us -> 123 us
  waiting for transfers between devices: 132 us -> 53.4 us
  local copies, waits for them, and re-layouts: 67.4 us -> 10.8 us
  other arithmetic: 34.7 us -> 0.1 us
  Pallas kernels: 0 us -> 23.6 us
  matrix products: 16 us -> 0.16 us
  between operations: 13.5 us -> 0.53 us
    all_to_all x1, blocking collectives: 295 us -> 56 us  [exchange(): return lax.all_to_all(x, 'ep', split_axis=0, concat_axis=0, tiled=True)]
    ppermute x0 -> x27, starting transfers between devices: none -> 85 us  [shift(): return lax.ppermute(x, axis, [(i, (i + by) % size) for i in range(size)])]
    all_gather x1 -> x0, waiting for transfers between devices: 55.3 us -> none  [per_device(): lax.all_gather(hidden, 'tp', axis=2, tiled=True)]
    ppermute x0 -> x27, waiting for transfers between devices: none -> 37.2 us  [shift(): return lax.ppermute(x, axis, [(i, (i + by) % size) for i in range(size)])]
    psum x1 -> x0, waiting for transfers between devices: 37 us -> none  [per_device(): gate_acts, up_acts = lax.psum((gate_half, up_half), 'sec')]
    psum x1 -> x0, blocking collectives: 25.1 us -> none  [per_device(): logits = lax.psum(partial_logits, ('sec', 'tp'))]
    pallas_call x0 -> x13, Pallas kernels: none -> 23.6 us  [call(): pl.pallas_call(body, out_shape=[jax.ShapeDtypeStruct(*o) for o in outs],...]
    all_to_all x1 -> x3, waiting for transfers between devices: 39.7 us -> 16.2 us  [exchange(): return lax.all_to_all(x, 'ep', split_axis=0, concat_axis=0, tiled=True)]
  transfers between devices with their start and end apart: 3 -> 30, of which waited for: 3 -> 18; matrix products, arithmetic and copies ran while one was open for 0% -> 2% of each run, Pallas kernels for 0% -> 8%
where the time goes in v2:
time: 269 us; the launch traced here: 267 us
  starting transfers between devices  123 us (46%)
  blocking collectives  56 us (21%)
  waiting for transfers between devices  53.4 us (20%)
  Pallas kernels  23.6 us (9%)
  local copies, waits for them, and re-layouts  10.8 us (4%)
    ppermute x27, starting transfers between devices, shift(): return lax.ppermute(x, axis, [(i, (i + by) % size) for i in range(size)])  85 us
    all_to_all x1, blocking collectives, exchange(): return lax.all_to_all(x, 'ep', split_axis=0, concat_axis=0, tiled=True)  56 us
    all_to_all x3, starting transfers between devices, exchange(): return lax.all_to_all(x, 'ep', split_axis=0, concat_axis=0, tiled=True)  37.5 us
    ppermute x27, waiting for transfers between devices, shift(): return lax.ppermute(x, axis, [(i, (i + by) % size) for i in range(size)])  37.2 us
    pallas_call x13, Pallas kernels, call(): pl.pallas_call(body, out_shape=[jax.ShapeDtypeStruct(*o) for o in outs],...  23.6 us
    all_to_all x3, waiting for transfers between devices, exchange(): return lax.all_to_all(x, 'ep', split_axis=0, concat_axis=0, tiled=True)  16.2 us
    unnamed x27, local copies, waits for them, and re-layouts  6.75 us
  transfers between devices with their start and end apart: 30, of which 18 were waited for; matrix products, arithmetic and copies ran while one was open for 2% of the time, Pallas kernels for 8%

profile of v2, /device:TPU:6, one launch (start us, length us, event | category | flops | bytes accessed | tf_op | source)
XLA Modules:
  0.0 267.3 jit_solution(12285766279137855789)
XLA Ops:
  0.0 0.9 copy-done.9
  1.6 1.5 shard_map.64
  3.2 0.8 copy-done.8
  4.0 56.0 %all_to_all.46 = bf16[64,8,640]{2,1,0:T(8,128)(2,1)} all-to-all(bf16[64,8,640]{2,1,0:T(8,128)(2,1)S(1)} %bitcast.35), channel_id=1, replica_groups=mesh['sec'=2,'ep'=64,'tp'=4] {'ep'}, dimensions={0} | all-to-all | bytes 1310720 | tf_op jit(solution)/shard_map/all_to_all | solution.py:188
  60.0 7.0 %all-to-all-start = ((bf16[64,8,640]{2,1,0:T(8,128)(2,1)}), bf16[64,8,640]{2,1,0:T(8,128)(2,1)}, u32[]{:S(2)}, u32[]{:S(2)}) async-start(bf16[64,8,640]{2,1,0:T(8,128)(2,1)} %bitcast.34), calls=%async_computation | async-start | bytes 1310720 | tf_op jit(solution)/shard_map/all_to_all | solution.py:188
  67.0 2.0 slice_bitcast_fusion
  69.0 3.5 %collective-permute-start = (bf16[256,640]{1,0:T(8,128)(2,1)}, bf16[256,640]{1,0:T(8,128)(2,1)S(1)}, u32[]{:S(2)}, u32[]{:S(2)}) collective-permute-start(bf16[256,640]{1,0:T(8,128)(2,1)} %get-tuple-element.34), channel_id=1, source_target_pairs={{0,1},{1,2},{2,3},{3,0},{4,5},{5,6},{6,7},{7,4},{8,9},{9,10},{10,1... | collective-permute-start | bytes 983048 | tf_op jit(solution)/shard_map/ppermute | solution.py:184
  72.5 3.6 %collective-permute-start.2 = (bf16[256,640]{1,0:T(8,128)(2,1)}, bf16[256,640]{1,0:T(8,128)(2,1)}, u32[]{:S(2)}, u32[]{:S(2)}) collective-permute-start(bf16[256,640]{1,0:T(8,128)(2,1)} %get-tuple-element.33), channel_id=1, source_target_pairs={{0,3},{1,0},{2,1},{3,2},{4,7},{5,4},{6,5},{7,6},{8,11},{9,8},{10,9... | collective-permute-start | bytes 983048 | tf_op jit(solution)/shard_map/ppermute | solution.py:184
  76.0 2.3 collective-permute-start.4
  78.3 4.8 %collective-permute-start.5 = (bf16[256,640]{1,0:T(8,128)(2,1)}, bf16[256,640]{1,0:T(8,128)(2,1)}, u32[]{:S(2)}, u32[]{:S(2)}) collective-permute-start(bf16[256,640]{1,0:T(8,128)(2,1)} %get-tuple-element.34), channel_id=1, source_target_pairs={{0,3},{1,0},{2,1},{3,2},{4,7},{5,4},{6,5},{7,6},{8,11},{9,8},{10,9... | collective-permute-start | bytes 983048 | tf_op jit(solution)/shard_map/ppermute | solution.py:184
  83.1 1.9 collective-permute-start.1
  85.1 5.1 %collective-permute-start.3 = (bf16[256,640]{1,0:T(8,128)(2,1)}, bf16[256,640]{1,0:T(8,128)(2,1)}, u32[]{:S(2)}, u32[]{:S(2)}) collective-permute-start(bf16[256,640]{1,0:T(8,128)(2,1)} %collective-permute-done.2.a_hi), channel_id=1, source_target_pairs={{0,3},{1,0},{2,1},{3,2},{4,7},{5,4},{6,5},{7,6},{8,11},{9,8},{10,9... | collective-permute-start | bytes 983048 | tf_op jit(solution)/shard_map/ppermute | solution.py:184
  90.3 1.4 collective-permute-done.5.a_lo
  91.7 1.1 copy-done.5
  92.8 3.7 %shard_map.65.acc_ref = f32[640,768]{1,0:T(8,128)S(1)} custom-call(s32[2]{0:T(128)S(1)} %pad_add_fusion.place_ref, bf16[512,640]{1,0:T(8,128)(2,1)S(1)} %bitcast.30, bf16[256,640]{1,0:T(8,128)(2,1)S(1)} %collective-permute-done.b_lo, bf16[256,640]{1,0:T(8,128)(2,1)} %collective-permute-done.4.b_hi, bf16[256,640]{1,0:T(8,128)(2,1)} %collective-permute-done.5.a_lo, ...), custom_call_target="tpu_custom_call" | custom-call | flops 1610612736 | bytes 5111816 | tf_op jit(solution)/shard_map/pallas_call | solution.py:20
  97.1 2.0 shard_map.66
  99.1 1.9 collective-permute-start.6
  101.1 1.8 collective-permute-done.6.got_ref
  103.1 3.5 %collective-permute-start.19 = (bf16[320,384]{1,0:T(8,128)(2,1)S(1)}, bf16[320,384]{1,0:T(8,128)(2,1)S(1)}, u32[]{:S(2)}, u32[]{:S(2)}) collective-permute-start(bf16[320,384]{1,0:T(8,128)(2,1)S(1)} %shard_map.67.own), channel_id=1, source_target_pairs={{0,1},{1,2},{2,3},{3,0},{4,5},{5,6},{6,7},{7,4},{8,9},{9,10},{10,1... | collective-permute-start | bytes 737288 | tf_op jit(solution)/shard_map/ppermute | solution.py:184
  106.6 3.6 %collective-permute-start.21 = (bf16[320,384]{1,0:T(8,128)(2,1)S(1)}, bf16[320,384]{1,0:T(8,128)(2,1)S(1)}, u32[]{:S(2)}, u32[]{:S(2)}) collective-permute-start(bf16[320,384]{1,0:T(8,128)(2,1)S(1)} %shard_map.67.own), channel_id=1, source_target_pairs={{0,3},{1,0},{2,1},{3,2},{4,7},{5,4},{6,5},{7,6},{8,11},{9,8},{10,9... | collective-permute-start | bytes 737288 | tf_op jit(solution)/shard_map/ppermute | solution.py:184
  110.2 4.0 %collective-permute-done.19.behind = bf16[320,384]{1,0:T(8,128)(2,1)S(1)} collective-permute-done((bf16[320,384]{1,0:T(8,128)(2,1)S(1)}, bf16[320,384]{1,0:T(8,128)(2,1)S(1)}, u32[]{:S(2)}, u32[]{:S(2)}) %collective-permute-start.19) | collective-permute-done | bytes 245792 | tf_op jit(solution)/shard_map/ppermute | solution.py:184
  114.2 2.3 collective-permute-start.20
  116.5 4.8 %collective-permute-start.22 = (bf16[160,384]{1,0:T(8,128)(2,1)S(1)}, bf16[160,384]{1,0:T(8,128)(2,1)S(1)}, u32[]{:S(2)}, u32[]{:S(2)}) collective-permute-start(bf16[160,384]{1,0:T(8,128)(2,1)S(1)} %slice.45), channel_id=1, source_target_pairs={{0,3},{1,0},{2,1},{3,2},{4,7},{5,4},{6,5},{7,6},{8,11},{9,8},{10,9... | collective-permute-start | bytes 368648 | tf_op jit(solution)/shard_map/ppermute | solution.py:184
  121.3 0.9 collective-permute-done.20.far_lo
  122.2 1.5 collective-permute-done.22.far_hi
  123.7 1.1 shard_map.73.full_ref
  124.8 1.9 collective-permute-start.23
  126.7 2.0 fusion
  128.7 2.7 %collective-permute-start.7 = (bf16[256,640]{1,0:T(8,128)(2,1)}, bf16[256,640]{1,0:T(8,128)(2,1)S(1)}, u32[]{:S(2)}, u32[]{:S(2)}) collective-permute-start(bf16[256,640]{1,0:T(8,128)(2,1)} %get-tuple-element.32), channel_id=1, source_target_pairs={{0,1},{1,2},{2,3},{3,0},{4,5},{5,6},{6,7},{7,4},{8,9},{9,10},{10,1... | collective-permute-start | bytes 983048 | tf_op jit(solution)/shard_map/ppermute | solution.py:184
  131.4 4.7 %collective-permute-start.9 = (bf16[256,640]{1,0:T(8,128)(2,1)}, bf16[256,640]{1,0:T(8,128)(2,1)}, u32[]{:S(2)}, u32[]{:S(2)}) collective-permute-start(bf16[256,640]{1,0:T(8,128)(2,1)} %get-tuple-element.31), channel_id=1, source_target_pairs={{0,3},{1,0},{2,1},{3,2},{4,7},{5,4},{6,5},{7,6},{8,11},{9,8},{10,9... | collective-permute-start | bytes 983048 | tf_op jit(solution)/shard_map/ppermute | solution.py:184
  136.2 1.4 copy-done.3
  137.6 3.3 %shard_map.74 = bf16[512,640]{1,0:T(8,128)(2,1)S(1)} custom-call(s32[2]{0:T(128)S(1)} %pad_add_fusion.place_ref, bf16[320,1536]{1,0:T(8,128)(2,1)} %shard_map.73.full_ref, bf16[320,1536]{1,0:T(8,128)(2,1)} %collective-permute-done.23.other_ref, bf16[1536,512]{1,0:T(8,128)(2,1)S(1)} %bitcast.28), custom_call_target="tpu_custom_call" | custom-call | flops 1073741824 | bytes 3538952 | tf_op jit(solution)/shard_map/pallas_call | solution.py:20
  141.7 15.3 %all-to-all-start.2 = ((bf16[64,8,640]{2,1,0:T(8,128)(2,1)}), bf16[64,8,640]{2,1,0:T(8,128)(2,1)}, u32[]{:S(2)}, u32[]{:S(2)}) async-start(bf16[64,8,640]{2,1,0:T(8,128)(2,1)} %bitcast.31), calls=%async_computation.2 | async-start | bytes 1310720 | tf_op jit(solution)/shard_map/all_to_all | solution.py:188
  157.0 1.9 collective-permute-start.11
  159.0 5.1 %collective-permute-start.12 = (bf16[256,640]{1,0:T(8,128)(2,1)}, bf16[256,640]{1,0:T(8,128)(2,1)S(1)}, u32[]{:S(2)}, u32[]{:S(2)}) collective-permute-start(bf16[256,640]{1,0:T(8,128)(2,1)} %get-tuple-element.32), channel_id=1, source_target_pairs={{0,3},{1,0},{2,1},{3,2},{4,7},{5,4},{6,5},{7,6},{8,11},{9,8},{10,9... | collective-permute-start | bytes 983048 | tf_op jit(solution)/shard_map/ppermute | solution.py:184
  164.1 2.7 %collective-permute-start.10 = (bf16[256,640]{1,0:T(8,128)(2,1)}, bf16[256,640]{1,0:T(8,128)(2,1)S(1)}, u32[]{:S(2)}, u32[]{:S(2)}) collective-permute-start(bf16[256,640]{1,0:T(8,128)(2,1)} %collective-permute-done.9.a_hi), channel_id=1, source_target_pairs={{0,3},{1,0},{2,1},{3,2},{4,7},{5,4},{6,5},{7,6},{8,11},{9,8},{10,9... | collective-permute-start | bytes 983048 | tf_op jit(solution)/shard_map/ppermute | solution.py:184
  166.8 3.1 %collective-permute-start.8 = (bf16[256,640]{1,0:T(8,128)(2,1)S(1)}, bf16[256,640]{1,0:T(8,128)(2,1)S(1)}, u32[]{:S(2)}, u32[]{:S(2)}) collective-permute-start(bf16[256,640]{1,0:T(8,128)(2,1)S(1)} %collective-permute-done.7.b_lo), channel_id=1, source_target_pairs={{0,1},{1,2},{2,3},{3,0},{4,5},{5,6},{6,7},{7,4},{8,9},{9,10},{10,1... | collective-permute-start | bytes 983048 | tf_op jit(solution)/shard_map/ppermute | solution.py:184
  170.0 2.6 collective-permute-done.12.a_lo
  172.6 3.7 %shard_map.68.acc_ref = f32[640,768]{1,0:T(8,128)S(1)} custom-call(s32[2]{0:T(128)S(1)} %pad_add_fusion.place_ref, bf16[512,640]{1,0:T(8,128)(2,1)} %bitcast.4.own_ref, bf16[256,640]{1,0:T(8,128)(2,1)S(1)} %collective-permute-done.7.b_lo, bf16[256,640]{1,0:T(8,128)(2,1)S(1)} %collective-permute-done.11.b_hi, ...), custom_call_target="tpu_custom_call" | custom-call | flops 1610612736 | bytes 5111816 | tf_op jit(solution)/shard_map/pallas_call | solution.py:20
  176.3 1.6 collective-permute-done.10.hi
  178.1 1.5 shard_map.69
  179.6 2.1 collective-permute-start.13
  181.7 1.6 collective-permute-done.13.got_ref
  183.6 2.4 collective-permute-start.14
  186.0 4.9 %collective-permute-start.16 = (bf16[320,384]{1,0:T(8,128)(2,1)S(1)}, bf16[320,384]{1,0:T(8,128)(2,1)S(1)}, u32[]{:S(2)}, u32[]{:S(2)}) collective-permute-start(bf16[320,384]{1,0:T(8,128)(2,1)S(1)} %shard_map.70.own), channel_id=1, source_target_pairs={{0,3},{1,0},{2,1},{3,2},{4,7},{5,4},{6,5},{7,6},{8,11},{9,8},{10,9... | collective-permute-start | bytes 737288 | tf_op jit(solution)/shard_map/ppermute | solution.py:184
  191.0 4.3 %collective-permute-done.14.behind = bf16[320,384]{1,0:T(8,128)(2,1)S(1)} collective-permute-done((bf16[320,384]{1,0:T(8,128)(2,1)S(1)}, bf16[320,384]{1,0:T(8,128)(2,1)S(1)}, u32[]{:S(2)}, u32[]{:S(2)}) %collective-permute-start.14) | collective-permute-done | bytes 245792 | tf_op jit(solution)/shard_map/ppermute | solution.py:184
  195.3 1.9 collective-permute-start.15
  197.3 5.1 %collective-permute-start.17 = (bf16[160,384]{1,0:T(8,128)(2,1)S(1)}, bf16[160,384]{1,0:T(8,128)(2,1)S(1)}, u32[]{:S(2)}, u32[]{:S(2)}) collective-permute-start(bf16[160,384]{1,0:T(8,128)(2,1)S(1)} %slice.43), channel_id=1, source_target_pairs={{0,3},{1,0},{2,1},{3,2},{4,7},{5,4},{6,5},{7,6},{8,11},{9,8},{10,9... | collective-permute-start | bytes 368648 | tf_op jit(solution)/shard_map/ppermute | solution.py:184
  202.4 0.9 collective-permute-done.15.far_lo
  203.3 1.5 collective-permute-done.17.far_hi
  204.9 2.1 collective-permute-start.18
  207.0 2.5 collective-permute-done.18.other_ref
  209.5 2.3 shard_map.72
  211.9 0.8 copy-done.7
  212.7 15.3 %all-to-all-start.3 = ((bf16[64,8,640]{2,1,0:T(8,128)(2,1)}), bf16[64,8,640]{2,1,0:T(8,128)(2,1)S(1)}, u32[]{:S(2)}, u32[]{:S(2)}) async-start(bf16[64,8,640]{2,1,0:T(8,128)(2,1)} %bitcast.32), calls=%async_computation.3 | async-start | bytes 1310720 | tf_op jit(solution)/shard_map/all_to_all | solution.py:188
  228.3 1.9 collective-permute-start.24
  230.2 1.2 collective-permute-done.24
  231.4 2.2 collective-permute-start.25
  233.7 5.7 %collective-permute-done.25 = f32[128,64]{1,0:T(8,128)S(1)} collective-permute-done((f32[128,64]{1,0:T(8,128)S(1)}, f32[128,64]{1,0:T(8,128)S(1)}, u32[]{:S(2)}, u32[]{:S(2)}) %collective-permute-start.25) | collective-permute-done | bytes 32800 | tf_op jit(solution)/shard_map/ppermute | solution.py:184
  239.4 2.9 %collective-permute-start.26 = (f32[128,64]{1,0:T(8,128)S(1)}, f32[128,64]{1,0:T(8,128)S(1)}, u32[]{:S(2)}, u32[]{:S(2)}) collective-permute-start(f32[128,64]{1,0:T(8,128)S(1)} %add.10), channel_id=1, source_target_pairs={{0,2},{1,3},{2,0},{3,1},{4,6},{5,7},{6,4},{7,5},{8,10},{9,11},{10,... | collective-permute-start | bytes 98312 | tf_op jit(solution)/shard_map/ppermute | solution.py:184
  242.4 4.7 %collective-permute-done.26 = f32[128,64]{1,0:T(8,128)S(1)} collective-permute-done((f32[128,64]{1,0:T(8,128)S(1)}, f32[128,64]{1,0:T(8,128)S(1)}, u32[]{:S(2)}, u32[]{:S(2)}) %collective-permute-start.26) | collective-permute-done | bytes 32800 | tf_op jit(solution)/shard_map/ppermute | solution.py:184
  247.1 2.3 shard_map.75
  249.4 16.2 %all-to-all-done.3 = bf16[64,8,640]{2,1,0:T(8,128)(2,1)S(1)} async-done(((bf16[64,8,640]{2,1,0:T(8,128)(2,1)}), bf16[64,8,640]{2,1,0:T(8,128)(2,1)S(1)}, u32[]{:S(2)}, u32[]{:S(2)}) %all-to-all-start.3) | async-done | bytes 655392 | tf_op jit(solution)/shard_map/all_to_all | solution.py:188
  265.6 1.6 shard_map.76
  (49 shorter events, 3.3 us)
Async XLA Ops:
  0.0 228.0 %copy-start = (bf16[512,64]{0,1:T(8,128)(2,1)S(1)}, bf16[512,64]{0,1:T(8,128)(2,1)}, u32[]{:S(2)}) copy-start(bf16[512,64]{0,1:T(8,128)(2,1)} %param.7) | copy-start | bytes 196612
  0.0 0.9 copy-start.9
  0.9 0.7 copy-start.11
  3.2 0.8 copy-start.8
  4.0 87.7 %copy-start.2 = (bf16[1,2048,384]{2,1,0:T(8,128)(2,1)S(1)}, bf16[1,2048,384]{2,1,0:T(8,128)(2,1)}, u32[]{:S(2)}) copy-start(bf16[1,2048,384]{2,1,0:T(8,128)(2,1)} %param.10) | copy-start | bytes 4718596
  60.0 31.7 %copy-start.1 = (bf16[1,2048,384]{2,1,0:T(8,128)(2,1)S(1)}, bf16[1,2048,384]{2,1,0:T(8,128)(2,1)}, u32[]{:S(2)}) copy-start(bf16[1,2048,384]{2,1,0:T(8,128)(2,1)} %param.9) | copy-start | bytes 4718596
  60.0 66.7 %all-to-all-start = ((bf16[64,8,640]{2,1,0:T(8,128)(2,1)}), bf16[64,8,640]{2,1,0:T(8,128)(2,1)}, u32[]{:S(2)}, u32[]{:S(2)}) async-start(bf16[64,8,640]{2,1,0:T(8,128)(2,1)} %bitcast.34), calls=%async_computation | async-start | bytes 1310720 | tf_op jit(solution)/shard_map/all_to_all | solution.py:188
  69.0 14.1 %collective-permute-start = (bf16[256,640]{1,0:T(8,128)(2,1)}, bf16[256,640]{1,0:T(8,128)(2,1)S(1)}, u32[]{:S(2)}, u32[]{:S(2)}) collective-permute-start(bf16[256,640]{1,0:T(8,128)(2,1)} %get-tuple-element.34), channel_id=1, source_target_pairs={{0,1},{1,2},{2,3},{3,0},{4,5},{5,6},{6,7},{7,4},{8,9},{9,10},{10,1... | collective-permute-start | bytes 983048 | tf_op jit(solution)/shard_map/ppermute | solution.py:184
  72.5 12.6 %collective-permute-start.2 = (bf16[256,640]{1,0:T(8,128)(2,1)}, bf16[256,640]{1,0:T(8,128)(2,1)}, u32[]{:S(2)}, u32[]{:S(2)}) collective-permute-start(bf16[256,640]{1,0:T(8,128)(2,1)} %get-tuple-element.33), channel_id=1, source_target_pairs={{0,3},{1,0},{2,1},{3,2},{4,7},{5,4},{6,5},{7,6},{8,11},{9,8},{10,9... | collective-permute-start | bytes 983048 | tf_op jit(solution)/shard_map/ppermute | solution.py:184
  76.0 14.2 %collective-permute-start.4 = (bf16[256,640]{1,0:T(8,128)(2,1)}, bf16[256,640]{1,0:T(8,128)(2,1)}, u32[]{:S(2)}, u32[]{:S(2)}) collective-permute-start(bf16[256,640]{1,0:T(8,128)(2,1)} %get-tuple-element.33), channel_id=1, source_target_pairs={{0,1},{1,2},{2,3},{3,0},{4,5},{5,6},{6,7},{7,4},{8,9},{9,10},{10,1... | collective-permute-start | bytes 983048 | tf_op jit(solution)/shard_map/ppermute | solution.py:184
  78.3 13.4 %collective-permute-start.5 = (bf16[256,640]{1,0:T(8,128)(2,1)}, bf16[256,640]{1,0:T(8,128)(2,1)}, u32[]{:S(2)}, u32[]{:S(2)}) collective-permute-start(bf16[256,640]{1,0:T(8,128)(2,1)} %get-tuple-element.34), channel_id=1, source_target_pairs={{0,3},{1,0},{2,1},{3,2},{4,7},{5,4},{6,5},{7,6},{8,11},{9,8},{10,9... | collective-permute-start | bytes 983048 | tf_op jit(solution)/shard_map/ppermute | solution.py:184
  83.1 13.4 %collective-permute-start.1 = (bf16[256,640]{1,0:T(8,128)(2,1)S(1)}, bf16[256,640]{1,0:T(8,128)(2,1)}, u32[]{:S(2)}, u32[]{:S(2)}) collective-permute-start(bf16[256,640]{1,0:T(8,128)(2,1)S(1)} %collective-permute-done.b_lo), channel_id=1, source_target_pairs={{0,1},{1,2},{2,3},{3,0},{4,5},{5,6},{6,7},{7,4},{8,9},{9,10},{10,1... | collective-permute-start | bytes 983048 | tf_op jit(solution)/shard_map/ppermute | solution.py:184
  85.1 12.0 %collective-permute-start.3 = (bf16[256,640]{1,0:T(8,128)(2,1)}, bf16[256,640]{1,0:T(8,128)(2,1)}, u32[]{:S(2)}, u32[]{:S(2)}) collective-permute-start(bf16[256,640]{1,0:T(8,128)(2,1)} %collective-permute-done.2.a_hi), channel_id=1, source_target_pairs={{0,3},{1,0},{2,1},{3,2},{4,7},{5,4},{6,5},{7,6},{8,11},{9,8},{10,9... | collective-permute-start | bytes 983048 | tf_op jit(solution)/shard_map/ppermute | solution.py:184
  91.7 1.1 copy-start.5
  99.1 3.8 %collective-permute-start.6 = (bf16[320,768]{1,0:T(8,128)(2,1)S(1)}, bf16[320,768]{1,0:T(8,128)(2,1)S(1)}, u32[]{:S(2)}, u32[]{:S(2)}) collective-permute-start(bf16[320,768]{1,0:T(8,128)(2,1)S(1)} %get-tuple-element.21), channel_id=1, source_target_pairs={{0,256},{256,0},{1,257},{257,1},{2,258},{258,2},{3,259},{259,3},{4... | collective-permute-start | bytes 1474568 | tf_op jit(solution)/shard_map/ppermute | solution.py:184
  103.1 11.1 %collective-permute-start.19 = (bf16[320,384]{1,0:T(8,128)(2,1)S(1)}, bf16[320,384]{1,0:T(8,128)(2,1)S(1)}, u32[]{:S(2)}, u32[]{:S(2)}) collective-permute-start(bf16[320,384]{1,0:T(8,128)(2,1)S(1)} %shard_map.67.own), channel_id=1, source_target_pairs={{0,1},{1,2},{2,3},{3,0},{4,5},{5,6},{6,7},{7,4},{8,9},{9,10},{10,1... | collective-permute-start | bytes 737288 | tf_op jit(solution)/shard_map/ppermute | solution.py:184
  106.6 9.9 %collective-permute-start.21 = (bf16[320,384]{1,0:T(8,128)(2,1)S(1)}, bf16[320,384]{1,0:T(8,128)(2,1)S(1)}, u32[]{:S(2)}, u32[]{:S(2)}) collective-permute-start(bf16[320,384]{1,0:T(8,128)(2,1)S(1)} %shard_map.67.own), channel_id=1, source_target_pairs={{0,3},{1,0},{2,1},{3,2},{4,7},{5,4},{6,5},{7,6},{8,11},{9,8},{10,9... | collective-permute-start | bytes 737288 | tf_op jit(solution)/shard_map/ppermute | solution.py:184
  114.2 8.0 %collective-permute-start.20 = (bf16[160,384]{1,0:T(8,128)(2,1)S(1)}, bf16[160,384]{1,0:T(8,128)(2,1)S(1)}, u32[]{:S(2)}, u32[]{:S(2)}) collective-permute-start(bf16[160,384]{1,0:T(8,128)(2,1)S(1)} %slice.44), channel_id=1, source_target_pairs={{0,1},{1,2},{2,3},{3,0},{4,5},{5,6},{6,7},{7,4},{8,9},{9,10},{10,1... | collective-permute-start | bytes 368648 | tf_op jit(solution)/shard_map/ppermute | solution.py:184
  116.5 7.2 %collective-permute-start.22 = (bf16[160,384]{1,0:T(8,128)(2,1)S(1)}, bf16[160,384]{1,0:T(8,128)(2,1)S(1)}, u32[]{:S(2)}, u32[]{:S(2)}) collective-permute-start(bf16[160,384]{1,0:T(8,128)(2,1)S(1)} %slice.45), channel_id=1, source_target_pairs={{0,3},{1,0},{2,1},{3,2},{4,7},{5,4},{6,5},{7,6},{8,11},{9,8},{10,9... | collective-permute-start | bytes 368648 | tf_op jit(solution)/shard_map/ppermute | solution.py:184
  124.8 11.4 %collective-permute-start.23 = (bf16[320,1536]{1,0:T(8,128)(2,1)}, bf16[320,1536]{1,0:T(8,128)(2,1)}, u32[]{:S(2)}, u32[]{:S(2)}) collective-permute-start(bf16[320,1536]{1,0:T(8,128)(2,1)} %shard_map.73.full_ref), channel_id=1, source_target_pairs={{0,256},{256,0},{1,257},{257,1},{2,258},{258,2},{3,259},{259,3},{4... | collective-permute-start | bytes 2949128 | tf_op jit(solution)/shard_map/ppermute | solution.py:184
  128.7 38.1 %collective-permute-start.7 = (bf16[256,640]{1,0:T(8,128)(2,1)}, bf16[256,640]{1,0:T(8,128)(2,1)S(1)}, u32[]{:S(2)}, u32[]{:S(2)}) collective-permute-start(bf16[256,640]{1,0:T(8,128)(2,1)} %get-tuple-element.32), channel_id=1, source_target_pairs={{0,1},{1,2},{2,3},{3,0},{4,5},{5,6},{6,7},{7,4},{8,9},{9,10},{10,1... | collective-permute-start | bytes 983048 | tf_op jit(solution)/shard_map/ppermute | solution.py:184
  131.4 32.7 %collective-permute-start.9 = (bf16[256,640]{1,0:T(8,128)(2,1)}, bf16[256,640]{1,0:T(8,128)(2,1)}, u32[]{:S(2)}, u32[]{:S(2)}) collective-permute-start(bf16[256,640]{1,0:T(8,128)(2,1)} %get-tuple-element.31), channel_id=1, source_target_pairs={{0,3},{1,0},{2,1},{3,2},{4,7},{5,4},{6,5},{7,6},{8,11},{9,8},{10,9... | collective-permute-start | bytes 983048 | tf_op jit(solution)/shard_map/ppermute | solution.py:184
  136.2 1.4 copy-start.3
  140.9 0.8 copy-start.6
  141.7 71.0 %all-to-all-start.2 = ((bf16[64,8,640]{2,1,0:T(8,128)(2,1)}), bf16[64,8,640]{2,1,0:T(8,128)(2,1)}, u32[]{:S(2)}, u32[]{:S(2)}) async-start(bf16[64,8,640]{2,1,0:T(8,128)(2,1)} %bitcast.31), calls=%async_computation.2 | async-start | bytes 1310720 | tf_op jit(solution)/shard_map/all_to_all | solution.py:188
  157.0 12.9 %collective-permute-start.11 = (bf16[256,640]{1,0:T(8,128)(2,1)}, bf16[256,640]{1,0:T(8,128)(2,1)S(1)}, u32[]{:S(2)}, u32[]{:S(2)}) collective-permute-start(bf16[256,640]{1,0:T(8,128)(2,1)} %get-tuple-element.31), channel_id=1, source_target_pairs={{0,1},{1,2},{2,3},{3,0},{4,5},{5,6},{6,7},{7,4},{8,9},{9,10},{10,1... | collective-permute-start | bytes 983048 | tf_op jit(solution)/shard_map/ppermute | solution.py:184
  159.0 13.6 %collective-permute-start.12 = (bf16[256,640]{1,0:T(8,128)(2,1)}, bf16[256,640]{1,0:T(8,128)(2,1)S(1)}, u32[]{:S(2)}, u32[]{:S(2)}) collective-permute-start(bf16[256,640]{1,0:T(8,128)(2,1)} %get-tuple-element.32), channel_id=1, source_target_pairs={{0,3},{1,0},{2,1},{3,2},{4,7},{5,4},{6,5},{7,6},{8,11},{9,8},{10,9... | collective-permute-start | bytes 983048 | tf_op jit(solution)/shard_map/ppermute | solution.py:184
  164.1 13.8 %collective-permute-start.10 = (bf16[256,640]{1,0:T(8,128)(2,1)}, bf16[256,640]{1,0:T(8,128)(2,1)S(1)}, u32[]{:S(2)}, u32[]{:S(2)}) collective-permute-start(bf16[256,640]{1,0:T(8,128)(2,1)} %collective-permute-done.9.a_hi), channel_id=1, source_target_pairs={{0,3},{1,0},{2,1},{3,2},{4,7},{5,4},{6,5},{7,6},{8,11},{9,8},{10,9... | collective-permute-start | bytes 983048 | tf_op jit(solution)/shard_map/ppermute | solution.py:184
  166.8 11.3 %collective-permute-start.8 = (bf16[256,640]{1,0:T(8,128)(2,1)S(1)}, bf16[256,640]{1,0:T(8,128)(2,1)S(1)}, u32[]{:S(2)}, u32[]{:S(2)}) collective-permute-start(bf16[256,640]{1,0:T(8,128)(2,1)S(1)} %collective-permute-done.7.b_lo), channel_id=1, source_target_pairs={{0,1},{1,2},{2,3},{3,0},{4,5},{5,6},{6,7},{7,4},{8,9},{9,10},{10,1... | collective-permute-start | bytes 983048 | tf_op jit(solution)/shard_map/ppermute | solution.py:184
  179.6 3.8 %collective-permute-start.13 = (bf16[320,768]{1,0:T(8,128)(2,1)S(1)}, bf16[320,768]{1,0:T(8,128)(2,1)S(1)}, u32[]{:S(2)}, u32[]{:S(2)}) collective-permute-start(bf16[320,768]{1,0:T(8,128)(2,1)S(1)} %get-tuple-element.24), channel_id=1, source_target_pairs={{0,256},{256,0},{1,257},{257,1},{2,258},{258,2},{3,259},{259,3},{4... | collective-permute-start | bytes 1474568 | tf_op jit(solution)/shard_map/ppermute | solution.py:184
  183.6 25.9 %copy-start.4 = (bf16[1,1536,512]{2,1,0:T(8,128)(2,1)S(1)}, bf16[1,1536,512]{2,1,0:T(8,128)(2,1)}, u32[]{:S(2)}) copy-start(bf16[1,1536,512]{2,1,0:T(8,128)(2,1)} %param.11) | copy-start | bytes 4718596
  183.6 11.7 %collective-permute-start.14 = (bf16[320,384]{1,0:T(8,128)(2,1)S(1)}, bf16[320,384]{1,0:T(8,128)(2,1)S(1)}, u32[]{:S(2)}, u32[]{:S(2)}) collective-permute-start(bf16[320,384]{1,0:T(8,128)(2,1)S(1)} %shard_map.70.own), channel_id=1, source_target_pairs={{0,1},{1,2},{2,3},{3,0},{4,5},{5,6},{6,7},{7,4},{8,9},{9,10},{10,1... | collective-permute-start | bytes 737288 | tf_op jit(solution)/shard_map/ppermute | solution.py:184
  186.0 11.2 %collective-permute-start.16 = (bf16[320,384]{1,0:T(8,128)(2,1)S(1)}, bf16[320,384]{1,0:T(8,128)(2,1)S(1)}, u32[]{:S(2)}, u32[]{:S(2)}) collective-permute-start(bf16[320,384]{1,0:T(8,128)(2,1)S(1)} %shard_map.70.own), channel_id=1, source_target_pairs={{0,3},{1,0},{2,1},{3,2},{4,7},{5,4},{6,5},{7,6},{8,11},{9,8},{10,9... | collective-permute-start | bytes 737288 | tf_op jit(solution)/shard_map/ppermute | solution.py:184
  195.3 8.0 %collective-permute-start.15 = (bf16[160,384]{1,0:T(8,128)(2,1)S(1)}, bf16[160,384]{1,0:T(8,128)(2,1)S(1)}, u32[]{:S(2)}, u32[]{:S(2)}) collective-permute-start(bf16[160,384]{1,0:T(8,128)(2,1)S(1)} %slice.42), channel_id=1, source_target_pairs={{0,1},{1,2},{2,3},{3,0},{4,5},{5,6},{6,7},{7,4},{8,9},{9,10},{10,1... | collective-permute-start | bytes 368648 | tf_op jit(solution)/shard_map/ppermute | solution.py:184
  197.3 7.6 %collective-permute-start.17 = (bf16[160,384]{1,0:T(8,128)(2,1)S(1)}, bf16[160,384]{1,0:T(8,128)(2,1)S(1)}, u32[]{:S(2)}, u32[]{:S(2)}) collective-permute-start(bf16[160,384]{1,0:T(8,128)(2,1)S(1)} %slice.43), channel_id=1, source_target_pairs={{0,3},{1,0},{2,1},{3,2},{4,7},{5,4},{6,5},{7,6},{8,11},{9,8},{10,9... | collective-permute-start | bytes 368648 | tf_op jit(solution)/shard_map/ppermute | solution.py:184
  204.9 23.1 %copy-start.10 = (bf16[128,512]{1,0:T(8,128)(2,1)S(1)}, bf16[128,512]{1,0:T(8,128)(2,1)}, u32[]{:S(2)}) copy-start(bf16[128,512]{1,0:T(8,128)(2,1)} %tokens_ref.1) | copy-start | bytes 393220
  204.9 4.6 %collective-permute-start.18 = (bf16[320,1536]{1,0:T(8,128)(2,1)S(1)}, bf16[320,1536]{1,0:T(8,128)(2,1)S(1)}, u32[]{:S(2)}, u32[]{:S(2)}) collective-permute-start(bf16[320,1536]{1,0:T(8,128)(2,1)S(1)} %shard_map.71.full_ref), channel_id=1, source_target_pairs={{0,256},{256,0},{1,257},{257,1},{2,258},{258,2},{3,259},{259,3},{4... | collective-permute-start | bytes 2949128 | tf_op jit(solution)/shard_map/ppermute | solution.py:184
  211.9 0.8 copy-start.7
  212.7 29.6 %copy-start.12 = (s32[128,8]{0,1:T(8,128)S(1)}, s32[128,8]{0,1:T(8,128)}, u32[]{:S(2)}) copy-start(s32[128,8]{0,1:T(8,128)} %param.8) | copy-start | bytes 12292
  212.7 52.9 %all-to-all-start.3 = ((bf16[64,8,640]{2,1,0:T(8,128)(2,1)}), bf16[64,8,640]{2,1,0:T(8,128)(2,1)S(1)}, u32[]{:S(2)}, u32[]{:S(2)}) async-start(bf16[64,8,640]{2,1,0:T(8,128)(2,1)} %bitcast.32), calls=%async_computation.3 | async-start | bytes 1310720 | tf_op jit(solution)/shard_map/all_to_all | solution.py:188
  228.3 3.1 %collective-permute-start.24 = (f32[128,64]{1,0:T(8,128)S(1)}, f32[128,64]{1,0:T(8,128)S(1)}, u32[]{:S(2)}, u32[]{:S(2)}) collective-permute-start(f32[128,64]{1,0:T(8,128)S(1)} %copy.8), channel_id=1, source_target_pairs={{0,256},{256,0},{1,257},{257,1},{2,258},{258,2},{3,259},{259,3},{4... | collective-permute-start | bytes 98312 | tf_op jit(solution)/shard_map/ppermute | solution.py:184
  231.4 8.0 %collective-permute-start.25 = (f32[128,64]{1,0:T(8,128)S(1)}, f32[128,64]{1,0:T(8,128)S(1)}, u32[]{:S(2)}, u32[]{:S(2)}) collective-permute-start(f32[128,64]{1,0:T(8,128)S(1)} %add.9), channel_id=1, source_target_pairs={{0,1},{1,2},{2,3},{3,0},{4,5},{5,6},{6,7},{7,4},{8,9},{9,10},{10,1... | collective-permute-start | bytes 98312 | tf_op jit(solution)/shard_map/ppermute | solution.py:184
  239.4 7.7 %collective-permute-start.26 = (f32[128,64]{1,0:T(8,128)S(1)}, f32[128,64]{1,0:T(8,128)S(1)}, u32[]{:S(2)}, u32[]{:S(2)}) collective-permute-start(f32[128,64]{1,0:T(8,128)S(1)} %add.10), channel_id=1, source_target_pairs={{0,2},{1,3},{2,0},{3,1},{4,6},{5,7},{6,4},{7,5},{8,10},{9,11},{10,... | collective-permute-start | bytes 98312 | tf_op jit(solution)/shard_map/ppermute | solution.py:184

commit v3 on v2

v3 whole, which is shorter than its diff:
```python
import functools

import jax
import jax.numpy as jnp
from jax import lax
from jax.experimental import pallas as pl
from jax.experimental.pallas import tpu as pltpu
from jax.sharding import PartitionSpec as P

EXPERTS = 64
TOP = 8
SLOTS = 10
BF = jnp.bfloat16
F32 = jnp.float32
VMEM = pl.BlockSpec(memory_space=pltpu.VMEM)
SMEM = pl.BlockSpec(memory_space=pltpu.SMEM)
HBM = pl.BlockSpec(memory_space=pltpu.HBM)


def call(body, outs, args, places=None, scratch=(), flops=0, aliases=None, out_places=None, limit=40):
    places = places or [VMEM] * len(args)
    moved = sum(a.size * a.dtype.itemsize for a in args)
    return pl.pallas_call(
        body,
        out_shape=[jax.ShapeDtypeStruct(*o) for o in outs],
        in_specs=places,
        out_specs=out_places or [VMEM] * len(outs),
        scratch_shapes=scratch,
        input_output_aliases=aliases or {},
        compiler_params=pltpu.CompilerParams(vmem_limit_bytes=limit << 20),
        cost_estimate=pl.CostEstimate(flops=flops, bytes_accessed=moved, transcendentals=0),
    )(*args)


def iota(shape, dim):
    return lax.broadcasted_iota(jnp.int32, shape, dim)


def ones_where(condition):
    return jnp.where(condition, F32(1.0), F32(0.0)).astype(BF)


def dot(a, b):
    return jnp.dot(a, b, preferred_element_type=F32)


def pack(extra):
    n = extra.shape[0]
    shape = (4 * n, n)
    total = jnp.zeros((4 * n, 128), F32)
    for f in range(4):
        total = total + dot(ones_where(iota(shape, 0) == 4 * iota(shape, 1) + f), extra[:, f * 128:(f + 1) * 128])
    return total.astype(BF)


def unpack(pieces):
    n = pieces.shape[0] // 4
    shape = (n, 4 * n)
    parts = [dot(ones_where(iota(shape, 1) == 4 * iota(shape, 0) + f), pieces).astype(BF) for f in range(4)]
    return jnp.concatenate(parts, axis=1)


def rows_of(half):
    return jnp.concatenate([half[:, :512], unpack(half[:, 512:])], axis=0)


def select_body(c, ids_ref, tokens_ref, out_ref, ids_at, tokens_at, sems):
    copies = [
        pltpu.make_async_copy(ids_ref, ids_at, sems.at[0]),
        pltpu.make_async_copy(tokens_ref, tokens_at, sems.at[1]),
    ]
    for copy in copies:
        copy.start()
    rows = tokens_at.shape[0]
    shape, square = (EXPERTS, rows), (rows, rows)
    big, small = (EXPERTS * 8, EXPERTS), (EXPERTS * 2, EXPERTS)
    spread = ones_where((iota(big, 0) >> 3) == iota(big, 1))
    spread2 = ones_where((iota(small, 0) >> 1) == iota(small, 1))
    before = ones_where(iota(square, 0) < iota(square, 1))
    copies[0].wait()
    ids = ids_at[...]
    chosen = jnp.zeros(shape, F32)
    for k in range(TOP):
        chosen = chosen + jnp.where(ids[k:k + 1, :] == iota(shape, 0), F32(1.0), F32(0.0))
    slot = jnp.where(chosen > 0, dot(chosen.astype(BF), before), F32(-1.0)).astype(BF)
    wide = dot(spread, slot)
    wide2 = dot(spread2, slot)
    number = (iota(wide.shape, 0) & 7).astype(F32) + SLOTS * c
    number2 = (iota(wide2.shape, 0) & 1).astype(F32) + (SLOTS * c + 8)
    copies[1].wait()
    tokens = tokens_at[...]
    out_ref[:, :512] = dot(ones_where(wide == number), tokens).astype(BF)
    out_ref[:, 512:] = pack(dot(ones_where(wide2 == number2), tokens).astype(BF))


def gate_up_body(place_ref, blocks_ref, gate_ref, up_ref, kept_ref, sent_ref, blocks_at, weights_at, total, sems):
    def copies(y):
        at = pl.ds(y * 512, 512)
        return (
            pltpu.make_async_copy(blocks_ref.at[at, :], blocks_at.at[at, :], sems.at[y, 0]),
            pltpu.make_async_copy(gate_ref.at[at, :], weights_at.at[at, pl.ds(0, 384)], sems.at[y, 1]),
            pltpu.make_async_copy(up_ref.at[at, :], weights_at.at[at, pl.ds(384, 384)], sems.at[y, 2]),
        )

    for y in range(2):
        for copy in copies(y):
            copy.start()
    first = place_ref[1] == 0
    for y in range(4):
        for copy in copies(y):
            copy.wait()
        if y < 2:
            for copy in copies(y + 2):
                copy.start()
        weights = weights_at[y * 512:(y + 1) * 512, :]
        sums = []
        for h in range(2):
            own = dot(rows_of(blocks_at[y * 512 + h * 256:y * 512 + (h + 1) * 256, :]), weights)
            sums.append(own if y == 0 else total[h * 320:(h + 1) * 320, :] + own)
        if y < 3:
            for h in range(2):
                total[h * 320:(h + 1) * 320, :] = sums[h]
        else:
            kept_ref[...] = jnp.where(first, sums[0], sums[1])
            sent_ref[...] = jnp.where(first, sums[1], sums[0]).astype(BF)


def act_body(kept_ref, got_ref, hidden_ref):
    gate = kept_ref[:, :384] + got_ref[:, :384].astype(F32)
    up = kept_ref[:, 384:] + got_ref[:, 384:].astype(F32)
    hidden_ref[...] = (gate / (1.0 + jnp.exp(-gate)) * up).astype(BF)


def down_half(side, hidden_ref, down_ref, out_ref, slab, sem):
    total = jnp.zeros((320, 512), F32)
    for y in range(4):
        total = total + dot(hidden_ref[y * 320:(y + 1) * 320, :], down_ref[y * 384:(y + 1) * 384, :])
    rows = total.astype(BF)
    slab[:, :512] = rows[:256]
    slab[:, 512:] = pack(rows[256:])
    copy = pltpu.make_async_copy(slab, out_ref.at[pl.ds(pl.multiple_of(side * 256, 256), 256), :], sem)
    copy.start()
    copy.wait()


def down_own_body(place_ref, hidden_ref, down_ref, out_ref, slab, sem):
    down_half(place_ref[1], hidden_ref, down_ref, out_ref, slab, sem)


def down_other_body(place_ref, hidden_ref, down_ref, own_ref, out_ref, slab, sem):
    down_half(1 - place_ref[1], hidden_ref, down_ref, out_ref, slab, sem)


def slots_of(ids):
    rows = ids.shape[0]
    shape = (rows, EXPERTS)
    chosen = jnp.zeros(shape, F32)
    for k in range(TOP):
        chosen = chosen + jnp.where(ids[:, k:k + 1] == iota(shape, 1), F32(1.0), F32(0.0))
    square = (rows, rows)
    rank = dot(ones_where(iota(square, 0) > iota(square, 1)), chosen.astype(BF))
    return chosen, jnp.where(chosen > 0, rank, F32(-1.0))


def weighted(slot, probs, block, c):
    slot = slot.astype(BF)
    high = probs.astype(BF)
    low = (probs - high.astype(F32)).astype(BF)
    total = jnp.zeros((slot.shape[0], 512), F32)
    for per, start, rows in ((8, 0, block[:, :512]), (2, 8, unpack(block[:, 512:]))):
        shape = (EXPERTS, EXPERTS * per)
        spread = ones_where((iota(shape, 1) >> (3 if per == 8 else 1)) == iota(shape, 0))
        wide = dot(slot, spread)
        number = (iota(wide.shape, 1) & (per - 1)).astype(F32) + (SLOTS * c + start)
        for part in (high, low):
            weight = jnp.where(wide == number, dot(part, spread), F32(0.0)).astype(BF)
            total = total + dot(weight, rows)
    return total


def combine_a_body(ids_ref, logits_ref, block_ref, acc_ref, probs_ref, slot_ref):
    chosen, slot = slots_of(ids_ref[...])
    raised = jnp.where(chosen > 0, jnp.exp(logits_ref[...]), F32(0.0))
    probs = raised / jnp.sum(raised, axis=1, keepdims=True)
    probs_ref[...] = probs
    slot_ref[...] = slot
    acc_ref[...] = weighted(slot, probs, block_ref[...], 0)


def combine_b_body(acc_ref, probs_ref, slot_ref, block_ref, out_ref):
    out_ref[...] = (acc_ref[...] + weighted(slot_ref[...], probs_ref[...], block_ref[...], 1)).astype(BF)


def shift(x, axis, size, by):
    return lax.ppermute(x, axis, [(i, (i + by) % size) for i in range(size)])


def exchange(x):
    return lax.all_to_all(x, "ep", split_axis=0, concat_axis=0, tiled=True)


def in_hbm(x):
    return pltpu.with_memory_space_constraint(x, pltpu.HBM)


def gate_up(place, blocks, gate_w, up_w):
    return call(
        gate_up_body,
        [((320, 768), F32), ((320, 768), BF)],
        (place, in_hbm(blocks), in_hbm(gate_w), in_hbm(up_w)),
        [SMEM, HBM, HBM, HBM],
        [
            pltpu.VMEM((2048, 640), BF),
            pltpu.VMEM((2048, 768), BF),
            pltpu.VMEM((640, 768), F32),
            pltpu.SemaphoreType.DMA((4, 3)),
        ],
        1 << 31,
    )


def activate(kept, sent):
    hidden, = call(act_body, [((320, 384), BF)], (kept, shift(sent, "sec", 2, 1)))
    return hidden


def contract(place, hidden, down_w):
    full = lax.all_gather(hidden, "tp", axis=0, tiled=True)
    other = shift(full, "sec", 2, 1)
    out = [((512, 640), BF)]
    scratch = [pltpu.VMEM((256, 640), BF), pltpu.SemaphoreType.DMA]
    own, = call(down_own_body, out, (place, full, down_w), [SMEM, VMEM, VMEM], scratch, 1 << 29, None, [HBM])
    produced, = call(
        down_other_body, out, (place, other, down_w, own), [SMEM, VMEM, VMEM, HBM], scratch, 1 << 29, {3: 0}, [HBM]
    )
    return produced


def per_device(tokens, router_weight, expert_ids, gate_weight, up_weight, down_weight):
    place = jnp.stack([lax.axis_index("tp"), lax.axis_index("sec")]).astype(jnp.int32)
    gate_w, up_w, down_w = gate_weight[0], up_weight[0], down_weight[0]
    names = expert_ids.T
    scratch = [pltpu.VMEM(names.shape, jnp.int32), pltpu.VMEM(tokens.shape, BF), pltpu.SemaphoreType.DMA((2,))]
    outgoing = [
        call(functools.partial(select_body, c), [((512, 640), BF)], (in_hbm(names), in_hbm(tokens)), [HBM, HBM], scratch)[0]
        for c in range(2)
    ]
    block_a = exchange(outgoing[0])
    block_a, slabs_b = lax.optimization_barrier((block_a, outgoing[1]))
    block_b = exchange(slabs_b)

    kept_a, sent_a = gate_up(place, lax.all_gather(block_a, "tp", axis=0, tiled=True), gate_w, up_w)
    block_b, _ = lax.optimization_barrier((block_b, sent_a))
    blocks_b = lax.all_gather(block_b, "tp", axis=0, tiled=True)
    produced_a = contract(place, activate(kept_a, sent_a), down_w)
    blocks_b, _ = lax.optimization_barrier((blocks_b, produced_a))
    back_a = exchange(produced_a)
    produced_b = contract(place, activate(*gate_up(place, blocks_b, gate_w, up_w)), down_w)
    produced_b, back_a = lax.optimization_barrier((produced_b, back_a))
    back_b = exchange(produced_b)

    logits = dot(tokens, router_weight)
    logits, _ = lax.optimization_barrier((logits, produced_b))
    logits = logits + shift(logits, "sec", 2, 1)
    logits = logits + shift(logits, "tp", 4, 1)
    logits = logits + shift(logits, "tp", 4, 2)
    table = ((128, EXPERTS), F32)
    acc, probs, slot = call(combine_a_body, [((128, 512), F32), table, table], (expert_ids, logits, back_a))
    mixture, = call(combine_b_body, [((128, 512), BF)], (acc, probs, slot, back_b))
    return mixture


def solution(mesh):
    placed = (
        P("ep", ("sec", "tp")),
        P(("sec", "tp"), None),
        P("ep", None),
        P("ep", "sec", "tp"),
        P("ep", "sec", "tp"),
        P("ep", None, ("sec", "tp")),
    )
    return jax.shard_map(
        per_device, mesh=mesh, in_specs=placed, out_specs=P("ep", ("sec", "tp")), check_vma=False
    )
```

time: 269 us -> 245 us (0.911)
  starting transfers between devices: 123 us -> 61.9 us
  waiting for transfers between devices: 53.4 us -> 108 us
  blocking collectives: 56 us -> 30.1 us
  between operations: 0.53 us -> 13.7 us
  local copies, waits for them, and re-layouts: 10.8 us -> 1.89 us
  Pallas kernels: 23.6 us -> 28.6 us
    ppermute x27 -> x7, starting transfers between devices: 85 us -> 14 us  [shift(): return lax.ppermute(x, axis, [(i, (i + by) % size) for i in range(size)])]
    all_to_all x1 -> x0, blocking collectives: 56 us -> none  [exchange(): return lax.all_to_all(x, 'ep', split_axis=0, concat_axis=0, tiled=True)]
    all_to_all x3 -> x4, waiting for transfers between devices: 16.2 us -> 62.1 us  [exchange(): return lax.all_to_all(x, 'ep', split_axis=0, concat_axis=0, tiled=True)]
    all_gather x0 -> x2, blocking collectives: none -> 30.1 us  [contract(): full = lax.all_gather(hidden, 'tp', axis=0, tiled=True)]
    all_gather x0 -> x2, waiting for transfers between devices: none -> 29.8 us  [the longest x1 28.5 us: per_device(): lax.all_gather(block_a, 'tp', axis=0, tiled=True)]
    ppermute x27 -> x7, waiting for transfers between devices: 37.2 us -> 15.8 us  [shift(): return lax.ppermute(x, axis, [(i, (i + by) % size) for i in range(size)])]
    all_to_all x3 -> x4, starting transfers between devices: 37.5 us -> 47.8 us  [exchange(): return lax.all_to_all(x, 'ep', split_axis=0, concat_axis=0, tiled=True)]
    pallas_call x13 -> x12, Pallas kernels: 23.6 us -> 28.6 us  [call(): pl.pallas_call(body, out_shape=[jax.ShapeDtypeStruct(*o) for o in outs],...]
  transfers between devices with their start and end apart: 30 -> 13, of which waited for: 18 -> 13; matrix products, arithmetic and copies ran while one was open for 2% -> 0% of each run, Pallas kernels for 8% -> 10%
where the time goes in v3:
time: 245 us; the launch traced here: 244 us
  waiting for transfers between devices  108 us (44%)
  starting transfers between devices  61.9 us (25%)
  blocking collectives  30.1 us (12%)
  Pallas kernels  28.6 us (12%)
  between operations  13.7 us (6%)
    all_to_all x4, waiting for transfers between devices, exchange(): return lax.all_to_all(x, 'ep', split_axis=0, concat_axis=0, tiled=True)  62.1 us
    all_to_all x4, starting transfers between devices, exchange(): return lax.all_to_all(x, 'ep', split_axis=0, concat_axis=0, tiled=True)  47.8 us
    all_gather x2, blocking collectives, contract(): full = lax.all_gather(hidden, 'tp', axis=0, tiled=True)  30.1 us
    pallas_call x12, Pallas kernels, call(): pl.pallas_call(body, out_shape=[jax.ShapeDtypeStruct(*o) for o in outs],...  28.6 us
    all_gather x1, waiting for transfers between devices, per_device(): lax.all_gather(block_a, 'tp', axis=0, tiled=True)  28.5 us
    ppermute x7, waiting for transfers between devices, shift(): return lax.ppermute(x, axis, [(i, (i + by) % size) for i in range(size)])  15.8 us
    ppermute x7, starting transfers between devices, shift(): return lax.ppermute(x, axis, [(i, (i + by) % size) for i in range(size)])  14 us
  transfers between devices with their start and end apart: 13, of which 13 were waited for; matrix products, arithmetic and copies ran while one was open for 0% of the time, Pallas kernels for 10%

profile of v3, /device:TPU:6, one launch (start us, length us, event | category | flops | bytes accessed | tf_op | source)
XLA Modules:
  0.0 244.0 jit_solution(16110926337622057176)
XLA Ops:
  6.5 0.0 copy-start
  6.5 2.7 %shard_map.64 = bf16[512,640]{1,0:T(8,128)(2,1)} custom-call(s32[8,128]{1,0:T(8,128)} %bitcast.24, bf16[128,512]{1,0:T(8,128)(2,1)} %tokens_ref.3), custom_call_target="tpu_custom_call" | custom-call | bytes 135168 | tf_op jit(solution)/shard_map/pallas_call | solution.py:23
  9.3 18.8 %all-to-all-start = ((bf16[64,8,640]{2,1,0:T(8,128)(2,1)}), bf16[64,8,640]{2,1,0:T(8,128)(2,1)S(1)}, u32[]{:S(2)}, u32[]{:S(2)}) async-start(bf16[64,8,640]{2,1,0:T(8,128)(2,1)} %bitcast.3), calls=%async_computation | async-start | bytes 1310720 | tf_op jit(solution)/shard_map/all_to_all | solution.py:199
  28.1 0.0 all-gather.3.cloned.1.call-start
  28.1 2.7 %shard_map.65 = bf16[512,640]{1,0:T(8,128)(2,1)} custom-call(s32[8,128]{1,0:T(8,128)} %bitcast.25, bf16[128,512]{1,0:T(8,128)(2,1)} %tokens_ref.3), custom_call_target="tpu_custom_call" | custom-call | bytes 135168 | tf_op jit(solution)/shard_map/pallas_call | solution.py:23
  30.8 34.5 %all-to-all-done = bf16[64,8,640]{2,1,0:T(8,128)(2,1)S(1)} async-done(((bf16[64,8,640]{2,1,0:T(8,128)(2,1)}), bf16[64,8,640]{2,1,0:T(8,128)(2,1)S(1)}, u32[]{:S(2)}, u32[]{:S(2)}) %all-to-all-start) | async-done | bytes 655392 | tf_op jit(solution)/shard_map/all_to_all | solution.py:199
  65.3 0.0 copy-start.3
  65.3 0.8 copy-done.3
  66.1 0.0 all-gather.3.cloned.1.call-update
  66.2 6.7 %all-to-all-start.1 = ((bf16[64,8,640]{2,1,0:T(8,128)(2,1)}), bf16[64,8,640]{2,1,0:T(8,128)(2,1)S(1)}, u32[]{:S(2)}, u32[]{:S(2)}) async-start(bf16[64,8,640]{2,1,0:T(8,128)(2,1)} %bitcast.5), calls=%async_computation.1 | async-start | bytes 1310720 | tf_op jit(solution)/shard_map/all_to_all | solution.py:199
  72.8 0.0 all-gather.5.cloned.1.call-start
  72.9 0.1 pad_add_fusion.place_ref
  73.0 28.5 %all-gather.3.cloned.1.call-done.blocks_ref = bf16[2048,640]{1,0:T(8,128)(2,1)} async-done(((bf16[512,640]{1,0:T(8,128)(2,1)}), bf16[2048,640]{1,0:T(8,128)(2,1)}) %all-gather.3.cloned.1.call-update) | async-done | bytes 2621456 | tf_op jit(solution)/shard_map/all_gather | solution.py:252
  101.5 5.2 %shard_map.66 = (f32[320,768]{1,0:T(8,128)S(1)}, bf16[320,768]{1,0:T(8,128)(2,1)S(1)}) custom-call(s32[2]{0:T(128)S(1)} %pad_add_fusion.place_ref, bf16[2048,640]{1,0:T(8,128)(2,1)} %all-gather.3.cloned.1.call-done.blocks_ref, bf16[2048,384]{1,0:T(8,128)(2,1)} %bitcast.26, bf16[2048,384]{1,0:T(8,128)(2,1)} %bitcast.28), custom_call_target="tpu_custom_call" | custom-call | flops 2147483648 | bytes 5767176 | tf_op jit(solution)/shard_map/pallas_call | solution.py:23
  106.7 3.1 %all-to-all-done.1 = bf16[64,8,640]{2,1,0:T(8,128)(2,1)S(1)} async-done(((bf16[64,8,640]{2,1,0:T(8,128)(2,1)}), bf16[64,8,640]{2,1,0:T(8,128)(2,1)S(1)}, u32[]{:S(2)}, u32[]{:S(2)}) %all-to-all-start.1) | async-done | bytes 655392 | tf_op jit(solution)/shard_map/all_to_all | solution.py:199
  109.8 0.0 copy-start.2
  109.8 0.8 copy-done.2
  110.7 0.0 all-gather.5.cloned.1.call-update
  110.7 0.0 copy-start.1
  110.7 2.1 collective-permute-start
  112.8 1.8 collective-permute-done.got_ref
  114.6 0.2 shard_map.67
  114.8 15.9 %all_gather.14.hidden_ref = bf16[1280,384]{1,0:T(8,128)(2,1)S(1)} all-gather(bf16[320,384]{1,0:T(8,128)(2,1)S(1)} %shard_map.67), channel_id=1, replica_groups=mesh['sec'=2,'ep'=64,'tp'=4] {'tp'}, dimensions={0}, use_global_device_ids=true | all-gather | bytes 1228800 | tf_op jit(solution)/shard_map/all_gather | solution.py:228
  130.7 1.9 collective-permute-start.1
  132.6 0.0 copy-done.1
  132.6 2.4 shard_map.68.own_ref
  135.0 0.1 collective-permute-done.1.hidden_ref
  135.1 2.4 shard_map.69
  137.5 12.2 %all-to-all-start.2 = ((bf16[64,8,640]{2,1,0:T(8,128)(2,1)}), bf16[64,8,640]{2,1,0:T(8,128)(2,1)S(1)}, u32[]{:S(2)}, u32[]{:S(2)}) async-start(bf16[64,8,640]{2,1,0:T(8,128)(2,1)} %bitcast.10), calls=%async_computation.2 | async-start | bytes 1310720 | tf_op jit(solution)/shard_map/all_to_all | solution.py:199
  149.7 1.3 all-gather.5.cloned.1.call-done.blocks_ref
  151.0 5.2 %shard_map.70 = (f32[320,768]{1,0:T(8,128)S(1)}, bf16[320,768]{1,0:T(8,128)(2,1)S(1)}) custom-call(s32[2]{0:T(128)S(1)} %pad_add_fusion.place_ref, bf16[2048,640]{1,0:T(8,128)(2,1)} %all-gather.5.cloned.1.call-done.blocks_ref, bf16[2048,384]{1,0:T(8,128)(2,1)} %bitcast.27, bf16[2048,384]{1,0:T(8,128)(2,1)} %bitcast.29), custom_call_target="tpu_custom_call" | custom-call | flops 2147483648 | bytes 5767176 | tf_op jit(solution)/shard_map/pallas_call | solution.py:23
  156.2 2.1 collective-permute-start.2
  158.3 1.6 collective-permute-done.2.got_ref
  160.0 0.2 shard_map.71
  160.2 14.2 %all_gather.15.hidden_ref = bf16[1280,384]{1,0:T(8,128)(2,1)S(1)} all-gather(bf16[320,384]{1,0:T(8,128)(2,1)S(1)} %shard_map.71), channel_id=1, replica_groups=mesh['sec'=2,'ep'=64,'tp'=4] {'tp'}, dimensions={0}, use_global_device_ids=true | all-gather | bytes 1228800 | tf_op jit(solution)/shard_map/all_gather | solution.py:228
  174.4 1.9 collective-permute-start.3
  176.3 2.4 shard_map.72.own_ref
  178.7 0.0 copy-start.4
  178.7 0.1 collective-permute-done.3.hidden_ref
  178.8 2.4 shard_map.73
  181.2 0.0 copy-start.5
  181.2 6.3 %all-to-all-done.2 = bf16[64,8,640]{2,1,0:T(8,128)(2,1)S(1)} async-done(((bf16[64,8,640]{2,1,0:T(8,128)(2,1)}), bf16[64,8,640]{2,1,0:T(8,128)(2,1)S(1)}, u32[]{:S(2)}, u32[]{:S(2)}) %all-to-all-start.2) | async-done | bytes 655392 | tf_op jit(solution)/shard_map/all_to_all | solution.py:199
  187.6 10.1 %all-to-all-start.3 = ((bf16[64,8,640]{2,1,0:T(8,128)(2,1)}), bf16[64,8,640]{2,1,0:T(8,128)(2,1)S(1)}, u32[]{:S(2)}, u32[]{:S(2)}) async-start(bf16[64,8,640]{2,1,0:T(8,128)(2,1)} %bitcast.12), calls=%async_computation.3 | async-start | bytes 1310720 | tf_op jit(solution)/shard_map/all_to_all | solution.py:199
  197.7 0.0 copy-done
  197.7 0.0 copy-done.4
  197.7 0.2 fusion
  197.9 0.1 copy.10
  198.0 1.9 collective-permute-start.4
  199.9 1.2 collective-permute-done.4
  201.1 1.9 collective-permute-start.5
  203.1 5.4 %collective-permute-done.5 = f32[128,64]{1,0:T(8,128)S(1)} collective-permute-done((f32[128,64]{1,0:T(8,128)S(1)}, f32[128,64]{1,0:T(8,128)S(1)}, u32[]{:S(2)}, u32[]{:S(2)}) %collective-permute-start.5) | collective-permute-done | bytes 32800 | tf_op jit(solution)/shard_map/ppermute | solution.py:195
  208.5 2.2 collective-permute-start.6
  210.7 0.0 copy-done.5
  210.7 0.1 copy.11.ids_ref
  210.8 5.4 %collective-permute-done.6 = f32[128,64]{1,0:T(8,128)S(1)} collective-permute-done((f32[128,64]{1,0:T(8,128)S(1)}, f32[128,64]{1,0:T(8,128)S(1)}, u32[]{:S(2)}, u32[]{:S(2)}) %collective-permute-start.6) | collective-permute-done | bytes 32800 | tf_op jit(solution)/shard_map/ppermute | solution.py:195
  216.2 1.2 shard_map.74
  217.4 18.1 %all-to-all-done.3 = bf16[64,8,640]{2,1,0:T(8,128)(2,1)S(1)} async-done(((bf16[64,8,640]{2,1,0:T(8,128)(2,1)}), bf16[64,8,640]{2,1,0:T(8,128)(2,1)S(1)}, u32[]{:S(2)}, u32[]{:S(2)}) %all-to-all-start.3) | async-done | bytes 655392 | tf_op jit(solution)/shard_map/all_to_all | solution.py:199
  235.6 1.6 shard_map.75
  (3 shorter events, 0.0 us)
Async XLA Ops:
  6.5 191.2 %copy-start = (bf16[512,64]{0,1:T(8,128)(2,1)S(1)}, bf16[512,64]{0,1:T(8,128)(2,1)}, u32[]{:S(2)}) copy-start(bf16[512,64]{0,1:T(8,128)(2,1)} %param.7) | copy-start | bytes 196612
  9.3 56.0 %all-to-all-start = ((bf16[64,8,640]{2,1,0:T(8,128)(2,1)}), bf16[64,8,640]{2,1,0:T(8,128)(2,1)S(1)}, u32[]{:S(2)}, u32[]{:S(2)}) async-start(bf16[64,8,640]{2,1,0:T(8,128)(2,1)} %bitcast.3), calls=%async_computation | async-start | bytes 1310720 | tf_op jit(solution)/shard_map/all_to_all | solution.py:199
  28.1 73.4 %all-gather.3.cloned.1.call-start = ((), (), s32[]{:S(2)}) async-start(), calls=%async_computation.4 | async-start | bytes 3276800 | tf_op jit(solution)/shard_map/all_gather | solution.py:252
  65.3 0.8 copy-start.3
  66.2 43.7 %all-to-all-start.1 = ((bf16[64,8,640]{2,1,0:T(8,128)(2,1)}), bf16[64,8,640]{2,1,0:T(8,128)(2,1)S(1)}, u32[]{:S(2)}, u32[]{:S(2)}) async-start(bf16[64,8,640]{2,1,0:T(8,128)(2,1)} %bitcast.5), calls=%async_computation.1 | async-start | bytes 1310720 | tf_op jit(solution)/shard_map/all_to_all | solution.py:199
  72.8 78.2 %all-gather.5.cloned.1.call-start = ((), (), s32[]{:S(2)}) async-start(), calls=%async_computation.5 | async-start | bytes 3276800 | tf_op jit(solution)/shard_map/all_gather | solution.py:254
  109.8 0.8 copy-start.2
  110.7 21.9 %copy-start.1 = (bf16[1,1536,512]{2,1,0:T(8,128)(2,1)S(1)}, bf16[1,1536,512]{2,1,0:T(8,128)(2,1)}, u32[]{:S(2)}) copy-start(bf16[1,1536,512]{2,1,0:T(8,128)(2,1)} %param.11) | copy-start | bytes 4718596
  110.7 3.9 %collective-permute-start = (bf16[320,768]{1,0:T(8,128)(2,1)S(1)}, bf16[320,768]{1,0:T(8,128)(2,1)S(1)}, u32[]{:S(2)}, u32[]{:S(2)}) collective-permute-start(bf16[320,768]{1,0:T(8,128)(2,1)S(1)} %get-tuple-element.21), channel_id=1, source_target_pairs={{0,256},{256,0},{1,257},{257,1},{2,258},{258,2},{3,259},{259,3},{4... | collective-permute-start | bytes 1474568 | tf_op jit(solution)/shard_map/ppermute | solution.py:195
  130.7 4.4 %collective-permute-start.1 = (bf16[1280,384]{1,0:T(8,128)(2,1)S(1)}, bf16[1280,384]{1,0:T(8,128)(2,1)S(1)}, u32[]{:S(2)}, u32[]{:S(2)}) collective-permute-start(bf16[1280,384]{1,0:T(8,128)(2,1)S(1)} %all_gather.14.hidden_ref), channel_id=1, source_target_pairs={{0,256},{256,0},{1,257},{257,1},{2,258},{258,2},{3,259},{259,3},{4... | collective-permute-start | bytes 2949128 | tf_op jit(solution)/shard_map/ppermute | solution.py:195
  137.5 50.1 %all-to-all-start.2 = ((bf16[64,8,640]{2,1,0:T(8,128)(2,1)}), bf16[64,8,640]{2,1,0:T(8,128)(2,1)S(1)}, u32[]{:S(2)}, u32[]{:S(2)}) async-start(bf16[64,8,640]{2,1,0:T(8,128)(2,1)} %bitcast.10), calls=%async_computation.2 | async-start | bytes 1310720 | tf_op jit(solution)/shard_map/all_to_all | solution.py:199
  156.2 3.8 %collective-permute-start.2 = (bf16[320,768]{1,0:T(8,128)(2,1)S(1)}, bf16[320,768]{1,0:T(8,128)(2,1)S(1)}, u32[]{:S(2)}, u32[]{:S(2)}) collective-permute-start(bf16[320,768]{1,0:T(8,128)(2,1)S(1)} %get-tuple-element.26), channel_id=1, source_target_pairs={{0,256},{256,0},{1,257},{257,1},{2,258},{258,2},{3,259},{259,3},{4... | collective-permute-start | bytes 1474568 | tf_op jit(solution)/shard_map/ppermute | solution.py:195
  174.4 4.4 %collective-permute-start.3 = (bf16[1280,384]{1,0:T(8,128)(2,1)S(1)}, bf16[1280,384]{1,0:T(8,128)(2,1)S(1)}, u32[]{:S(2)}, u32[]{:S(2)}) collective-permute-start(bf16[1280,384]{1,0:T(8,128)(2,1)S(1)} %all_gather.15.hidden_ref), channel_id=1, source_target_pairs={{0,256},{256,0},{1,257},{257,1},{2,258},{258,2},{3,259},{259,3},{4... | collective-permute-start | bytes 2949128 | tf_op jit(solution)/shard_map/ppermute | solution.py:195
  178.7 19.0 %copy-start.4 = (bf16[128,512]{1,0:T(8,128)(2,1)S(1)}, bf16[128,512]{1,0:T(8,128)(2,1)}, u32[]{:S(2)}) copy-start(bf16[128,512]{1,0:T(8,128)(2,1)} %tokens_ref.3) | copy-start | bytes 393220
  181.2 29.5 %copy-start.5 = (s32[128,8]{0,1:T(8,128)S(1)}, s32[128,8]{0,1:T(8,128)}, u32[]{:S(2)}) copy-start(s32[128,8]{0,1:T(8,128)} %param.8) | copy-start | bytes 12292
  187.6 48.0 %all-to-all-start.3 = ((bf16[64,8,640]{2,1,0:T(8,128)(2,1)}), bf16[64,8,640]{2,1,0:T(8,128)(2,1)S(1)}, u32[]{:S(2)}, u32[]{:S(2)}) async-start(bf16[64,8,640]{2,1,0:T(8,128)(2,1)} %bitcast.12), calls=%async_computation.3 | async-start | bytes 1310720 | tf_op jit(solution)/shard_map/all_to_all | solution.py:199
  198.0 3.1 %collective-permute-start.4 = (f32[128,64]{1,0:T(8,128)S(1)}, f32[128,64]{1,0:T(8,128)S(1)}, u32[]{:S(2)}, u32[]{:S(2)}) collective-permute-start(f32[128,64]{1,0:T(8,128)S(1)} %copy.10), channel_id=1, source_target_pairs={{0,256},{256,0},{1,257},{257,1},{2,258},{258,2},{3,259},{259,3},{4... | collective-permute-start | bytes 98312 | tf_op jit(solution)/shard_map/ppermute | solution.py:195
  201.1 7.4 %collective-permute-start.5 = (f32[128,64]{1,0:T(8,128)S(1)}, f32[128,64]{1,0:T(8,128)S(1)}, u32[]{:S(2)}, u32[]{:S(2)}) collective-permute-start(f32[128,64]{1,0:T(8,128)S(1)} %add.9), channel_id=1, source_target_pairs={{0,1},{1,2},{2,3},{3,0},{4,5},{5,6},{6,7},{7,4},{8,9},{9,10},{10,1... | collective-permute-start | bytes 98312 | tf_op jit(solution)/shard_map/ppermute | solution.py:195
  208.5 7.7 %collective-permute-start.6 = (f32[128,64]{1,0:T(8,128)S(1)}, f32[128,64]{1,0:T(8,128)S(1)}, u32[]{:S(2)}, u32[]{:S(2)}) collective-permute-start(f32[128,64]{1,0:T(8,128)S(1)} %add.10), channel_id=1, source_target_pairs={{0,2},{1,3},{2,0},{3,1},{4,6},{5,7},{6,4},{7,5},{8,10},{9,11},{10,... | collective-permute-start | bytes 98312 | tf_op jit(solution)/shard_map/ppermute | solution.py:195
Sparse Core Ops, SparseCore 0:
  66.3 35.1 all-gather.2
  110.8 40.1 all-gather.4

commit v4 on v3

--- a/solution.py
+++ b/solution.py
@@ -53,6 +53,10 @@
     return total.astype(BF)
 
 
+def z_first(i):
+    return ((i & 3) << 4) + (i >> 2)
+
+
 def unpack(pieces):
     n = pieces.shape[0] // 4
     shape = (n, 4 * n)
@@ -64,7 +68,8 @@
     return jnp.concatenate([half[:, :512], unpack(half[:, 512:])], axis=0)
 
 
-def select_body(c, ids_ref, tokens_ref, out_ref, ids_at, tokens_at, sems):
+def select_body(c, *refs):
+    ids_ref, tokens_ref, out_ref, ids_at, tokens_at, sems = refs[c:]
     copies = [
         pltpu.make_async_copy(ids_ref, ids_at, sems.at[0]),
         pltpu.make_async_copy(tokens_ref, tokens_at, sems.at[1]),
@@ -73,9 +78,14 @@
         copy.start()
     rows = tokens_at.shape[0]
     shape, square = (EXPERTS, rows), (rows, rows)
-    big, small = (EXPERTS * 8, EXPERTS), (EXPERTS * 2, EXPERTS)
-    spread = ones_where((iota(big, 0) >> 3) == iota(big, 1))
-    spread2 = ones_where((iota(small, 0) >> 1) == iota(small, 1))
+    big = (EXPERTS * 8, EXPERTS)
+
+    def expert(i):
+        if c == 0:
+            return z_first(i)
+        return ((((i >> 4) + refs[0][2]) & 3) << 4) + (i & 15)
+
+    spread = ones_where(expert(iota(big, 0) >> 3) == iota(big, 1))
     before = ones_where(iota(square, 0) < iota(square, 1))
     copies[0].wait()
     ids = ids_at[...]
@@ -84,13 +94,17 @@
         chosen = chosen + jnp.where(ids[k:k + 1, :] == iota(shape, 0), F32(1.0), F32(0.0))
     slot = jnp.where(chosen > 0, dot(chosen.astype(BF), before), F32(-1.0)).astype(BF)
     wide = dot(spread, slot)
-    wide2 = dot(spread2, slot)
-    number = (iota(wide.shape, 0) & 7).astype(F32) + SLOTS * c
-    number2 = (iota(wide2.shape, 0) & 1).astype(F32) + (SLOTS * c + 8)
+    row = iota(wide.shape, 0) & 7
+    main = ones_where(wide == (row + SLOTS * c).astype(F32))
+    extra = wide == ((row >> 2) + (SLOTS * c + 8)).astype(F32)
+    pieces = [ones_where(extra & ((row & 3) == f)) for f in range(4)]
     copies[1].wait()
     tokens = tokens_at[...]
-    out_ref[:, :512] = dot(ones_where(wide == number), tokens).astype(BF)
-    out_ref[:, 512:] = pack(dot(ones_where(wide2 == number2), tokens).astype(BF))
+    out_ref[:, :512] = dot(main, tokens).astype(BF)
+    total = jnp.zeros((EXPERTS * 8, 128), F32)
+    for f in range(4):
+        total = total + dot(pieces[f], tokens[:, f * 128:(f + 1) * 128])
+    out_ref[:, 512:] = total.astype(BF)
 
 
 def gate_up_body(place_ref, blocks_ref, gate_ref, up_ref, kept_ref, sent_ref, blocks_at, weights_at, total, sems):
@@ -162,41 +176,74 @@
     return chosen, jnp.where(chosen > 0, rank, F32(-1.0))
 
 
-def weighted(slot, probs, block, c):
-    slot = slot.astype(BF)
+def weighted(slot, probs, block, c, expert):
     high = probs.astype(BF)
     low = (probs - high.astype(F32)).astype(BF)
+    shape = (EXPERTS, EXPERTS * 8)
+    spread = ones_where(expert(iota(shape, 1) >> 3) == iota(shape, 0))
+    wide = dot(slot.astype(BF), spread)
+    row = iota(wide.shape, 1) & 7
+    main = wide == (row + SLOTS * c).astype(F32)
+    extra = wide == ((row >> 2) + (SLOTS * c + 8)).astype(F32)
     total = jnp.zeros((slot.shape[0], 512), F32)
-    for per, start, rows in ((8, 0, block[:, :512]), (2, 8, unpack(block[:, 512:]))):
-        shape = (EXPERTS, EXPERTS * per)
-        spread = ones_where((iota(shape, 1) >> (3 if per == 8 else 1)) == iota(shape, 0))
-        wide = dot(slot, spread)
-        number = (iota(wide.shape, 1) & (per - 1)).astype(F32) + (SLOTS * c + start)
-        for part in (high, low):
-            weight = jnp.where(wide == number, dot(part, spread), F32(0.0)).astype(BF)
-            total = total + dot(weight, rows)
+    for part in (high, low):
+        weight = dot(part, spread)
+        total = total + dot(jnp.where(main, weight, F32(0.0)).astype(BF), block[:, :512])
+        pieces = [
+            dot(jnp.where(extra & ((row & 3) == f), weight, F32(0.0)).astype(BF), block[:, 512:]) for f in range(4)
+        ]
+        total = total + jnp.concatenate(pieces, axis=1)
     return total
 
 
-def combine_a_body(ids_ref, logits_ref, block_ref, acc_ref, probs_ref, slot_ref):
+def combine_a_body(place_ref, ids_ref, logits_ref, block_ref, acc_ref, probs_ref, slot_ref):
     chosen, slot = slots_of(ids_ref[...])
     raised = jnp.where(chosen > 0, jnp.exp(logits_ref[...]), F32(0.0))
     probs = raised / jnp.sum(raised, axis=1, keepdims=True)
     probs_ref[...] = probs
     slot_ref[...] = slot
-    acc_ref[...] = weighted(slot, probs, block_ref[...], 0)
+
+    def expert(i):
+        return (((place_ref[2] + 4 - (i >> 4)) & 3) << 4) + (i & 15)
+
+    acc_ref[...] = weighted(slot, probs, block_ref[...], 0, expert)
 
 
 def combine_b_body(acc_ref, probs_ref, slot_ref, block_ref, out_ref):
-    out_ref[...] = (acc_ref[...] + weighted(slot_ref[...], probs_ref[...], block_ref[...], 1)).astype(BF)
+    out_ref[...] = (acc_ref[...] + weighted(slot_ref[...], probs_ref[...], block_ref[...], 1, z_first)).astype(BF)
 
 
 def shift(x, axis, size, by):
     return lax.ppermute(x, axis, [(i, (i + by) % size) for i in range(size)])
 
 
-def exchange(x):
-    return lax.all_to_all(x, "ep", split_axis=0, concat_axis=0, tiled=True)
+def exchange(x, groups):
+    return lax.all_to_all(x, "ep", split_axis=0, concat_axis=0, tiled=True, axis_index_groups=groups)
+
+
+WHOLE = [[z_first(i) for i in range(64)]]
+ALONG_Z = [[x * 16 + z for z in range(16)] for x in range(4)]
+
+
+def shift_x(part, by):
+    return lax.ppermute(part, "ep", [(i, (i + 16 * by) % 64) for i in range(64)])
+
+
+def out_along_x(slabs, x):
+    own, one, two, three = (slabs[d * 128:(d + 1) * 128] for d in range(4))
+    parts = [own, shift_x(three, 3), shift_x(two, 2), shift_x(one, 1)]
+    parts = jnp.stack([p.reshape(16, 8, 640) for p in parts + parts[:3]])
+    parts = lax.dynamic_slice_in_dim(parts, (4 - x) & 3, 4, 0)
+    return parts.transpose(1, 0, 2, 3).reshape(512, 640)
+
+
+def back_along_x(slabs, x):
+    slabs = slabs.reshape(16, 4, 8, 640)
+    parts = []
+    for d in range(4):
+        part = lax.dynamic_slice_in_dim(slabs, (x + d) & 3, 1, 1).reshape(128, 640)
+        parts.append(shift_x(part, d) if d else part)
+    return jnp.concatenate(parts, axis=0)
 
 
 def in_hbm(x):
@@ -224,8 +271,11 @@
     return hidden
 
 
-def contract(place, hidden, down_w):
-    full = lax.all_gather(hidden, "tp", axis=0, tiled=True)
+def gather(hidden):
+    return lax.all_gather(hidden, "tp", axis=0, tiled=True)
+
+
+def contract(place, full, down_w):
     other = shift(full, "sec", 2, 1)
     out = [((512, 640), BF)]
     scratch = [pltpu.VMEM((256, 640), BF), pltpu.SemaphoreType.DMA]
@@ -237,27 +287,31 @@
 
 
 def per_device(tokens, router_weight, expert_ids, gate_weight, up_weight, down_weight):
-    place = jnp.stack([lax.axis_index("tp"), lax.axis_index("sec")]).astype(jnp.int32)
+    x = (lax.axis_index("ep") >> 4).astype(jnp.int32)
+    place = jnp.stack([lax.axis_index("tp"), lax.axis_index("sec"), x]).astype(jnp.int32)
     gate_w, up_w, down_w = gate_weight[0], up_weight[0], down_weight[0]
     names = expert_ids.T
     scratch = [pltpu.VMEM(names.shape, jnp.int32), pltpu.VMEM(tokens.shape, BF), pltpu.SemaphoreType.DMA((2,))]
-    outgoing = [
-        call(functools.partial(select_body, c), [((512, 640), BF)], (in_hbm(names), in_hbm(tokens)), [HBM, HBM], scratch)[0]
-        for c in range(2)
-    ]
-    block_a = exchange(outgoing[0])
-    block_a, slabs_b = lax.optimization_barrier((block_a, outgoing[1]))
-    block_b = exchange(slabs_b)
-
-    kept_a, sent_a = gate_up(place, lax.all_gather(block_a, "tp", axis=0, tiled=True), gate_w, up_w)
-    block_b, _ = lax.optimization_barrier((block_b, sent_a))
+    sources = (in_hbm(names), in_hbm(tokens))
+    out = [((512, 640), BF)]
+    slabs_a, = call(functools.partial(select_body, 0), out, sources, [HBM, HBM], scratch)
+    slabs_b, = call(functools.partial(select_body, 1), out, (place, *sources), [SMEM, HBM, HBM], scratch)
+    block_a = exchange(slabs_a, WHOLE)
+    slabs_b = out_along_x(slabs_b, x)
+    block_a, slabs_b = lax.optimization_barrier((block_a, slabs_b))
+    block_b = exchange(slabs_b, ALONG_Z)
+
+    blocks_a = lax.all_gather(block_a, "tp", axis=0, tiled=True)
+    blocks_a, block_b = lax.optimization_barrier((blocks_a, block_b))
+    kept_a, sent_a = gate_up(place, blocks_a, gate_w, up_w)
     blocks_b = lax.all_gather(block_b, "tp", axis=0, tiled=True)
-    produced_a = contract(place, activate(kept_a, sent_a), down_w)
+    produced_a = contract(place, gather(activate(kept_a, sent_a)), down_w)
     blocks_b, _ = lax.optimization_barrier((blocks_b, produced_a))
-    back_a = exchange(produced_a)
-    produced_b = contract(place, activate(*gate_up(place, blocks_b, gate_w, up_w)), down_w)
+    back_a = exchange(produced_a, ALONG_Z)
+    produced_b = contract(place, gather(activate(*gate_up(place, blocks_b, gate_w, up_w))), down_w)
     produced_b, back_a = lax.optimization_barrier((produced_b, back_a))
-    back_b = exchange(produced_b)
+    back_b = exchange(produced_b, WHOLE)
+    back_a = back_along_x(back_a, x)
 
     logits = dot(tokens, router_weight)
     logits, _ = lax.optimization_barrier((logits, produced_b))
@@ -265,7 +319,7 @@
     logits = logits + shift(logits, "tp", 4, 1)
     logits = logits + shift(logits, "tp", 4, 2)
     table = ((128, EXPERTS), F32)
-    acc, probs, slot = call(combine_a_body, [((128, 512), F32), table, table], (expert_ids, logits, back_a))
+    acc, probs, slot = call(combine_a_body, [((128, 512), F32), table, table], (place, expert_ids, logits, back_a), [SMEM] + [VMEM] * 3)
     mixture, = call(combine_b_body, [((128, 512), BF)], (acc, probs, slot, back_b))
     return mixture
 

time: 245 us -> 243 us (level)
  waiting for transfers between devices: 108 us -> 56.6 us
  blocking collectives: 30.1 us -> 73.9 us
  starting transfers between devices: 61.9 us -> 67.4 us
    all_to_all x0 -> x1, blocking collectives: none -> 39.3 us  [exchange(): lax.all_to_all(x, 'ep', split_axis=0, concat_axis=0, tiled=True, axis_ind...]
    all_to_all x4 -> x3, waiting for transfers between devices: 62.1 us -> 28.9 us  [exchange(): lax.all_to_all(x, 'ep', split_axis=0, concat_axis=0, tiled=True, axis_ind...]
    all_gather x1, waiting for transfers between devices: 28.5 us -> 0.01 us  [per_device(): blocks_a = lax.all_gather(block_a, 'tp', axis=0, tiled=True)]
    ppermute x0 -> x6, starting transfers between devices: none -> 18.5 us  [shift_x(): lax.ppermute(part, 'ep', [(i, (i + 16 * by) % 64) for i in range(64)])]
    all_to_all x4 -> x3, starting transfers between devices: 47.8 us -> 35 us  [exchange(): lax.all_to_all(x, 'ep', split_axis=0, concat_axis=0, tiled=True, axis_ind...]
    ppermute x0 -> x6, waiting for transfers between devices: none -> 6.84 us  [shift_x(): lax.ppermute(part, 'ep', [(i, (i + 16 * by) % 64) for i in range(64)])]
    all_gather x2, blocking collectives: 30.1 us -> 34.7 us  [gather(): return lax.all_gather(hidden, 'tp', axis=0, tiled=True)]
    all_gather x1, waiting for transfers between devices: 1.32 us -> 5.06 us  [per_device(): blocks_b = lax.all_gather(block_b, 'tp', axis=0, tiled=True)]
  transfers between devices with their start and end apart: 13 -> 18, of which waited for: 13 -> 11; matrix products, arithmetic and copies ran while one was open for 0% -> 0% of each run, Pallas kernels for 10% -> 10%
where the time goes in v4:
time: 243 us; the launch traced here: 242 us
  blocking collectives  73.9 us (30%)
  starting transfers between devices  67.4 us (28%)
  waiting for transfers between devices  56.6 us (23%)
  Pallas kernels  28.4 us (12%)
  between operations  13.8 us (6%)
    all_to_all x1, blocking collectives, exchange(): lax.all_to_all(x, 'ep', split_axis=0, concat_axis=0, tiled=True, axis_ind...  39.3 us
    all_to_all x3, starting transfers between devices, exchange(): lax.all_to_all(x, 'ep', split_axis=0, concat_axis=0, tiled=True, axis_ind...  35 us
    all_gather x2, blocking collectives, gather(): return lax.all_gather(hidden, 'tp', axis=0, tiled=True)  34.7 us
    all_to_all x3, waiting for transfers between devices, exchange(): lax.all_to_all(x, 'ep', split_axis=0, concat_axis=0, tiled=True, axis_ind...  28.9 us
    pallas_call x12, Pallas kernels, call(): pl.pallas_call(body, out_shape=[jax.ShapeDtypeStruct(*o) for o in outs],...  28.4 us
    ppermute x6, starting transfers between devices, shift_x(): lax.ppermute(part, 'ep', [(i, (i + 16 * by) % 64) for i in range(64)])  18.5 us
    ppermute x7, waiting for transfers between devices, shift(): return lax.ppermute(x, axis, [(i, (i + by) % size) for i in range(size)])  15.8 us
    ppermute x7, starting transfers between devices, shift(): return lax.ppermute(x, axis, [(i, (i + by) % size) for i in range(size)])  13.9 us
  transfers between devices with their start and end apart: 18, of which 11 were waited for; matrix products, arithmetic and copies ran while one was open for 0% of the time, Pallas kernels for 10%

profile of v4, /device:TPU:6, one launch (start us, length us, event | category | flops | bytes accessed | tf_op | source)
XLA Modules:
  0.0 241.8 jit_solution(1793808009471609063)
XLA Ops:
  6.5 0.0 copy-start
  6.5 2.4 shard_map.64
  8.9 18.6 %all-to-all-start = ((bf16[64,8,640]{2,1,0:T(8,128)(2,1)}), bf16[64,8,640]{2,1,0:T(8,128)(2,1)S(1)}, u32[]{:S(2)}, u32[]{:S(2)}) async-start(bf16[64,8,640]{2,1,0:T(8,128)(2,1)} %bitcast.4), calls=%async_computation | async-start | bytes 1310720 | tf_op jit(solution)/shard_map/all_to_all | solution.py:221
  27.5 0.0 all-gather.3.cloned.1.call-start
  27.6 0.1 pad_add_fusion.refs_0_.place_ref
  27.7 2.1 shard_map.65
  29.8 2.8 %collective-permute-start = (bf16[128,640]{1,0:T(8,128)(2,1)S(1)}, bf16[128,640]{1,0:T(8,128)(2,1)S(1)}, u32[]{:S(2)}, u32[]{:S(2)}) collective-permute-start(bf16[128,640]{1,0:T(8,128)(2,1)S(1)} %get-tuple-element.41), channel_id=1, source_target_pairs={{0,192},{4,196},{8,200},{12,204},{16,208},{20,212},{24,216},{28,22... | collective-permute-start | bytes 491528 | tf_op jit(solution)/shard_map/ppermute | solution.py:229
  32.6 3.0 %collective-permute-start.1 = (bf16[128,640]{1,0:T(8,128)(2,1)S(1)}, bf16[128,640]{1,0:T(8,128)(2,1)S(1)}, u32[]{:S(2)}, u32[]{:S(2)}) collective-permute-start(bf16[128,640]{1,0:T(8,128)(2,1)S(1)} %get-tuple-element.40), channel_id=1, source_target_pairs={{0,128},{4,132},{8,136},{12,140},{16,144},{20,148},{24,152},{28,15... | collective-permute-start | bytes 491528 | tf_op jit(solution)/shard_map/ppermute | solution.py:229
  35.5 4.1 %collective-permute-start.2 = (bf16[128,640]{1,0:T(8,128)(2,1)S(1)}, bf16[128,640]{1,0:T(8,128)(2,1)S(1)}, u32[]{:S(2)}, u32[]{:S(2)}) collective-permute-start(bf16[128,640]{1,0:T(8,128)(2,1)S(1)} %get-tuple-element.39), channel_id=1, source_target_pairs={{0,64},{4,68},{8,72},{12,76},{16,80},{20,84},{24,88},{28,92},{32,9... | collective-permute-start | bytes 491528 | tf_op jit(solution)/shard_map/ppermute | solution.py:229
  39.7 4.3 %collective-permute-done = bf16[128,640]{1,0:T(8,128)(2,1)S(1)} collective-permute-done((bf16[128,640]{1,0:T(8,128)(2,1)S(1)}, bf16[128,640]{1,0:T(8,128)(2,1)S(1)}, u32[]{:S(2)}, u32[]{:S(2)}) %collective-permute-start) | collective-permute-done | bytes 163872 | tf_op jit(solution)/shard_map/ppermute | solution.py:229
  44.0 0.0 collective-permute-done.1
  44.0 2.5 %collective-permute-done.2 = bf16[128,640]{1,0:T(8,128)(2,1)S(1)} collective-permute-done((bf16[128,640]{1,0:T(8,128)(2,1)S(1)}, bf16[128,640]{1,0:T(8,128)(2,1)S(1)}, u32[]{:S(2)}, u32[]{:S(2)}) %collective-permute-start.2) | collective-permute-done | bytes 163872 | tf_op jit(solution)/shard_map/ppermute | solution.py:229
  46.7 0.1 constant_dynamic-slice_fusion
  46.8 19.1 %all-to-all-done = bf16[64,8,640]{2,1,0:T(8,128)(2,1)S(1)} async-done(((bf16[64,8,640]{2,1,0:T(8,128)(2,1)}), bf16[64,8,640]{2,1,0:T(8,128)(2,1)S(1)}, u32[]{:S(2)}, u32[]{:S(2)}) %all-to-all-start) | async-done | bytes 655392 | tf_op jit(solution)/shard_map/all_to_all | solution.py:221
  65.9 0.8 copy-done.2
  66.7 0.0 all-gather.3.cloned.1.call-update
  66.8 0.0 all-gather.5.cloned.1.call-start
  66.8 39.3 %all_to_all.47 = bf16[16,32,640]{2,1,0:T(8,128)(2,1)} all-to-all(bf16[16,32,640]{2,1,0:T(8,128)(2,1)S(1)} %bitcast.62), channel_id=1, replica_groups={{0,4,8,12,16,20,24,28,32,36,40,44,48,52,56,60},{64,68,72,76,80,84,88,92..., dimensions={0} | all-to-all | bytes 1310720 | tf_op jit(solution)/shard_map/all_to_all | solution.py:221
  106.1 0.0 all-gather.5.cloned.1.call-update
  106.1 5.2 %shard_map.66 = (f32[320,768]{1,0:T(8,128)S(1)}, bf16[320,768]{1,0:T(8,128)(2,1)S(1)}) custom-call(s32[3]{0:T(128)S(1)} %pad_add_fusion.refs_0_.place_ref, bf16[2048,640]{1,0:T(8,128)(2,1)} %all-gather.3.cloned.1.call-done.blocks_ref, bf16[2048,384]{1,0:T(8,128)(2,1)} %bitcast.65, bf16[2048,384]{1,0:T(8,128)(2,1)} %bitcast.67), custom_call_target="tpu_custom_call" | custom-call | flops 2147483648 | bytes 5767180 | tf_op jit(solution)/shard_map/pallas_call | solution.py:23
  111.3 1.9 collective-permute-start.3
  113.2 1.8 collective-permute-done.3.got_ref
  115.1 0.2 shard_map.67
  115.3 19.8 %all_gather.14.hidden_ref = bf16[1280,384]{1,0:T(8,128)(2,1)S(1)} all-gather(bf16[320,384]{1,0:T(8,128)(2,1)S(1)} %shard_map.67), channel_id=1, replica_groups=mesh['sec'=2,'ep'=64,'tp'=4] {'tp'}, dimensions={0}, use_global_device_ids=true | all-gather | bytes 1228800 | tf_op jit(solution)/shard_map/all_gather | solution.py:275
  135.1 1.9 collective-permute-start.4
  137.1 2.4 shard_map.68.own_ref
  139.4 0.1 collective-permute-done.4.hidden_ref
  139.6 2.4 shard_map.69
  142.0 4.2 %all-to-all-start.2 = ((bf16[16,32,640]{2,1,0:T(8,128)(2,1)}), bf16[16,32,640]{2,1,0:T(8,128)(2,1)S(1)}, u32[]{:S(2)}, u32[]{:S(2)}) async-start(bf16[16,32,640]{2,1,0:T(8,128)(2,1)} %bitcast.24), calls=%async_computation.2 | async-start | bytes 1310720 | tf_op jit(solution)/shard_map/all_to_all | solution.py:221
  146.2 5.1 %all-gather.5.cloned.1.call-done.blocks_ref = bf16[2048,640]{1,0:T(8,128)(2,1)} async-done(((bf16[512,640]{1,0:T(8,128)(2,1)}), bf16[2048,640]{1,0:T(8,128)(2,1)}) %all-gather.5.cloned.1.call-update) | async-done | bytes 2621456 | tf_op jit(solution)/shard_map/all_gather | solution.py:307
  151.2 5.2 %shard_map.70 = (f32[320,768]{1,0:T(8,128)S(1)}, bf16[320,768]{1,0:T(8,128)(2,1)S(1)}) custom-call(s32[3]{0:T(128)S(1)} %pad_add_fusion.refs_0_.place_ref, bf16[2048,640]{1,0:T(8,128)(2,1)} %all-gather.5.cloned.1.call-done.blocks_ref, bf16[2048,384]{1,0:T(8,128)(2,1)} %bitcast.66, bf16[2048,384]{1,0:T(8,128)(2,1)} %bitcast.68), custom_call_target="tpu_custom_call" | custom-call | flops 2147483648 | bytes 5767180 | tf_op jit(solution)/shard_map/pallas_call | solution.py:23
  156.4 1.9 collective-permute-start.5
  158.4 1.8 collective-permute-done.5.got_ref
  160.2 0.2 shard_map.71
  160.4 14.8 %all_gather.15.hidden_ref = bf16[1280,384]{1,0:T(8,128)(2,1)S(1)} all-gather(bf16[320,384]{1,0:T(8,128)(2,1)S(1)} %shard_map.71), channel_id=1, replica_groups=mesh['sec'=2,'ep'=64,'tp'=4] {'tp'}, dimensions={0}, use_global_device_ids=true | all-gather | bytes 1228800 | tf_op jit(solution)/shard_map/all_gather | solution.py:275
  175.2 2.1 collective-permute-start.6
  177.3 2.4 shard_map.72.own_ref
  179.7 0.0 collective-permute-done.6.hidden_ref
  179.7 2.4 shard_map.73
  182.1 0.0 all-to-all-done.2
  182.1 0.0 copy-start.3
  182.1 12.2 %all-to-all-start.3 = ((bf16[64,8,640]{2,1,0:T(8,128)(2,1)}), bf16[64,8,640]{2,1,0:T(8,128)(2,1)S(1)}, u32[]{:S(2)}, u32[]{:S(2)}) async-start(bf16[64,8,640]{2,1,0:T(8,128)(2,1)} %bitcast.31), calls=%async_computation.3 | async-start | bytes 1310720 | tf_op jit(solution)/shard_map/all_to_all | solution.py:221
  194.3 0.0 copy-start.4
  194.4 0.1 dynamic-slice_bitcast_fusion.3
  194.4 2.4 collective-permute-start.10
  196.8 4.4 %collective-permute-start.11 = (bf16[128,640]{1,0:T(8,128)(2,1)S(1)}, bf16[128,640]{1,0:T(8,128)(2,1)S(1)}, u32[]{:S(2)}, u32[]{:S(2)}) collective-permute-start(bf16[128,640]{1,0:T(8,128)(2,1)S(1)} %get-tuple-element.37), channel_id=1, source_target_pairs={{0,128},{4,132},{8,136},{12,140},{16,144},{20,148},{24,152},{28,15... | collective-permute-start | bytes 491528 | tf_op jit(solution)/shard_map/ppermute | solution.py:229
  201.2 1.9 collective-permute-start.12
  203.1 0.2 fusion.3
  203.3 0.1 copy.20
  203.4 1.9 collective-permute-start.7
  205.3 1.2 collective-permute-done.7
  206.6 1.9 collective-permute-start.8
  208.5 5.4 %collective-permute-done.8 = f32[128,64]{1,0:T(8,128)S(1)} collective-permute-done((f32[128,64]{1,0:T(8,128)S(1)}, f32[128,64]{1,0:T(8,128)S(1)}, u32[]{:S(2)}, u32[]{:S(2)}) %collective-permute-start.8) | collective-permute-done | bytes 32800 | tf_op jit(solution)/shard_map/ppermute | solution.py:217
  214.0 2.2 collective-permute-start.9
  216.1 0.0 copy-done.4
  216.1 0.1 copy.21.ids_ref
  216.2 5.4 %collective-permute-done.9 = f32[128,64]{1,0:T(8,128)S(1)} collective-permute-done((f32[128,64]{1,0:T(8,128)S(1)}, f32[128,64]{1,0:T(8,128)S(1)}, u32[]{:S(2)}, u32[]{:S(2)}) %collective-permute-start.9) | collective-permute-done | bytes 32800 | tf_op jit(solution)/shard_map/ppermute | solution.py:217
  221.6 0.0 collective-permute-done.10
  221.6 0.0 collective-permute-done.11
  221.7 0.0 collective-permute-done.12
  221.7 0.1 pad_maximum_fusion.block_ref
  221.7 1.9 shard_map.74
  223.7 9.7 %all-to-all-done.3 = bf16[64,8,640]{2,1,0:T(8,128)(2,1)S(1)} async-done(((bf16[64,8,640]{2,1,0:T(8,128)(2,1)}), bf16[64,8,640]{2,1,0:T(8,128)(2,1)S(1)}, u32[]{:S(2)}, u32[]{:S(2)}) %all-to-all-start.3) | async-done | bytes 655392 | tf_op jit(solution)/shard_map/all_to_all | solution.py:221
  233.4 1.6 shard_map.75
  (17 shorter events, 0.2 us)
Async XLA Ops:
  6.5 196.6 %copy-start = (bf16[512,64]{0,1:T(8,128)(2,1)S(1)}, bf16[512,64]{0,1:T(8,128)(2,1)}, u32[]{:S(2)}) copy-start(bf16[512,64]{0,1:T(8,128)(2,1)} %param.7) | copy-start | bytes 196612
  8.9 57.0 %all-to-all-start = ((bf16[64,8,640]{2,1,0:T(8,128)(2,1)}), bf16[64,8,640]{2,1,0:T(8,128)(2,1)S(1)}, u32[]{:S(2)}, u32[]{:S(2)}) async-start(bf16[64,8,640]{2,1,0:T(8,128)(2,1)} %bitcast.4), calls=%async_computation | async-start | bytes 1310720 | tf_op jit(solution)/shard_map/all_to_all | solution.py:221
  27.5 78.5 %all-gather.3.cloned.1.call-start = ((), (), s32[]{:S(2)}) async-start(), calls=%async_computation.4 | async-start | bytes 3276800 | tf_op jit(solution)/shard_map/all_gather | solution.py:304
  29.8 14.2 %collective-permute-start = (bf16[128,640]{1,0:T(8,128)(2,1)S(1)}, bf16[128,640]{1,0:T(8,128)(2,1)S(1)}, u32[]{:S(2)}, u32[]{:S(2)}) collective-permute-start(bf16[128,640]{1,0:T(8,128)(2,1)S(1)} %get-tuple-element.41), channel_id=1, source_target_pairs={{0,192},{4,196},{8,200},{12,204},{16,208},{20,212},{24,216},{28,22... | collective-permute-start | bytes 491528 | tf_op jit(solution)/shard_map/ppermute | solution.py:229
  32.6 11.4 %collective-permute-start.1 = (bf16[128,640]{1,0:T(8,128)(2,1)S(1)}, bf16[128,640]{1,0:T(8,128)(2,1)S(1)}, u32[]{:S(2)}, u32[]{:S(2)}) collective-permute-start(bf16[128,640]{1,0:T(8,128)(2,1)S(1)} %get-tuple-element.40), channel_id=1, source_target_pairs={{0,128},{4,132},{8,136},{12,140},{16,144},{20,148},{24,152},{28,15... | collective-permute-start | bytes 491528 | tf_op jit(solution)/shard_map/ppermute | solution.py:229
  35.5 11.0 %collective-permute-start.2 = (bf16[128,640]{1,0:T(8,128)(2,1)S(1)}, bf16[128,640]{1,0:T(8,128)(2,1)S(1)}, u32[]{:S(2)}, u32[]{:S(2)}) collective-permute-start(bf16[128,640]{1,0:T(8,128)(2,1)S(1)} %get-tuple-element.39), channel_id=1, source_target_pairs={{0,64},{4,68},{8,72},{12,76},{16,80},{20,84},{24,88},{28,92},{32,9... | collective-permute-start | bytes 491528 | tf_op jit(solution)/shard_map/ppermute | solution.py:229
  65.9 0.8 copy-start.2
  66.8 84.5 %all-gather.5.cloned.1.call-start = ((), (), s32[]{:S(2)}) async-start(), calls=%async_computation.5 | async-start | bytes 3276800 | tf_op jit(solution)/shard_map/all_gather | solution.py:307
  111.3 3.8 %collective-permute-start.3 = (bf16[320,768]{1,0:T(8,128)(2,1)S(1)}, bf16[320,768]{1,0:T(8,128)(2,1)S(1)}, u32[]{:S(2)}, u32[]{:S(2)}) collective-permute-start(bf16[320,768]{1,0:T(8,128)(2,1)S(1)} %get-tuple-element.25), channel_id=1, source_target_pairs={{0,256},{256,0},{1,257},{257,1},{2,258},{258,2},{3,259},{259,3},{4... | collective-permute-start | bytes 1474568 | tf_op jit(solution)/shard_map/ppermute | solution.py:217
  115.1 22.0 %copy-start.1 = (bf16[1,1536,512]{2,1,0:T(8,128)(2,1)S(1)}, bf16[1,1536,512]{2,1,0:T(8,128)(2,1)}, u32[]{:S(2)}) copy-start(bf16[1,1536,512]{2,1,0:T(8,128)(2,1)} %param.11) | copy-start | bytes 4718596
  135.1 4.4 %collective-permute-start.4 = (bf16[1280,384]{1,0:T(8,128)(2,1)S(1)}, bf16[1280,384]{1,0:T(8,128)(2,1)S(1)}, u32[]{:S(2)}, u32[]{:S(2)}) collective-permute-start(bf16[1280,384]{1,0:T(8,128)(2,1)S(1)} %all_gather.14.hidden_ref), channel_id=1, source_target_pairs={{0,256},{256,0},{1,257},{257,1},{2,258},{258,2},{3,259},{259,3},{4... | collective-permute-start | bytes 2949128 | tf_op jit(solution)/shard_map/ppermute | solution.py:217
  142.0 40.1 %all-to-all-start.2 = ((bf16[16,32,640]{2,1,0:T(8,128)(2,1)}), bf16[16,32,640]{2,1,0:T(8,128)(2,1)S(1)}, u32[]{:S(2)}, u32[]{:S(2)}) async-start(bf16[16,32,640]{2,1,0:T(8,128)(2,1)} %bitcast.24), calls=%async_computation.2 | async-start | bytes 1310720 | tf_op jit(solution)/shard_map/all_to_all | solution.py:221
  156.4 3.8 %collective-permute-start.5 = (bf16[320,768]{1,0:T(8,128)(2,1)S(1)}, bf16[320,768]{1,0:T(8,128)(2,1)S(1)}, u32[]{:S(2)}, u32[]{:S(2)}) collective-permute-start(bf16[320,768]{1,0:T(8,128)(2,1)S(1)} %get-tuple-element.28), channel_id=1, source_target_pairs={{0,256},{256,0},{1,257},{257,1},{2,258},{258,2},{3,259},{259,3},{4... | collective-permute-start | bytes 1474568 | tf_op jit(solution)/shard_map/ppermute | solution.py:217
  175.2 4.5 %collective-permute-start.6 = (bf16[1280,384]{1,0:T(8,128)(2,1)S(1)}, bf16[1280,384]{1,0:T(8,128)(2,1)S(1)}, u32[]{:S(2)}, u32[]{:S(2)}) collective-permute-start(bf16[1280,384]{1,0:T(8,128)(2,1)S(1)} %all_gather.15.hidden_ref), channel_id=1, source_target_pairs={{0,256},{256,0},{1,257},{257,1},{2,258},{258,2},{3,259},{259,3},{4... | collective-permute-start | bytes 2949128 | tf_op jit(solution)/shard_map/ppermute | solution.py:217
  182.1 21.0 %copy-start.3 = (bf16[128,512]{1,0:T(8,128)(2,1)S(1)}, bf16[128,512]{1,0:T(8,128)(2,1)}, u32[]{:S(2)}) copy-start(bf16[128,512]{1,0:T(8,128)(2,1)} %refs_2_.1) | copy-start | bytes 393220
  182.1 51.2 %all-to-all-start.3 = ((bf16[64,8,640]{2,1,0:T(8,128)(2,1)}), bf16[64,8,640]{2,1,0:T(8,128)(2,1)S(1)}, u32[]{:S(2)}, u32[]{:S(2)}) async-start(bf16[64,8,640]{2,1,0:T(8,128)(2,1)} %bitcast.31), calls=%async_computation.3 | async-start | bytes 1310720 | tf_op jit(solution)/shard_map/all_to_all | solution.py:221
  194.3 21.8 %copy-start.4 = (s32[128,8]{0,1:T(8,128)S(1)}, s32[128,8]{0,1:T(8,128)}, u32[]{:S(2)}) copy-start(s32[128,8]{0,1:T(8,128)} %param.8) | copy-start | bytes 12292
  194.4 27.2 %collective-permute-start.10 = (bf16[128,640]{1,0:T(8,128)(2,1)S(1)}, bf16[128,640]{1,0:T(8,128)(2,1)S(1)}, u32[]{:S(2)}, u32[]{:S(2)}) collective-permute-start(bf16[128,640]{1,0:T(8,128)(2,1)S(1)} %get-tuple-element.38), channel_id=1, source_target_pairs={{0,64},{4,68},{8,72},{12,76},{16,80},{20,84},{24,88},{28,92},{32,9... | collective-permute-start | bytes 491528 | tf_op jit(solution)/shard_map/ppermute | solution.py:229
  196.8 24.8 %collective-permute-start.11 = (bf16[128,640]{1,0:T(8,128)(2,1)S(1)}, bf16[128,640]{1,0:T(8,128)(2,1)S(1)}, u32[]{:S(2)}, u32[]{:S(2)}) collective-permute-start(bf16[128,640]{1,0:T(8,128)(2,1)S(1)} %get-tuple-element.37), channel_id=1, source_target_pairs={{0,128},{4,132},{8,136},{12,140},{16,144},{20,148},{24,152},{28,15... | collective-permute-start | bytes 491528 | tf_op jit(solution)/shard_map/ppermute | solution.py:229
  201.2 20.5 %collective-permute-start.12 = (bf16[128,640]{1,0:T(8,128)(2,1)S(1)}, bf16[128,640]{1,0:T(8,128)(2,1)S(1)}, u32[]{:S(2)}, u32[]{:S(2)}) collective-permute-start(bf16[128,640]{1,0:T(8,128)(2,1)S(1)} %get-tuple-element.36), channel_id=1, source_target_pairs={{0,192},{4,196},{8,200},{12,204},{16,208},{20,212},{24,216},{28,22... | collective-permute-start | bytes 491528 | tf_op jit(solution)/shard_map/ppermute | solution.py:229
  203.4 3.1 %collective-permute-start.7 = (f32[128,64]{1,0:T(8,128)S(1)}, f32[128,64]{1,0:T(8,128)S(1)}, u32[]{:S(2)}, u32[]{:S(2)}) collective-permute-start(f32[128,64]{1,0:T(8,128)S(1)} %copy.20), channel_id=1, source_target_pairs={{0,256},{256,0},{1,257},{257,1},{2,258},{258,2},{3,259},{259,3},{4... | collective-permute-start | bytes 98312 | tf_op jit(solution)/shard_map/ppermute | solution.py:217
  206.6 7.4 %collective-permute-start.8 = (f32[128,64]{1,0:T(8,128)S(1)}, f32[128,64]{1,0:T(8,128)S(1)}, u32[]{:S(2)}, u32[]{:S(2)}) collective-permute-start(f32[128,64]{1,0:T(8,128)S(1)} %add.34), channel_id=1, source_target_pairs={{0,1},{1,2},{2,3},{3,0},{4,5},{5,6},{6,7},{7,4},{8,9},{9,10},{10,1... | collective-permute-start | bytes 98312 | tf_op jit(solution)/shard_map/ppermute | solution.py:217
  214.0 7.7 %collective-permute-start.9 = (f32[128,64]{1,0:T(8,128)S(1)}, f32[128,64]{1,0:T(8,128)S(1)}, u32[]{:S(2)}, u32[]{:S(2)}) collective-permute-start(f32[128,64]{1,0:T(8,128)S(1)} %add.35), channel_id=1, source_target_pairs={{0,2},{1,3},{2,0},{3,1},{4,6},{5,7},{6,4},{7,5},{8,10},{9,11},{10,... | collective-permute-start | bytes 98312 | tf_op jit(solution)/shard_map/ppermute | solution.py:217
Sparse Core Ops, SparseCore 0:
  66.9 34.6 all-gather.2
  106.2 44.9 all-gather.4

commit v5 on v4

--- a/solution.py
+++ b/solution.py
@@ -146,9 +146,8 @@
 
 
 def down_half(side, hidden_ref, down_ref, out_ref, slab, sem):
-    total = jnp.zeros((320, 512), F32)
-    for y in range(4):
-        total = total + dot(hidden_ref[y * 320:(y + 1) * 320, :], down_ref[y * 384:(y + 1) * 384, :])
+    units = jnp.concatenate([hidden_ref[y * 320:(y + 1) * 320, :] for y in range(4)], axis=1)
+    total = dot(units, down_ref[...])
     rows = total.astype(BF)
     slab[:, :512] = rows[:256]
     slab[:, 512:] = pack(rows[256:])
@@ -176,7 +175,7 @@
     return chosen, jnp.where(chosen > 0, rank, F32(-1.0))
 
 
-def weighted(slot, probs, block, c, expert):
+def weights_of(slot, probs, c, expert):
     high = probs.astype(BF)
     low = (probs - high.astype(F32)).astype(BF)
     shape = (EXPERTS, EXPERTS * 8)
@@ -185,32 +184,34 @@
     row = iota(wide.shape, 1) & 7
     main = wide == (row + SLOTS * c).astype(F32)
     extra = wide == ((row >> 2) + (SLOTS * c + 8)).astype(F32)
-    total = jnp.zeros((slot.shape[0], 512), F32)
-    for part in (high, low):
-        weight = dot(part, spread)
-        total = total + dot(jnp.where(main, weight, F32(0.0)).astype(BF), block[:, :512])
-        pieces = [
-            dot(jnp.where(extra & ((row & 3) == f), weight, F32(0.0)).astype(BF), block[:, 512:]) for f in range(4)
-        ]
-        total = total + jnp.concatenate(pieces, axis=1)
-    return total
-
-
-def combine_a_body(place_ref, ids_ref, logits_ref, block_ref, acc_ref, probs_ref, slot_ref):
+    parts = [dot(part, spread) for part in (high, low)]
+    masks = [main] + [extra & ((row & 3) == f) for f in range(4)]
+    return [jnp.where(mask, part, F32(0.0)).astype(BF) for mask in masks for part in parts]
+
+
+def weighted(weights, block):
+    n = weights.shape[0] // 10
+    main = dot(weights[:2 * n], block[:, :512])
+    extra = dot(weights[2 * n:], block[:, 512:])
+    pieces = [extra[2 * f * n:(2 * f + 1) * n] + extra[(2 * f + 1) * n:(2 * f + 2) * n] for f in range(4)]
+    return main[:n] + main[n:] + jnp.concatenate(pieces, axis=1)
+
+
+def combine_a_body(place_ref, ids_ref, logits_ref, block_ref, acc_ref, weights_ref):
     chosen, slot = slots_of(ids_ref[...])
     raised = jnp.where(chosen > 0, jnp.exp(logits_ref[...]), F32(0.0))
     probs = raised / jnp.sum(raised, axis=1, keepdims=True)
-    probs_ref[...] = probs
-    slot_ref[...] = slot
 
     def expert(i):
         return (((place_ref[2] + 4 - (i >> 4)) & 3) << 4) + (i & 15)
 
-    acc_ref[...] = weighted(slot, probs, block_ref[...], 0, expert)
-
-
-def combine_b_body(acc_ref, probs_ref, slot_ref, block_ref, out_ref):
-    out_ref[...] = (acc_ref[...] + weighted(slot_ref[...], probs_ref[...], block_ref[...], 1, z_first)).astype(BF)
+    acc_ref[...] = weighted(jnp.concatenate(weights_of(slot, probs, 0, expert), axis=0), block_ref[...])
+    for i, part in enumerate(weights_of(slot, probs, 1, z_first)):
+        weights_ref[i * 128:(i + 1) * 128, :] = part
+
+
+def combine_b_body(acc_ref, weights_ref, block_ref, out_ref):
+    out_ref[...] = (acc_ref[...] + weighted(weights_ref[...], block_ref[...])).astype(BF)
 
 
 def shift(x, axis, size, by):
@@ -318,9 +319,13 @@
     logits = logits + shift(logits, "sec", 2, 1)
     logits = logits + shift(logits, "tp", 4, 1)
     logits = logits + shift(logits, "tp", 4, 2)
-    table = ((128, EXPERTS), F32)
-    acc, probs, slot = call(combine_a_body, [((128, 512), F32), table, table], (place, expert_ids, logits, back_a), [SMEM] + [VMEM] * 3)
-    mixture, = call(combine_b_body, [((128, 512), BF)], (acc, probs, slot, back_b))
+    acc, weights_b = call(
+        combine_a_body,
+        [((128, 512), F32), ((1280, 512), BF)],
+        (place, expert_ids, logits, back_a),
+        [SMEM] + [VMEM] * 3,
+    )
+    mixture, = call(combine_b_body, [((128, 512), BF)], (acc, weights_b, back_b))
     return mixture
 
 

time: 243 us -> 242 us (level)
  transfers between devices with their start and end apart: 18 -> 18, of which waited for: 11 -> 12; matrix products, arithmetic and copies ran while one was open for 0% -> 0% of each run, Pallas kernels for 10% -> 10%
where the time goes in v5:
time: 242 us; the launch traced here: 241 us
  blocking collectives  74 us (31%)
  starting transfers between devices  67.4 us (28%)
  waiting for transfers between devices  56.8 us (23%)
  Pallas kernels  27.4 us (11%)
  between operations  13.8 us (6%)
    all_to_all x1, blocking collectives, exchange(): lax.all_to_all(x, 'ep', split_axis=0, concat_axis=0, tiled=True, axis_ind...  39.3 us
    all_to_all x3, starting transfers between devices, exchange(): lax.all_to_all(x, 'ep', split_axis=0, concat_axis=0, tiled=True, axis_ind...  35 us
    all_gather x2, blocking collectives, gather(): return lax.all_gather(hidden, 'tp', axis=0, tiled=True)  34.7 us
    all_to_all x3, waiting for transfers between devices, exchange(): lax.all_to_all(x, 'ep', split_axis=0, concat_axis=0, tiled=True, axis_ind...  28.6 us
    pallas_call x12, Pallas kernels, call(): pl.pallas_call(body, out_shape=[jax.ShapeDtypeStruct(*o) for o in outs],...  27.4 us
    ppermute x6, starting transfers between devices, shift_x(): lax.ppermute(part, 'ep', [(i, (i + 16 * by) % 64) for i in range(64)])  18.5 us
    ppermute x7, waiting for transfers between devices, shift(): return lax.ppermute(x, axis, [(i, (i + by) % size) for i in range(size)])  16.1 us
    ppermute x7, starting transfers between devices, shift(): return lax.ppermute(x, axis, [(i, (i + by) % size) for i in range(size)])  13.9 us
  transfers between devices with their start and end apart: 18, of which 12 were waited for; matrix products, arithmetic and copies ran while one was open for 0% of the time, Pallas kernels for 10%

profile of v5, /device:TPU:6, one launch (start us, length us, event | category | flops | bytes accessed | tf_op | source)
XLA Modules:
  0.0 241.1 jit_solution(15170078295561438653)
XLA Ops:
  6.5 0.0 copy-start
  6.5 2.4 shard_map.64
  8.9 18.6 %all-to-all-start = ((bf16[64,8,640]{2,1,0:T(8,128)(2,1)}), bf16[64,8,640]{2,1,0:T(8,128)(2,1)S(1)}, u32[]{:S(2)}, u32[]{:S(2)}) async-start(bf16[64,8,640]{2,1,0:T(8,128)(2,1)} %bitcast.4), calls=%async_computation | async-start | bytes 1310720 | tf_op jit(solution)/shard_map/all_to_all | solution.py:222
  27.5 0.0 all-gather.3.cloned.1.call-start
  27.6 0.1 pad_add_fusion.refs_0_.place_ref
  27.7 2.1 shard_map.65
  29.8 2.8 %collective-permute-start = (bf16[128,640]{1,0:T(8,128)(2,1)S(1)}, bf16[128,640]{1,0:T(8,128)(2,1)S(1)}, u32[]{:S(2)}, u32[]{:S(2)}) collective-permute-start(bf16[128,640]{1,0:T(8,128)(2,1)S(1)} %get-tuple-element.39), channel_id=1, source_target_pairs={{0,192},{4,196},{8,200},{12,204},{16,208},{20,212},{24,216},{28,22... | collective-permute-start | bytes 491528 | tf_op jit(solution)/shard_map/ppermute | solution.py:230
  32.6 3.0 %collective-permute-start.1 = (bf16[128,640]{1,0:T(8,128)(2,1)S(1)}, bf16[128,640]{1,0:T(8,128)(2,1)S(1)}, u32[]{:S(2)}, u32[]{:S(2)}) collective-permute-start(bf16[128,640]{1,0:T(8,128)(2,1)S(1)} %get-tuple-element.38), channel_id=1, source_target_pairs={{0,128},{4,132},{8,136},{12,140},{16,144},{20,148},{24,152},{28,15... | collective-permute-start | bytes 491528 | tf_op jit(solution)/shard_map/ppermute | solution.py:230
  35.5 4.1 %collective-permute-start.2 = (bf16[128,640]{1,0:T(8,128)(2,1)S(1)}, bf16[128,640]{1,0:T(8,128)(2,1)S(1)}, u32[]{:S(2)}, u32[]{:S(2)}) collective-permute-start(bf16[128,640]{1,0:T(8,128)(2,1)S(1)} %get-tuple-element.37), channel_id=1, source_target_pairs={{0,64},{4,68},{8,72},{12,76},{16,80},{20,84},{24,88},{28,92},{32,9... | collective-permute-start | bytes 491528 | tf_op jit(solution)/shard_map/ppermute | solution.py:230
  39.7 4.3 %collective-permute-done = bf16[128,640]{1,0:T(8,128)(2,1)S(1)} collective-permute-done((bf16[128,640]{1,0:T(8,128)(2,1)S(1)}, bf16[128,640]{1,0:T(8,128)(2,1)S(1)}, u32[]{:S(2)}, u32[]{:S(2)}) %collective-permute-start) | collective-permute-done | bytes 163872 | tf_op jit(solution)/shard_map/ppermute | solution.py:230
  44.0 0.0 collective-permute-done.1
  44.0 2.5 %collective-permute-done.2 = bf16[128,640]{1,0:T(8,128)(2,1)S(1)} collective-permute-done((bf16[128,640]{1,0:T(8,128)(2,1)S(1)}, bf16[128,640]{1,0:T(8,128)(2,1)S(1)}, u32[]{:S(2)}, u32[]{:S(2)}) %collective-permute-start.2) | collective-permute-done | bytes 163872 | tf_op jit(solution)/shard_map/ppermute | solution.py:230
  46.7 0.1 constant_dynamic-slice_fusion
  46.8 19.1 %all-to-all-done = bf16[64,8,640]{2,1,0:T(8,128)(2,1)S(1)} async-done(((bf16[64,8,640]{2,1,0:T(8,128)(2,1)}), bf16[64,8,640]{2,1,0:T(8,128)(2,1)S(1)}, u32[]{:S(2)}, u32[]{:S(2)}) %all-to-all-start) | async-done | bytes 655392 | tf_op jit(solution)/shard_map/all_to_all | solution.py:222
  65.9 0.8 copy-done.2
  66.7 0.0 all-gather.3.cloned.1.call-update
  66.8 0.0 all-gather.5.cloned.1.call-start
  66.8 39.3 %all_to_all.47 = bf16[16,32,640]{2,1,0:T(8,128)(2,1)} all-to-all(bf16[16,32,640]{2,1,0:T(8,128)(2,1)S(1)} %bitcast.62), channel_id=1, replica_groups={{0,4,8,12,16,20,24,28,32,36,40,44,48,52,56,60},{64,68,72,76,80,84,88,92..., dimensions={0} | all-to-all | bytes 1310720 | tf_op jit(solution)/shard_map/all_to_all | solution.py:222
  106.1 0.0 all-gather.5.cloned.1.call-update
  106.1 5.2 %shard_map.66 = (f32[320,768]{1,0:T(8,128)S(1)}, bf16[320,768]{1,0:T(8,128)(2,1)S(1)}) custom-call(s32[3]{0:T(128)S(1)} %pad_add_fusion.refs_0_.place_ref, bf16[2048,640]{1,0:T(8,128)(2,1)} %all-gather.3.cloned.1.call-done.blocks_ref, bf16[2048,384]{1,0:T(8,128)(2,1)} %bitcast.65, bf16[2048,384]{1,0:T(8,128)(2,1)} %bitcast.67), custom_call_target="tpu_custom_call" | custom-call | flops 2147483648 | bytes 5767180 | tf_op jit(solution)/shard_map/pallas_call | solution.py:23
  111.3 1.9 collective-permute-start.3
  113.2 1.8 collective-permute-done.3.got_ref
  115.1 0.2 shard_map.67
  115.3 19.8 %all_gather.14.hidden_ref = bf16[1280,384]{1,0:T(8,128)(2,1)S(1)} all-gather(bf16[320,384]{1,0:T(8,128)(2,1)S(1)} %shard_map.67), channel_id=1, replica_groups=mesh['sec'=2,'ep'=64,'tp'=4] {'tp'}, dimensions={0}, use_global_device_ids=true | all-gather | bytes 1228800 | tf_op jit(solution)/shard_map/all_gather | solution.py:276
  135.1 1.9 collective-permute-start.4
  137.1 2.2 shard_map.68.own_ref
  139.3 0.3 collective-permute-done.4.hidden_ref
  139.6 2.2 shard_map.69
  141.8 4.2 %all-to-all-start.2 = ((bf16[16,32,640]{2,1,0:T(8,128)(2,1)}), bf16[16,32,640]{2,1,0:T(8,128)(2,1)S(1)}, u32[]{:S(2)}, u32[]{:S(2)}) async-start(bf16[16,32,640]{2,1,0:T(8,128)(2,1)} %bitcast.24), calls=%async_computation.2 | async-start | bytes 1310720 | tf_op jit(solution)/shard_map/all_to_all | solution.py:222
  146.0 5.2 %all-gather.5.cloned.1.call-done.blocks_ref = bf16[2048,640]{1,0:T(8,128)(2,1)} async-done(((bf16[512,640]{1,0:T(8,128)(2,1)}), bf16[2048,640]{1,0:T(8,128)(2,1)}) %all-gather.5.cloned.1.call-update) | async-done | bytes 2621456 | tf_op jit(solution)/shard_map/all_gather | solution.py:308
  151.2 5.2 %shard_map.70 = (f32[320,768]{1,0:T(8,128)S(1)}, bf16[320,768]{1,0:T(8,128)(2,1)S(1)}) custom-call(s32[3]{0:T(128)S(1)} %pad_add_fusion.refs_0_.place_ref, bf16[2048,640]{1,0:T(8,128)(2,1)} %all-gather.5.cloned.1.call-done.blocks_ref, bf16[2048,384]{1,0:T(8,128)(2,1)} %bitcast.66, bf16[2048,384]{1,0:T(8,128)(2,1)} %bitcast.68), custom_call_target="tpu_custom_call" | custom-call | flops 2147483648 | bytes 5767180 | tf_op jit(solution)/shard_map/pallas_call | solution.py:23
  156.4 1.9 collective-permute-start.5
  158.4 1.8 collective-permute-done.5.got_ref
  160.2 0.2 shard_map.71
  160.4 14.8 %all_gather.15.hidden_ref = bf16[1280,384]{1,0:T(8,128)(2,1)S(1)} all-gather(bf16[320,384]{1,0:T(8,128)(2,1)S(1)} %shard_map.71), channel_id=1, replica_groups=mesh['sec'=2,'ep'=64,'tp'=4] {'tp'}, dimensions={0}, use_global_device_ids=true | all-gather | bytes 1228800 | tf_op jit(solution)/shard_map/all_gather | solution.py:276
  175.2 2.1 collective-permute-start.6
  177.3 2.2 shard_map.72.own_ref
  179.6 0.1 collective-permute-done.6.hidden_ref
  179.7 2.2 shard_map.73
  181.9 0.0 all-to-all-done.2
  181.9 0.0 copy-start.3
  181.9 12.2 %all-to-all-start.3 = ((bf16[64,8,640]{2,1,0:T(8,128)(2,1)}), bf16[64,8,640]{2,1,0:T(8,128)(2,1)S(1)}, u32[]{:S(2)}, u32[]{:S(2)}) async-start(bf16[64,8,640]{2,1,0:T(8,128)(2,1)} %bitcast.31), calls=%async_computation.3 | async-start | bytes 1310720 | tf_op jit(solution)/shard_map/all_to_all | solution.py:222
  194.2 0.0 copy-start.4
  194.2 0.1 dynamic-slice_bitcast_fusion.3
  194.3 2.4 collective-permute-start.10
  196.6 4.4 %collective-permute-start.11 = (bf16[128,640]{1,0:T(8,128)(2,1)S(1)}, bf16[128,640]{1,0:T(8,128)(2,1)S(1)}, u32[]{:S(2)}, u32[]{:S(2)}) collective-permute-start(bf16[128,640]{1,0:T(8,128)(2,1)S(1)} %get-tuple-element.35), channel_id=1, source_target_pairs={{0,128},{4,132},{8,136},{12,140},{16,144},{20,148},{24,152},{28,15... | collective-permute-start | bytes 491528 | tf_op jit(solution)/shard_map/ppermute | solution.py:230
  201.0 1.9 collective-permute-start.12
  202.9 0.0 copy-done
  203.0 0.2 fusion.3
  203.1 0.1 copy.20
  203.2 1.9 collective-permute-start.7
  205.1 1.2 collective-permute-done.7
  206.4 1.9 collective-permute-start.8
  208.3 5.4 %collective-permute-done.8 = f32[128,64]{1,0:T(8,128)S(1)} collective-permute-done((f32[128,64]{1,0:T(8,128)S(1)}, f32[128,64]{1,0:T(8,128)S(1)}, u32[]{:S(2)}, u32[]{:S(2)}) %collective-permute-start.8) | collective-permute-done | bytes 32800 | tf_op jit(solution)/shard_map/ppermute | solution.py:218
  213.8 2.2 collective-permute-start.9
  215.9 0.1 copy.21.ids_ref
  216.0 5.4 %collective-permute-done.9 = f32[128,64]{1,0:T(8,128)S(1)} collective-permute-done((f32[128,64]{1,0:T(8,128)S(1)}, f32[128,64]{1,0:T(8,128)S(1)}, u32[]{:S(2)}, u32[]{:S(2)}) %collective-permute-start.9) | collective-permute-done | bytes 32800 | tf_op jit(solution)/shard_map/ppermute | solution.py:218
  221.4 0.0 collective-permute-done.10
  221.5 0.0 collective-permute-done.11
  221.5 0.0 collective-permute-done.12
  221.5 0.1 pad_maximum_fusion.block_ref
  221.5 2.0 shard_map.74
  223.6 9.5 %all-to-all-done.3 = bf16[64,8,640]{2,1,0:T(8,128)(2,1)S(1)} async-done(((bf16[64,8,640]{2,1,0:T(8,128)(2,1)}), bf16[64,8,640]{2,1,0:T(8,128)(2,1)S(1)}, u32[]{:S(2)}, u32[]{:S(2)}) %all-to-all-start.3) | async-done | bytes 655392 | tf_op jit(solution)/shard_map/all_to_all | solution.py:222
  233.0 1.2 shard_map.75
  (17 shorter events, 0.2 us)
Async XLA Ops:
  6.5 196.4 %copy-start = (bf16[512,64]{0,1:T(8,128)(2,1)S(1)}, bf16[512,64]{0,1:T(8,128)(2,1)}, u32[]{:S(2)}) copy-start(bf16[512,64]{0,1:T(8,128)(2,1)} %param.7) | copy-start | bytes 196612
  8.9 57.0 %all-to-all-start = ((bf16[64,8,640]{2,1,0:T(8,128)(2,1)}), bf16[64,8,640]{2,1,0:T(8,128)(2,1)S(1)}, u32[]{:S(2)}, u32[]{:S(2)}) async-start(bf16[64,8,640]{2,1,0:T(8,128)(2,1)} %bitcast.4), calls=%async_computation | async-start | bytes 1310720 | tf_op jit(solution)/shard_map/all_to_all | solution.py:222
  27.5 78.5 %all-gather.3.cloned.1.call-start = ((), (), s32[]{:S(2)}) async-start(), calls=%async_computation.4 | async-start | bytes 3276800 | tf_op jit(solution)/shard_map/all_gather | solution.py:305
  29.8 14.2 %collective-permute-start = (bf16[128,640]{1,0:T(8,128)(2,1)S(1)}, bf16[128,640]{1,0:T(8,128)(2,1)S(1)}, u32[]{:S(2)}, u32[]{:S(2)}) collective-permute-start(bf16[128,640]{1,0:T(8,128)(2,1)S(1)} %get-tuple-element.39), channel_id=1, source_target_pairs={{0,192},{4,196},{8,200},{12,204},{16,208},{20,212},{24,216},{28,22... | collective-permute-start | bytes 491528 | tf_op jit(solution)/shard_map/ppermute | solution.py:230
  32.6 11.4 %collective-permute-start.1 = (bf16[128,640]{1,0:T(8,128)(2,1)S(1)}, bf16[128,640]{1,0:T(8,128)(2,1)S(1)}, u32[]{:S(2)}, u32[]{:S(2)}) collective-permute-start(bf16[128,640]{1,0:T(8,128)(2,1)S(1)} %get-tuple-element.38), channel_id=1, source_target_pairs={{0,128},{4,132},{8,136},{12,140},{16,144},{20,148},{24,152},{28,15... | collective-permute-start | bytes 491528 | tf_op jit(solution)/shard_map/ppermute | solution.py:230
  35.5 11.0 %collective-permute-start.2 = (bf16[128,640]{1,0:T(8,128)(2,1)S(1)}, bf16[128,640]{1,0:T(8,128)(2,1)S(1)}, u32[]{:S(2)}, u32[]{:S(2)}) collective-permute-start(bf16[128,640]{1,0:T(8,128)(2,1)S(1)} %get-tuple-element.37), channel_id=1, source_target_pairs={{0,64},{4,68},{8,72},{12,76},{16,80},{20,84},{24,88},{28,92},{32,9... | collective-permute-start | bytes 491528 | tf_op jit(solution)/shard_map/ppermute | solution.py:230
  65.9 0.8 copy-start.2
  66.8 84.5 %all-gather.5.cloned.1.call-start = ((), (), s32[]{:S(2)}) async-start(), calls=%async_computation.5 | async-start | bytes 3276800 | tf_op jit(solution)/shard_map/all_gather | solution.py:308
  111.3 3.8 %collective-permute-start.3 = (bf16[320,768]{1,0:T(8,128)(2,1)S(1)}, bf16[320,768]{1,0:T(8,128)(2,1)S(1)}, u32[]{:S(2)}, u32[]{:S(2)}) collective-permute-start(bf16[320,768]{1,0:T(8,128)(2,1)S(1)} %get-tuple-element.24), channel_id=1, source_target_pairs={{0,256},{256,0},{1,257},{257,1},{2,258},{258,2},{3,259},{259,3},{4... | collective-permute-start | bytes 1474568 | tf_op jit(solution)/shard_map/ppermute | solution.py:218
  115.1 22.0 %copy-start.1 = (bf16[1,1536,512]{2,1,0:T(8,128)(2,1)S(1)}, bf16[1,1536,512]{2,1,0:T(8,128)(2,1)}, u32[]{:S(2)}) copy-start(bf16[1,1536,512]{2,1,0:T(8,128)(2,1)} %param.11) | copy-start | bytes 4718596
  135.1 4.4 %collective-permute-start.4 = (bf16[1280,384]{1,0:T(8,128)(2,1)S(1)}, bf16[1280,384]{1,0:T(8,128)(2,1)S(1)}, u32[]{:S(2)}, u32[]{:S(2)}) collective-permute-start(bf16[1280,384]{1,0:T(8,128)(2,1)S(1)} %all_gather.14.hidden_ref), channel_id=1, source_target_pairs={{0,256},{256,0},{1,257},{257,1},{2,258},{258,2},{3,259},{259,3},{4... | collective-permute-start | bytes 2949128 | tf_op jit(solution)/shard_map/ppermute | solution.py:218
  141.8 40.1 %all-to-all-start.2 = ((bf16[16,32,640]{2,1,0:T(8,128)(2,1)}), bf16[16,32,640]{2,1,0:T(8,128)(2,1)S(1)}, u32[]{:S(2)}, u32[]{:S(2)}) async-start(bf16[16,32,640]{2,1,0:T(8,128)(2,1)} %bitcast.24), calls=%async_computation.2 | async-start | bytes 1310720 | tf_op jit(solution)/shard_map/all_to_all | solution.py:222
  156.4 3.8 %collective-permute-start.5 = (bf16[320,768]{1,0:T(8,128)(2,1)S(1)}, bf16[320,768]{1,0:T(8,128)(2,1)S(1)}, u32[]{:S(2)}, u32[]{:S(2)}) collective-permute-start(bf16[320,768]{1,0:T(8,128)(2,1)S(1)} %get-tuple-element.27), channel_id=1, source_target_pairs={{0,256},{256,0},{1,257},{257,1},{2,258},{258,2},{3,259},{259,3},{4... | collective-permute-start | bytes 1474568 | tf_op jit(solution)/shard_map/ppermute | solution.py:218
  175.2 4.4 %collective-permute-start.6 = (bf16[1280,384]{1,0:T(8,128)(2,1)S(1)}, bf16[1280,384]{1,0:T(8,128)(2,1)S(1)}, u32[]{:S(2)}, u32[]{:S(2)}) collective-permute-start(bf16[1280,384]{1,0:T(8,128)(2,1)S(1)} %all_gather.15.hidden_ref), channel_id=1, source_target_pairs={{0,256},{256,0},{1,257},{257,1},{2,258},{258,2},{3,259},{259,3},{4... | collective-permute-start | bytes 2949128 | tf_op jit(solution)/shard_map/ppermute | solution.py:218
  181.9 21.0 %copy-start.3 = (bf16[128,512]{1,0:T(8,128)(2,1)S(1)}, bf16[128,512]{1,0:T(8,128)(2,1)}, u32[]{:S(2)}) copy-start(bf16[128,512]{1,0:T(8,128)(2,1)} %refs_2_.1) | copy-start | bytes 393220
  181.9 51.1 %all-to-all-start.3 = ((bf16[64,8,640]{2,1,0:T(8,128)(2,1)}), bf16[64,8,640]{2,1,0:T(8,128)(2,1)S(1)}, u32[]{:S(2)}, u32[]{:S(2)}) async-start(bf16[64,8,640]{2,1,0:T(8,128)(2,1)} %bitcast.31), calls=%async_computation.3 | async-start | bytes 1310720 | tf_op jit(solution)/shard_map/all_to_all | solution.py:222
  194.2 21.8 %copy-start.4 = (s32[128,8]{0,1:T(8,128)S(1)}, s32[128,8]{0,1:T(8,128)}, u32[]{:S(2)}) copy-start(s32[128,8]{0,1:T(8,128)} %param.8) | copy-start | bytes 12292
  194.3 27.2 %collective-permute-start.10 = (bf16[128,640]{1,0:T(8,128)(2,1)S(1)}, bf16[128,640]{1,0:T(8,128)(2,1)S(1)}, u32[]{:S(2)}, u32[]{:S(2)}) collective-permute-start(bf16[128,640]{1,0:T(8,128)(2,1)S(1)} %get-tuple-element.36), channel_id=1, source_target_pairs={{0,64},{4,68},{8,72},{12,76},{16,80},{20,84},{24,88},{28,92},{32,9... | collective-permute-start | bytes 491528 | tf_op jit(solution)/shard_map/ppermute | solution.py:230
  196.6 24.8 %collective-permute-start.11 = (bf16[128,640]{1,0:T(8,128)(2,1)S(1)}, bf16[128,640]{1,0:T(8,128)(2,1)S(1)}, u32[]{:S(2)}, u32[]{:S(2)}) collective-permute-start(bf16[128,640]{1,0:T(8,128)(2,1)S(1)} %get-tuple-element.35), channel_id=1, source_target_pairs={{0,128},{4,132},{8,136},{12,140},{16,144},{20,148},{24,152},{28,15... | collective-permute-start | bytes 491528 | tf_op jit(solution)/shard_map/ppermute | solution.py:230
  201.0 20.5 %collective-permute-start.12 = (bf16[128,640]{1,0:T(8,128)(2,1)S(1)}, bf16[128,640]{1,0:T(8,128)(2,1)S(1)}, u32[]{:S(2)}, u32[]{:S(2)}) collective-permute-start(bf16[128,640]{1,0:T(8,128)(2,1)S(1)} %get-tuple-element.34), channel_id=1, source_target_pairs={{0,192},{4,196},{8,200},{12,204},{16,208},{20,212},{24,216},{28,22... | collective-permute-start | bytes 491528 | tf_op jit(solution)/shard_map/ppermute | solution.py:230
  203.2 3.1 %collective-permute-start.7 = (f32[128,64]{1,0:T(8,128)S(1)}, f32[128,64]{1,0:T(8,128)S(1)}, u32[]{:S(2)}, u32[]{:S(2)}) collective-permute-start(f32[128,64]{1,0:T(8,128)S(1)} %copy.20), channel_id=1, source_target_pairs={{0,256},{256,0},{1,257},{257,1},{2,258},{258,2},{3,259},{259,3},{4... | collective-permute-start | bytes 98312 | tf_op jit(solution)/shard_map/ppermute | solution.py:218
  206.4 7.4 %collective-permute-start.8 = (f32[128,64]{1,0:T(8,128)S(1)}, f32[128,64]{1,0:T(8,128)S(1)}, u32[]{:S(2)}, u32[]{:S(2)}) collective-permute-start(f32[128,64]{1,0:T(8,128)S(1)} %add.34), channel_id=1, source_target_pairs={{0,1},{1,2},{2,3},{3,0},{4,5},{5,6},{6,7},{7,4},{8,9},{9,10},{10,1... | collective-permute-start | bytes 98312 | tf_op jit(solution)/shard_map/ppermute | solution.py:218
  213.8 7.7 %collective-permute-start.9 = (f32[128,64]{1,0:T(8,128)S(1)}, f32[128,64]{1,0:T(8,128)S(1)}, u32[]{:S(2)}, u32[]{:S(2)}) collective-permute-start(f32[128,64]{1,0:T(8,128)S(1)} %add.35), channel_id=1, source_target_pairs={{0,2},{1,3},{2,0},{3,1},{4,6},{5,7},{6,4},{7,5},{8,10},{9,11},{10,... | collective-permute-start | bytes 98312 | tf_op jit(solution)/shard_map/ppermute | solution.py:218
Sparse Core Ops, SparseCore 0:
  66.9 34.6 all-gather.2
  106.2 44.9 all-gather.4

commit v6 on v5

--- a/solution.py
+++ b/solution.py
@@ -46,11 +46,9 @@
 
 def pack(extra):
     n = extra.shape[0]
-    shape = (4 * n, n)
-    total = jnp.zeros((4 * n, 128), F32)
-    for f in range(4):
-        total = total + dot(ones_where(iota(shape, 0) == 4 * iota(shape, 1) + f), extra[:, f * 128:(f + 1) * 128])
-    return total.astype(BF)
+    shape = (4 * n, 4 * n)
+    pieces = jnp.concatenate([extra[:, f * 128:(f + 1) * 128] for f in range(4)], axis=0)
+    return dot(ones_where(iota(shape, 1) == (iota(shape, 0) & 3) * n + (iota(shape, 0) >> 2)), pieces).astype(BF)
 
 
 def z_first(i):
@@ -59,9 +57,10 @@
 
 def unpack(pieces):
     n = pieces.shape[0] // 4
-    shape = (n, 4 * n)
-    parts = [dot(ones_where(iota(shape, 1) == 4 * iota(shape, 0) + f), pieces).astype(BF) for f in range(4)]
-    return jnp.concatenate(parts, axis=1)
+    shape = (4 * n, 4 * n)
+    order = ones_where(iota(shape, 0) == (iota(shape, 1) & 3) * n + (iota(shape, 1) >> 2))
+    parts = dot(order, pieces).astype(BF)
+    return jnp.concatenate([parts[f * n:(f + 1) * n] for f in range(4)], axis=1)
 
 
 def rows_of(half):

time: 242 us -> 242 us (level)
  no operation moved by 1% of the time
where the time goes in v6:
time: 242 us; the launch traced here: 241 us
  blocking collectives  74 us (31%)
  starting transfers between devices  67 us (28%)
  waiting for transfers between devices  57.3 us (24%)
  Pallas kernels  27.1 us (11%)
  between operations  13.8 us (6%)
    all_to_all x1, blocking collectives, exchange(): lax.all_to_all(x, 'ep', split_axis=0, concat_axis=0, tiled=True, axis_ind...  39.3 us
    all_gather x2, blocking collectives, gather(): return lax.all_gather(hidden, 'tp', axis=0, tiled=True)  34.7 us
    all_to_all x3, starting transfers between devices, exchange(): lax.all_to_all(x, 'ep', split_axis=0, concat_axis=0, tiled=True, axis_ind...  34.6 us
    all_to_all x3, waiting for transfers between devices, exchange(): lax.all_to_all(x, 'ep', split_axis=0, concat_axis=0, tiled=True, axis_ind...  28.6 us
    pallas_call x12, Pallas kernels, call(): pl.pallas_call(body, out_shape=[jax.ShapeDtypeStruct(*o) for o in outs],...  27.1 us
    ppermute x6, starting transfers between devices, shift_x(): lax.ppermute(part, 'ep', [(i, (i + 16 * by) % 64) for i in range(64)])  18.5 us
    ppermute x7, waiting for transfers between devices, shift(): return lax.ppermute(x, axis, [(i, (i + by) % size) for i in range(size)])  16.2 us
    ppermute x7, starting transfers between devices, shift(): return lax.ppermute(x, axis, [(i, (i + by) % size) for i in range(size)])  13.8 us
  transfers between devices with their start and end apart: 18, of which 12 were waited for; matrix products, arithmetic and copies ran while one was open for 0% of the time, Pallas kernels for 10%

profile of v6, /device:TPU:6, one launch (start us, length us, event | category | flops | bytes accessed | tf_op | source)
XLA Modules:
  0.0 240.8 jit_solution(8336827869798958042)
XLA Ops:
  6.5 0.0 copy-start
  6.5 2.4 shard_map.64
  8.9 18.6 %all-to-all-start = ((bf16[64,8,640]{2,1,0:T(8,128)(2,1)}), bf16[64,8,640]{2,1,0:T(8,128)(2,1)S(1)}, u32[]{:S(2)}, u32[]{:S(2)}) async-start(bf16[64,8,640]{2,1,0:T(8,128)(2,1)} %bitcast.4), calls=%async_computation | async-start | bytes 1310720 | tf_op jit(solution)/shard_map/all_to_all | solution.py:221
  27.5 0.0 all-gather.3.cloned.1.call-start
  27.6 0.1 pad_add_fusion.refs_0_.place_ref
  27.7 2.1 shard_map.65
  29.8 2.8 %collective-permute-start = (bf16[128,640]{1,0:T(8,128)(2,1)S(1)}, bf16[128,640]{1,0:T(8,128)(2,1)S(1)}, u32[]{:S(2)}, u32[]{:S(2)}) collective-permute-start(bf16[128,640]{1,0:T(8,128)(2,1)S(1)} %get-tuple-element.39), channel_id=1, source_target_pairs={{0,192},{4,196},{8,200},{12,204},{16,208},{20,212},{24,216},{28,22... | collective-permute-start | bytes 491528 | tf_op jit(solution)/shard_map/ppermute | solution.py:229
  32.6 3.0 %collective-permute-start.1 = (bf16[128,640]{1,0:T(8,128)(2,1)S(1)}, bf16[128,640]{1,0:T(8,128)(2,1)S(1)}, u32[]{:S(2)}, u32[]{:S(2)}) collective-permute-start(bf16[128,640]{1,0:T(8,128)(2,1)S(1)} %get-tuple-element.38), channel_id=1, source_target_pairs={{0,128},{4,132},{8,136},{12,140},{16,144},{20,148},{24,152},{28,15... | collective-permute-start | bytes 491528 | tf_op jit(solution)/shard_map/ppermute | solution.py:229
  35.5 4.1 %collective-permute-start.2 = (bf16[128,640]{1,0:T(8,128)(2,1)S(1)}, bf16[128,640]{1,0:T(8,128)(2,1)S(1)}, u32[]{:S(2)}, u32[]{:S(2)}) collective-permute-start(bf16[128,640]{1,0:T(8,128)(2,1)S(1)} %get-tuple-element.37), channel_id=1, source_target_pairs={{0,64},{4,68},{8,72},{12,76},{16,80},{20,84},{24,88},{28,92},{32,9... | collective-permute-start | bytes 491528 | tf_op jit(solution)/shard_map/ppermute | solution.py:229
  39.7 4.3 %collective-permute-done = bf16[128,640]{1,0:T(8,128)(2,1)S(1)} collective-permute-done((bf16[128,640]{1,0:T(8,128)(2,1)S(1)}, bf16[128,640]{1,0:T(8,128)(2,1)S(1)}, u32[]{:S(2)}, u32[]{:S(2)}) %collective-permute-start) | collective-permute-done | bytes 163872 | tf_op jit(solution)/shard_map/ppermute | solution.py:229
  44.0 0.0 collective-permute-done.1
  44.0 2.5 %collective-permute-done.2 = bf16[128,640]{1,0:T(8,128)(2,1)S(1)} collective-permute-done((bf16[128,640]{1,0:T(8,128)(2,1)S(1)}, bf16[128,640]{1,0:T(8,128)(2,1)S(1)}, u32[]{:S(2)}, u32[]{:S(2)}) %collective-permute-start.2) | collective-permute-done | bytes 163872 | tf_op jit(solution)/shard_map/ppermute | solution.py:229
  46.7 0.1 constant_dynamic-slice_fusion
  46.8 19.1 %all-to-all-done = bf16[64,8,640]{2,1,0:T(8,128)(2,1)S(1)} async-done(((bf16[64,8,640]{2,1,0:T(8,128)(2,1)}), bf16[64,8,640]{2,1,0:T(8,128)(2,1)S(1)}, u32[]{:S(2)}, u32[]{:S(2)}) %all-to-all-start) | async-done | bytes 655392 | tf_op jit(solution)/shard_map/all_to_all | solution.py:221
  65.9 0.8 copy-done.2
  66.7 0.0 all-gather.3.cloned.1.call-update
  66.8 0.0 all-gather.5.cloned.1.call-start
  66.8 39.3 %all_to_all.47 = bf16[16,32,640]{2,1,0:T(8,128)(2,1)} all-to-all(bf16[16,32,640]{2,1,0:T(8,128)(2,1)S(1)} %bitcast.62), channel_id=1, replica_groups={{0,4,8,12,16,20,24,28,32,36,40,44,48,52,56,60},{64,68,72,76,80,84,88,92..., dimensions={0} | all-to-all | bytes 1310720 | tf_op jit(solution)/shard_map/all_to_all | solution.py:221
  106.1 0.0 all-gather.5.cloned.1.call-update
  106.1 5.1 %shard_map.66 = (f32[320,768]{1,0:T(8,128)S(1)}, bf16[320,768]{1,0:T(8,128)(2,1)S(1)}) custom-call(s32[3]{0:T(128)S(1)} %pad_add_fusion.refs_0_.place_ref, bf16[2048,640]{1,0:T(8,128)(2,1)} %all-gather.3.cloned.1.call-done.blocks_ref, bf16[2048,384]{1,0:T(8,128)(2,1)} %bitcast.65, bf16[2048,384]{1,0:T(8,128)(2,1)} %bitcast.67), custom_call_target="tpu_custom_call" | custom-call | flops 2147483648 | bytes 5767180 | tf_op jit(solution)/shard_map/pallas_call | solution.py:23
  111.2 1.9 collective-permute-start.3
  113.1 1.8 collective-permute-done.3.got_ref
  114.9 0.2 shard_map.67
  115.1 19.9 %all_gather.14.hidden_ref = bf16[1280,384]{1,0:T(8,128)(2,1)S(1)} all-gather(bf16[320,384]{1,0:T(8,128)(2,1)S(1)} %shard_map.67), channel_id=1, replica_groups=mesh['sec'=2,'ep'=64,'tp'=4] {'tp'}, dimensions={0}, use_global_device_ids=true | all-gather | bytes 1228800 | tf_op jit(solution)/shard_map/all_gather | solution.py:275
  135.0 1.9 collective-permute-start.4
  137.0 2.2 shard_map.68.own_ref
  139.2 0.3 collective-permute-done.4.hidden_ref
  139.5 2.2 shard_map.69
  141.7 3.7 %all-to-all-start.2 = ((bf16[16,32,640]{2,1,0:T(8,128)(2,1)}), bf16[16,32,640]{2,1,0:T(8,128)(2,1)S(1)}, u32[]{:S(2)}, u32[]{:S(2)}) async-start(bf16[16,32,640]{2,1,0:T(8,128)(2,1)} %bitcast.24), calls=%async_computation.2 | async-start | bytes 1310720 | tf_op jit(solution)/shard_map/all_to_all | solution.py:221
  145.5 5.6 %all-gather.5.cloned.1.call-done.blocks_ref = bf16[2048,640]{1,0:T(8,128)(2,1)} async-done(((bf16[512,640]{1,0:T(8,128)(2,1)}), bf16[2048,640]{1,0:T(8,128)(2,1)}) %all-gather.5.cloned.1.call-update) | async-done | bytes 2621456 | tf_op jit(solution)/shard_map/all_gather | solution.py:307
  151.1 5.1 %shard_map.70 = (f32[320,768]{1,0:T(8,128)S(1)}, bf16[320,768]{1,0:T(8,128)(2,1)S(1)}) custom-call(s32[3]{0:T(128)S(1)} %pad_add_fusion.refs_0_.place_ref, bf16[2048,640]{1,0:T(8,128)(2,1)} %all-gather.5.cloned.1.call-done.blocks_ref, bf16[2048,384]{1,0:T(8,128)(2,1)} %bitcast.66, bf16[2048,384]{1,0:T(8,128)(2,1)} %bitcast.68), custom_call_target="tpu_custom_call" | custom-call | flops 2147483648 | bytes 5767180 | tf_op jit(solution)/shard_map/pallas_call | solution.py:23
  156.2 1.9 collective-permute-start.5
  158.1 1.8 collective-permute-done.5.got_ref
  159.9 0.2 shard_map.71
  160.1 14.8 %all_gather.15.hidden_ref = bf16[1280,384]{1,0:T(8,128)(2,1)S(1)} all-gather(bf16[320,384]{1,0:T(8,128)(2,1)S(1)} %shard_map.71), channel_id=1, replica_groups=mesh['sec'=2,'ep'=64,'tp'=4] {'tp'}, dimensions={0}, use_global_device_ids=true | all-gather | bytes 1228800 | tf_op jit(solution)/shard_map/all_gather | solution.py:275
  175.0 2.1 collective-permute-start.6
  177.1 2.2 shard_map.72.own_ref
  179.3 0.1 collective-permute-done.6.hidden_ref
  179.4 2.2 shard_map.73
  181.6 0.0 all-to-all-done.2
  181.6 0.0 copy-start.3
  181.6 12.2 %all-to-all-start.3 = ((bf16[64,8,640]{2,1,0:T(8,128)(2,1)}), bf16[64,8,640]{2,1,0:T(8,128)(2,1)S(1)}, u32[]{:S(2)}, u32[]{:S(2)}) async-start(bf16[64,8,640]{2,1,0:T(8,128)(2,1)} %bitcast.31), calls=%async_computation.3 | async-start | bytes 1310720 | tf_op jit(solution)/shard_map/all_to_all | solution.py:221
  193.9 0.0 copy-start.4
  193.9 0.1 dynamic-slice_bitcast_fusion.3
  193.9 2.4 collective-permute-start.10
  196.3 4.4 %collective-permute-start.11 = (bf16[128,640]{1,0:T(8,128)(2,1)S(1)}, bf16[128,640]{1,0:T(8,128)(2,1)S(1)}, u32[]{:S(2)}, u32[]{:S(2)}) collective-permute-start(bf16[128,640]{1,0:T(8,128)(2,1)S(1)} %get-tuple-element.35), channel_id=1, source_target_pairs={{0,128},{4,132},{8,136},{12,140},{16,144},{20,148},{24,152},{28,15... | collective-permute-start | bytes 491528 | tf_op jit(solution)/shard_map/ppermute | solution.py:229
  200.7 1.9 collective-permute-start.12
  202.7 0.2 fusion.3
  202.8 0.1 copy.20
  202.9 1.9 collective-permute-start.7
  204.8 1.2 collective-permute-done.7
  206.1 1.9 collective-permute-start.8
  208.0 5.4 %collective-permute-done.8 = f32[128,64]{1,0:T(8,128)S(1)} collective-permute-done((f32[128,64]{1,0:T(8,128)S(1)}, f32[128,64]{1,0:T(8,128)S(1)}, u32[]{:S(2)}, u32[]{:S(2)}) %collective-permute-start.8) | collective-permute-done | bytes 32800 | tf_op jit(solution)/shard_map/ppermute | solution.py:217
  213.5 2.2 collective-permute-start.9
  215.6 0.0 copy-done.4
  215.6 0.1 copy.21.ids_ref
  215.7 5.4 %collective-permute-done.9 = f32[128,64]{1,0:T(8,128)S(1)} collective-permute-done((f32[128,64]{1,0:T(8,128)S(1)}, f32[128,64]{1,0:T(8,128)S(1)}, u32[]{:S(2)}, u32[]{:S(2)}) %collective-permute-start.9) | collective-permute-done | bytes 32800 | tf_op jit(solution)/shard_map/ppermute | solution.py:217
  221.1 0.0 collective-permute-done.10
  221.1 0.0 collective-permute-done.11
  221.2 0.0 collective-permute-done.12
  221.2 0.1 pad_maximum_fusion.block_ref
  221.2 2.0 shard_map.74
  223.3 9.5 %all-to-all-done.3 = bf16[64,8,640]{2,1,0:T(8,128)(2,1)S(1)} async-done(((bf16[64,8,640]{2,1,0:T(8,128)(2,1)}), bf16[64,8,640]{2,1,0:T(8,128)(2,1)S(1)}, u32[]{:S(2)}, u32[]{:S(2)}) %all-to-all-start.3) | async-done | bytes 655392 | tf_op jit(solution)/shard_map/all_to_all | solution.py:221
  232.7 1.2 shard_map.75
  (17 shorter events, 0.2 us)
Async XLA Ops:
  6.5 196.1 %copy-start = (bf16[512,64]{0,1:T(8,128)(2,1)S(1)}, bf16[512,64]{0,1:T(8,128)(2,1)}, u32[]{:S(2)}) copy-start(bf16[512,64]{0,1:T(8,128)(2,1)} %param.7) | copy-start | bytes 196612
  8.9 57.0 %all-to-all-start = ((bf16[64,8,640]{2,1,0:T(8,128)(2,1)}), bf16[64,8,640]{2,1,0:T(8,128)(2,1)S(1)}, u32[]{:S(2)}, u32[]{:S(2)}) async-start(bf16[64,8,640]{2,1,0:T(8,128)(2,1)} %bitcast.4), calls=%async_computation | async-start | bytes 1310720 | tf_op jit(solution)/shard_map/all_to_all | solution.py:221
  27.5 78.5 %all-gather.3.cloned.1.call-start = ((), (), s32[]{:S(2)}) async-start(), calls=%async_computation.4 | async-start | bytes 3276800 | tf_op jit(solution)/shard_map/all_gather | solution.py:304
  29.8 14.2 %collective-permute-start = (bf16[128,640]{1,0:T(8,128)(2,1)S(1)}, bf16[128,640]{1,0:T(8,128)(2,1)S(1)}, u32[]{:S(2)}, u32[]{:S(2)}) collective-permute-start(bf16[128,640]{1,0:T(8,128)(2,1)S(1)} %get-tuple-element.39), channel_id=1, source_target_pairs={{0,192},{4,196},{8,200},{12,204},{16,208},{20,212},{24,216},{28,22... | collective-permute-start | bytes 491528 | tf_op jit(solution)/shard_map/ppermute | solution.py:229
  32.6 11.4 %collective-permute-start.1 = (bf16[128,640]{1,0:T(8,128)(2,1)S(1)}, bf16[128,640]{1,0:T(8,128)(2,1)S(1)}, u32[]{:S(2)}, u32[]{:S(2)}) collective-permute-start(bf16[128,640]{1,0:T(8,128)(2,1)S(1)} %get-tuple-element.38), channel_id=1, source_target_pairs={{0,128},{4,132},{8,136},{12,140},{16,144},{20,148},{24,152},{28,15... | collective-permute-start | bytes 491528 | tf_op jit(solution)/shard_map/ppermute | solution.py:229
  35.5 11.0 %collective-permute-start.2 = (bf16[128,640]{1,0:T(8,128)(2,1)S(1)}, bf16[128,640]{1,0:T(8,128)(2,1)S(1)}, u32[]{:S(2)}, u32[]{:S(2)}) collective-permute-start(bf16[128,640]{1,0:T(8,128)(2,1)S(1)} %get-tuple-element.37), channel_id=1, source_target_pairs={{0,64},{4,68},{8,72},{12,76},{16,80},{20,84},{24,88},{28,92},{32,9... | collective-permute-start | bytes 491528 | tf_op jit(solution)/shard_map/ppermute | solution.py:229
  65.9 0.8 copy-start.2
  66.8 84.3 %all-gather.5.cloned.1.call-start = ((), (), s32[]{:S(2)}) async-start(), calls=%async_computation.5 | async-start | bytes 3276800 | tf_op jit(solution)/shard_map/all_gather | solution.py:307
  111.2 3.8 %collective-permute-start.3 = (bf16[320,768]{1,0:T(8,128)(2,1)S(1)}, bf16[320,768]{1,0:T(8,128)(2,1)S(1)}, u32[]{:S(2)}, u32[]{:S(2)}) collective-permute-start(bf16[320,768]{1,0:T(8,128)(2,1)S(1)} %get-tuple-element.24), channel_id=1, source_target_pairs={{0,256},{256,0},{1,257},{257,1},{2,258},{258,2},{3,259},{259,3},{4... | collective-permute-start | bytes 1474568 | tf_op jit(solution)/shard_map/ppermute | solution.py:217
  114.9 22.0 %copy-start.1 = (bf16[1,1536,512]{2,1,0:T(8,128)(2,1)S(1)}, bf16[1,1536,512]{2,1,0:T(8,128)(2,1)}, u32[]{:S(2)}) copy-start(bf16[1,1536,512]{2,1,0:T(8,128)(2,1)} %param.11) | copy-start | bytes 4718596
  135.0 4.4 %collective-permute-start.4 = (bf16[1280,384]{1,0:T(8,128)(2,1)S(1)}, bf16[1280,384]{1,0:T(8,128)(2,1)S(1)}, u32[]{:S(2)}, u32[]{:S(2)}) collective-permute-start(bf16[1280,384]{1,0:T(8,128)(2,1)S(1)} %all_gather.14.hidden_ref), channel_id=1, source_target_pairs={{0,256},{256,0},{1,257},{257,1},{2,258},{258,2},{3,259},{259,3},{4... | collective-permute-start | bytes 2949128 | tf_op jit(solution)/shard_map/ppermute | solution.py:217
  141.7 39.9 %all-to-all-start.2 = ((bf16[16,32,640]{2,1,0:T(8,128)(2,1)}), bf16[16,32,640]{2,1,0:T(8,128)(2,1)S(1)}, u32[]{:S(2)}, u32[]{:S(2)}) async-start(bf16[16,32,640]{2,1,0:T(8,128)(2,1)} %bitcast.24), calls=%async_computation.2 | async-start | bytes 1310720 | tf_op jit(solution)/shard_map/all_to_all | solution.py:221
  156.2 3.8 %collective-permute-start.5 = (bf16[320,768]{1,0:T(8,128)(2,1)S(1)}, bf16[320,768]{1,0:T(8,128)(2,1)S(1)}, u32[]{:S(2)}, u32[]{:S(2)}) collective-permute-start(bf16[320,768]{1,0:T(8,128)(2,1)S(1)} %get-tuple-element.27), channel_id=1, source_target_pairs={{0,256},{256,0},{1,257},{257,1},{2,258},{258,2},{3,259},{259,3},{4... | collective-permute-start | bytes 1474568 | tf_op jit(solution)/shard_map/ppermute | solution.py:217
  175.0 4.4 %collective-permute-start.6 = (bf16[1280,384]{1,0:T(8,128)(2,1)S(1)}, bf16[1280,384]{1,0:T(8,128)(2,1)S(1)}, u32[]{:S(2)}, u32[]{:S(2)}) collective-permute-start(bf16[1280,384]{1,0:T(8,128)(2,1)S(1)} %all_gather.15.hidden_ref), channel_id=1, source_target_pairs={{0,256},{256,0},{1,257},{257,1},{2,258},{258,2},{3,259},{259,3},{4... | collective-permute-start | bytes 2949128 | tf_op jit(solution)/shard_map/ppermute | solution.py:217
  181.6 21.0 %copy-start.3 = (bf16[128,512]{1,0:T(8,128)(2,1)S(1)}, bf16[128,512]{1,0:T(8,128)(2,1)}, u32[]{:S(2)}) copy-start(bf16[128,512]{1,0:T(8,128)(2,1)} %refs_2_.1) | copy-start | bytes 393220
  181.6 51.1 %all-to-all-start.3 = ((bf16[64,8,640]{2,1,0:T(8,128)(2,1)}), bf16[64,8,640]{2,1,0:T(8,128)(2,1)S(1)}, u32[]{:S(2)}, u32[]{:S(2)}) async-start(bf16[64,8,640]{2,1,0:T(8,128)(2,1)} %bitcast.31), calls=%async_computation.3 | async-start | bytes 1310720 | tf_op jit(solution)/shard_map/all_to_all | solution.py:221
  193.9 21.8 %copy-start.4 = (s32[128,8]{0,1:T(8,128)S(1)}, s32[128,8]{0,1:T(8,128)}, u32[]{:S(2)}) copy-start(s32[128,8]{0,1:T(8,128)} %param.8) | copy-start | bytes 12292
  193.9 27.2 %collective-permute-start.10 = (bf16[128,640]{1,0:T(8,128)(2,1)S(1)}, bf16[128,640]{1,0:T(8,128)(2,1)S(1)}, u32[]{:S(2)}, u32[]{:S(2)}) collective-permute-start(bf16[128,640]{1,0:T(8,128)(2,1)S(1)} %get-tuple-element.36), channel_id=1, source_target_pairs={{0,64},{4,68},{8,72},{12,76},{16,80},{20,84},{24,88},{28,92},{32,9... | collective-permute-start | bytes 491528 | tf_op jit(solution)/shard_map/ppermute | solution.py:229
  196.3 24.8 %collective-permute-start.11 = (bf16[128,640]{1,0:T(8,128)(2,1)S(1)}, bf16[128,640]{1,0:T(8,128)(2,1)S(1)}, u32[]{:S(2)}, u32[]{:S(2)}) collective-permute-start(bf16[128,640]{1,0:T(8,128)(2,1)S(1)} %get-tuple-element.35), channel_id=1, source_target_pairs={{0,128},{4,132},{8,136},{12,140},{16,144},{20,148},{24,152},{28,15... | collective-permute-start | bytes 491528 | tf_op jit(solution)/shard_map/ppermute | solution.py:229
  200.7 20.5 %collective-permute-start.12 = (bf16[128,640]{1,0:T(8,128)(2,1)S(1)}, bf16[128,640]{1,0:T(8,128)(2,1)S(1)}, u32[]{:S(2)}, u32[]{:S(2)}) collective-permute-start(bf16[128,640]{1,0:T(8,128)(2,1)S(1)} %get-tuple-element.34), channel_id=1, source_target_pairs={{0,192},{4,196},{8,200},{12,204},{16,208},{20,212},{24,216},{28,22... | collective-permute-start | bytes 491528 | tf_op jit(solution)/shard_map/ppermute | solution.py:229
  202.9 3.1 %collective-permute-start.7 = (f32[128,64]{1,0:T(8,128)S(1)}, f32[128,64]{1,0:T(8,128)S(1)}, u32[]{:S(2)}, u32[]{:S(2)}) collective-permute-start(f32[128,64]{1,0:T(8,128)S(1)} %copy.20), channel_id=1, source_target_pairs={{0,256},{256,0},{1,257},{257,1},{2,258},{258,2},{3,259},{259,3},{4... | collective-permute-start | bytes 98312 | tf_op jit(solution)/shard_map/ppermute | solution.py:217
  206.1 7.4 %collective-permute-start.8 = (f32[128,64]{1,0:T(8,128)S(1)}, f32[128,64]{1,0:T(8,128)S(1)}, u32[]{:S(2)}, u32[]{:S(2)}) collective-permute-start(f32[128,64]{1,0:T(8,128)S(1)} %add.34), channel_id=1, source_target_pairs={{0,1},{1,2},{2,3},{3,0},{4,5},{5,6},{6,7},{7,4},{8,9},{9,10},{10,1... | collective-permute-start | bytes 98312 | tf_op jit(solution)/shard_map/ppermute | solution.py:217
  213.5 7.7 %collective-permute-start.9 = (f32[128,64]{1,0:T(8,128)S(1)}, f32[128,64]{1,0:T(8,128)S(1)}, u32[]{:S(2)}, u32[]{:S(2)}) collective-permute-start(f32[128,64]{1,0:T(8,128)S(1)} %add.35), channel_id=1, source_target_pairs={{0,2},{1,3},{2,0},{3,1},{4,6},{5,7},{6,4},{7,5},{8,10},{9,11},{10,... | collective-permute-start | bytes 98312 | tf_op jit(solution)/shard_map/ppermute | solution.py:217
Sparse Core Ops, SparseCore 0:
  66.9 34.6 all-gather.2
  106.2 44.8 all-gather.4
